TPU v7x, 32 devices: a whole 2x2x4 slice. The times are simulated.
32 devices in a mesh: dp: 16 (over z, y, core), seq: 2 (over x).
Axes of the slice: x: 2, y: 2, z: 4, core: 2. Of those that a mesh axis runs over, the one named last changes fastest.
Arguments:
- patches: bfloat16 [64, 256, 48], P('dp', 'seq'), may hold values from -4 to 4
- labels: int32 [64], P('dp'), may hold values from 0 to 1023
- valid_mask: int32 [64, 256], P('dp', 'seq'), may hold values 0 or 1
- class_slot: int32 [1024], replicated, may hold values from 0 to 1023, each once
- w_patch: bfloat16 [48, 768], replicated, may hold values from -0.875 to 0.875
- b_patch: bfloat16 [768], replicated, may hold values from -4 to 4
- pos_embed: bfloat16 [256, 768], replicated, may hold values from -4 to 4
- class_embed: bfloat16 [1024, 768], replicated, may hold values from -4 to 4
- norm1_gain: bfloat16 [768], replicated, may hold values from 0.5 to 1.5
- norm1_shift: bfloat16 [768], replicated, may hold values from -4 to 4
- w_qkv: bfloat16 [768, 2304], replicated, may hold values from -0.21875 to 0.21875
- w_out: bfloat16 [768, 768], replicated, may hold values from -0.875 to 0.875
- norm2_gain: bfloat16 [768], replicated, may hold values from 0.5 to 1.5
- norm2_shift: bfloat16 [768], replicated, may hold values from -4 to 4
- w_fc1: bfloat16 [768, 3072], replicated, may hold values from -0.21875 to 0.21875
- b_fc1: bfloat16 [3072], replicated, may hold values from -4 to 4
- w_fc2: bfloat16 [3072, 768], replicated, may hold values from -0.109375 to 0.109375
- b_fc2: bfloat16 [768], replicated, may hold values from -4 to 4
- final_gain: bfloat16 [768], replicated, may hold values from 0.5 to 1.5
- final_shift: bfloat16 [768], replicated, may hold values from -4 to 4
- w_head: bfloat16 [768, 96], replicated, may hold values from -0.109375 to 0.109375
- b_head: bfloat16 [96], replicated, may hold values from -3 to 3
- cot_latent: float32 [64, 256, 48], P('dp', 'seq'), may hold values from -6 to 6
- cot_logdet: float32 [64], P('dp'), may hold values from -4 to 4
Outputs:
- latent: float32 [64, 256, 48], P('dp', 'seq')
- logdet: float32 [64], P('dp')
- grad_patches: float32 [64, 256, 48], P('dp', 'seq')
- grad_w_patch: float32 [48, 768], replicated
- grad_b_patch: float32 [768], replicated
- grad_pos_embed: float32 [256, 768], replicated
- grad_class_embed: float32 [1024, 768], P(('dp', 'seq'))
- grad_norm1_gain: float32 [768], replicated
- grad_norm1_shift: float32 [768], replicated
- grad_w_qkv: float32 [768, 2304], replicated
- grad_w_out: float32 [768, 768], replicated
- grad_norm2_gain: float32 [768], replicated
- grad_norm2_shift: float32 [768], replicated
- grad_w_fc1: float32 [768, 3072], P(None, ('dp', 'seq'))
- grad_b_fc1: float32 [3072], P(('dp', 'seq'))
- grad_w_fc2: float32 [3072, 768], P(('dp', 'seq'))
- grad_b_fc2: float32 [768], replicated
- grad_final_gain: float32 [768], replicated
- grad_final_shift: float32 [768], replicated
- grad_w_head: float32 [768, 96], replicated
- grad_b_head: float32 [96], replicated
- mean_logscale: float32 [], replicated
- max_logscale: float32 [], replicated
Inputs may be any that keep to these rules, and one draw needn't show every extreme that they name: `class_slot`: each row number appears exactly once.
All inputs are finite; a program needn't handle non-finite values. No bound on the sum of `valid_mask` on one device may be relied on, other than what follows from the above.
Results may differ from a plain program's by a relative error of at most 0.009.
Values may be sent and summed in bfloat16 or wider, within the bound.
No kernel may reach another device: no remote copies, remote signals or barrier semaphores. Data moves between devices by JAX's collectives and lax.ppermute only.
A program may use at most 192 MiB of HBM per device.

v0:
```python
import math

import jax
import jax.numpy as jnp
from jax import lax
from jax.sharding import PartitionSpec as P

HEADS = 12


EPS = 1e-05
HIGH = lax.Precision.HIGHEST


def passed_along(block, axis, distance):
    devices = range(lax.axis_size(axis))
    route = [(i - distance, i) for i in devices if i - distance in devices]
    return lax.ppermute(block, axis, route)


def layer_norm(hidden, gain, offset):
    center = hidden - jnp.mean(hidden, axis=-1, keepdims=True)
    spread = jnp.mean(center * center, axis=-1, keepdims=True)
    return center * lax.rsqrt(spread + EPS) * gain + offset


def gelu_tanh(values):
    return jax.nn.gelu(values, approximate=True)


def inner_rows(left, right):
    return lax.dot_general(
        left, right, (((0,), (0,)), ((), ())), preferred_element_type=jnp.float32
    )


def inner_cols(left, right):
    return lax.dot_general(
        left, right, (((1,), (1,)), ((), ())), preferred_element_type=jnp.float32
    )


def attention_scores(query, keys_all, query_pos, key_pos, scale):
    scores = (
        jnp.einsum("bqhd,bkhd->bhqk", query, keys_all, preferred_element_type=jnp.float32) * scale
    )
    allowed = (key_pos[None, :] <= query_pos[:, None]) & (key_pos[None, :] >= 0)
    scores = jnp.where(allowed[None, None], scores, -1e30)
    return (scores, allowed)


def local(
    patches,
    labels,
    valid_mask,
    class_slot,
    w_patch,
    b_patch,
    pos_embed,
    class_embed,
    norm1_gain,
    norm1_shift,
    w_qkv,
    w_out,
    norm2_gain,
    norm2_shift,
    w_fc1,
    b_fc1,
    w_fc2,
    b_fc2,
    final_gain,
    final_shift,
    w_head,
    b_head,
    cot_latent,
    cot_logdet,
):
    item_count, span_len, patch_dim = patches.shape
    model_width = w_out.shape[0]
    head_dim = model_width // HEADS
    scale = 1.0 / math.sqrt(head_dim)
    class_total = class_embed.shape[0]
    row_count = item_count * span_len
    seq_rank = lax.axis_index("seq")
    span_start = seq_rank * span_len
    query_pos = span_start + jnp.arange(span_len, dtype=jnp.int32)
    gain1 = norm1_gain.astype(jnp.float32)
    shift1 = norm1_shift.astype(jnp.float32)
    gain2 = norm2_gain.astype(jnp.float32)
    shift2 = norm2_shift.astype(jnp.float32)
    gainf = final_gain.astype(jnp.float32)
    shiftf = final_shift.astype(jnp.float32)
    before = passed_along(patches[:, span_len - 1, :], "seq", 1)
    shifted = jnp.concatenate([before[:, None, :], patches[:, :-1, :]], axis=1)
    flat_in = shifted.reshape(row_count, patch_dim)
    label_hot = labels[:, None] == jnp.arange(class_total, dtype=jnp.int32)[None, :]
    class_rows = jnp.dot(
        label_hot.astype(jnp.bfloat16), class_embed, preferred_element_type=jnp.float32
    )
    positions = lax.dynamic_slice_in_dim(pos_embed, span_start, span_len, 0).astype(jnp.float32)
    hidden0 = jnp.dot(flat_in, w_patch, preferred_element_type=jnp.float32).reshape(
        item_count, span_len, model_width
    )
    hidden0 = hidden0 + b_patch.astype(jnp.float32) + positions[None] + class_rows[:, None, :]
    hidden0 = hidden0.reshape(row_count, model_width)
    normed1 = layer_norm(hidden0, gain1, shift1).astype(jnp.bfloat16)
    qkv = jnp.dot(normed1, w_qkv, preferred_element_type=jnp.float32).astype(jnp.bfloat16)
    qkv = qkv.reshape(item_count, span_len, 3, HEADS, head_dim)
    query = qkv[:, :, 0]
    key_own = qkv[:, :, 1]
    value_own = qkv[:, :, 2]
    keys_all, values_all = (
        lax.all_gather(key_own, "seq", axis=1, tiled=True),
        lax.all_gather(value_own, "seq", axis=1, tiled=True),
    )
    key_pos = jnp.arange(keys_all.shape[1], dtype=jnp.int32)
    scores, allowed = attention_scores(query, keys_all, query_pos, key_pos, scale)
    top = jnp.max(scores, axis=-1, keepdims=True)
    total = jnp.sum(jnp.exp(scores - top), axis=-1, keepdims=True)
    log_total = top + jnp.log(total)
    probs = jnp.where(allowed[None, None], jnp.exp(scores - log_total), 0.0)
    attended = (
        jnp.einsum(
            "bhqk,bkhd->bqhd",
            probs.astype(jnp.bfloat16),
            values_all,
            preferred_element_type=jnp.float32,
        )
        .astype(jnp.bfloat16)
        .reshape(row_count, model_width)
    )
    hidden1 = hidden0 + jnp.dot(attended, w_out, preferred_element_type=jnp.float32)
    normed2 = layer_norm(hidden1, gain2, shift2).astype(jnp.bfloat16)
    up_values = jnp.dot(normed2, w_fc1, preferred_element_type=jnp.float32) + b_fc1.astype(
        jnp.float32
    )
    act_values = gelu_tanh(up_values).astype(jnp.bfloat16)
    hidden2 = (
        hidden1
        + jnp.dot(act_values, w_fc2, preferred_element_type=jnp.float32)
        + b_fc2.astype(jnp.float32)
    )
    normed3 = layer_norm(hidden2, gainf, shiftf).astype(jnp.bfloat16)
    head_out = jnp.dot(normed3, w_head, preferred_element_type=jnp.float32) + b_head.astype(
        jnp.float32
    )
    head_out = head_out.reshape(item_count, span_len, 2 * patch_dim)
    shift_part = head_out[..., :patch_dim]
    log_scale = head_out[..., patch_dim:]
    valid_f = valid_mask.astype(jnp.float32)[..., None]
    inputs = patches.astype(jnp.float32)
    inverse = jnp.exp(-log_scale)
    moved = (inputs - shift_part) * inverse
    latent = valid_f * moved + (1.0 - valid_f) * inputs
    logdet = lax.psum(-jnp.sum(valid_f * log_scale, axis=(1, 2)), "seq")
    scale_sum = jnp.sum(valid_f * log_scale)
    scale_count = jnp.sum(valid_f) * patch_dim
    local_top = jnp.max(jnp.where(valid_f > 0, log_scale, -1e30))
    top_scale = lax.pmax(local_top, ("dp", "seq"))
    d_moved = valid_f * cot_latent
    d_shift = -d_moved * inverse
    d_scale = -d_moved * moved - valid_f * cot_logdet[:, None, None]
    d_head = (
        jnp.concatenate([d_shift, d_scale], axis=-1)
        .astype(jnp.bfloat16)
        .reshape(row_count, 2 * patch_dim)
    )
    grad_b_head = jnp.sum(d_head.astype(jnp.float32), axis=0)
    grad_w_head = inner_rows(normed3, d_head)
    d_normed3 = inner_cols(d_head, w_head)
    pull_final = jax.vjp(layer_norm, hidden2, gainf, shiftf)[1]
    d_hidden2, grad_final_gain, grad_final_shift = pull_final(d_normed3)
    d_mlp = d_hidden2.astype(jnp.bfloat16)
    grad_b_fc2 = jnp.sum(d_mlp.astype(jnp.float32), axis=0)
    grad_w_fc2 = inner_rows(act_values, d_mlp)
    d_act = inner_cols(d_mlp, w_fc2)
    pull_gelu = jax.vjp(gelu_tanh, up_values)[1]
    d_up = pull_gelu(d_act)[0].astype(jnp.bfloat16)
    grad_b_fc1 = jnp.sum(d_up.astype(jnp.float32), axis=0)
    grad_w_fc1 = inner_rows(normed2, d_up)
    d_normed2 = inner_cols(d_up, w_fc1)
    pull_second = jax.vjp(layer_norm, hidden1, gain2, shift2)[1]
    d_part1, grad_norm2_gain, grad_norm2_shift = pull_second(d_normed2)
    d_hidden1 = d_hidden2 + d_part1
    d_out = d_hidden1.astype(jnp.bfloat16)
    grad_w_out = inner_rows(attended, d_out)
    d_attended = (
        inner_cols(d_out, w_out).astype(jnp.bfloat16).reshape(item_count, span_len, HEADS, head_dim)
    )
    scores_again, allowed_again = attention_scores(query, keys_all, query_pos, key_pos, scale)
    probs_again = jnp.where(allowed_again[None, None], jnp.exp(scores_again - log_total), 0.0)
    d_probs = jnp.einsum(
        "bqhd,bkhd->bhqk", d_attended, values_all, preferred_element_type=jnp.float32
    )
    d_scores = probs_again * (d_probs - jnp.sum(probs_again * d_probs, axis=-1, keepdims=True))
    d_scores = d_scores.astype(jnp.bfloat16)
    d_query = (
        jnp.einsum("bhqk,bkhd->bqhd", d_scores, keys_all, preferred_element_type=jnp.float32)
        * scale
    )
    d_keys = (
        jnp.einsum("bhqk,bqhd->bkhd", d_scores, query, preferred_element_type=jnp.float32) * scale
    )
    d_values = jnp.einsum(
        "bhqk,bqhd->bkhd",
        probs_again.astype(jnp.bfloat16),
        d_attended,
        preferred_element_type=jnp.float32,
    )
    d_key_own, d_value_own = (
        lax.psum_scatter(d_keys, "seq", scatter_dimension=1, tiled=True),
        lax.psum_scatter(d_values, "seq", scatter_dimension=1, tiled=True),
    )
    d_qkv = jnp.stack([d_query, d_key_own, d_value_own], axis=2).astype(jnp.bfloat16)
    d_qkv = d_qkv.reshape(row_count, 3 * model_width)
    grad_w_qkv = inner_rows(normed1, d_qkv)
    d_normed1 = inner_cols(d_qkv, w_qkv)
    pull_first = jax.vjp(layer_norm, hidden0, gain1, shift1)[1]
    d_part0, grad_norm1_gain, grad_norm1_shift = pull_first(d_normed1)
    d_hidden0 = d_hidden1 + d_part0
    grad_b_patch = jnp.sum(d_hidden0, axis=0)
    grad_w_patch = lax.dot_general(
        flat_in.astype(jnp.float32),
        d_hidden0,
        (((0,), (0,)), ((), ())),
        precision=HIGH,
        preferred_element_type=jnp.float32,
    )
    d_items = d_hidden0.reshape(item_count, span_len, model_width)
    pos_local = jnp.sum(d_items, axis=0)
    grad_pos_full = lax.dynamic_update_slice_in_dim(
        jnp.zeros((pos_embed.shape[0], model_width), jnp.float32), pos_local, span_start, 0
    )
    item_sums = jnp.sum(d_items, axis=1)
    slot_of = jnp.sum(jnp.where(label_hot, class_slot[None, :], 0), axis=1)
    slot_hot = (slot_of[:, None] == jnp.arange(class_total, dtype=jnp.int32)[None, :]).astype(
        jnp.float32
    )
    class_local = lax.dot_general(
        slot_hot,
        item_sums,
        (((0,), (0,)), ((), ())),
        precision=HIGH,
        preferred_element_type=jnp.float32,
    )
    d_shifted = lax.dot_general(
        d_hidden0,
        w_patch.astype(jnp.float32),
        (((1,), (1,)), ((), ())),
        precision=HIGH,
        preferred_element_type=jnp.float32,
    )
    d_shifted = d_shifted.reshape(item_count, span_len, patch_dim)
    incoming = passed_along(d_shifted[:, 0, :], "seq", -1)
    from_shift = jnp.concatenate([d_shifted[:, 1:, :], incoming[:, None, :]], axis=1)
    grad_patches = cot_latent * (1.0 - valid_f) + d_moved * inverse + from_shift
    summed = lax.psum(
        (
            grad_w_patch,
            grad_b_patch,
            grad_pos_full,
            grad_norm1_gain,
            grad_norm1_shift,
            grad_w_qkv,
            grad_w_out,
            grad_norm2_gain,
            grad_norm2_shift,
            grad_b_fc2,
            grad_final_gain,
            grad_final_shift,
            grad_w_head,
            grad_b_head,
            scale_sum,
            scale_count,
        ),
        ("dp", "seq"),
    )
    owned = (
        lax.psum_scatter(grad_w_fc1, ("dp", "seq"), scatter_dimension=1, tiled=True),
        lax.psum_scatter(grad_b_fc1, ("dp", "seq"), scatter_dimension=0, tiled=True),
        lax.psum_scatter(grad_w_fc2, ("dp", "seq"), scatter_dimension=0, tiled=True),
        lax.psum_scatter(class_local, ("dp", "seq"), scatter_dimension=0, tiled=True),
    )
    mean_scale = summed[14] / summed[15]
    return (
        latent,
        logdet,
        grad_patches,
        summed[0],
        summed[1],
        summed[2],
        owned[3],
        summed[3],
        summed[4],
        summed[5],
        summed[6],
        summed[7],
        summed[8],
        owned[0],
        owned[1],
        owned[2],
        summed[9],
        summed[10],
        summed[11],
        summed[12],
        summed[13],
        mean_scale,
        top_scale,
    )


def solution(mesh):
    placed = (
        P("dp", "seq", None),
        P("dp"),
        P("dp", "seq"),
        P(),
        P(),
        P(),
        P(),
        P(),
        P(),
        P(),
        P(),
        P(),
        P(),
        P(),
        P(),
        P(),
        P(),
        P(),
        P(),
        P(),
        P(),
        P(),
        P("dp", "seq", None),
        P("dp"),
    )
    return jax.shard_map(
        local,
        mesh=mesh,
        in_specs=placed,
        out_specs=(
            P("dp", "seq", None),
            P("dp"),
            P("dp", "seq", None),
            P(),
            P(),
            P(),
            P(("dp", "seq"), None),
            P(),
            P(),
            P(),
            P(),
            P(),
            P(),
            P(None, ("dp", "seq")),
            P(("dp", "seq")),
            P(("dp", "seq"), None),
            P(),
            P(),
            P(),
            P(),
            P(),
            P(),
            P(),
        ),
        check_vma=False,
    )
```

profile of v0, /device:TPU:0, one launch (start us, length us, event | category | flops | bytes accessed | tf_op | source)
XLA Modules:
  0.0 901.0 jit_solution(5369003504972583936)
XLA Ops:
  9.0 5.4 collective-permute-start
  23.2 3.4 convolution_convert_fusion
  26.6 4.3 copy.112
  30.9 5.3 reshape.278
  36.1 3.9 fusion.67
  49.3 2.2 copy.129
  51.6 1.9 convert_reduce_fusion.3
  54.9 13.9 %all-gather.7.cloned.1.call-done = bf16[4,256,1,12,64]{1,4,3,0,2:T(8,128)(2,1)} async-done(((bf16[4,128,1,12,64]{1,4,3,0,2:T(8,128)(2,1)}), bf16[4,256,1,12,64]{1,4,3,0,2:T(8,128)(2,1)}) %all-gather.7.cloned.1.call-update) | async-done | bytes 1572880 | tf_op jit(solution)/shard_map/all_gather | solution.py:113
  68.8 3.5 fusion.7
  72.3 3.0 exponential_reduce_fusion
  76.0 22.1 %all-gather.5.cloned.1.call-done = bf16[4,256,1,12,64]{1,4,3,0,2:T(8,128)(2,1)} async-done(((bf16[4,128,1,12,64]{1,4,3,0,2:T(8,128)(2,1)}), bf16[4,256,1,12,64]{1,4,3,0,2:T(8,128)(2,1)}) %all-gather.5.cloned.1.call-update) | async-done | bytes 1572880 | tf_op jit(solution)/shard_map/all_gather | solution.py:114
  98.1 5.1 fusion.28
  106.5 5.5 fusion.61
  112.1 4.1 fusion.71
  123.9 3.0 multiply_reduce_fusion.1
  128.5 10.7 %convert_reduce_fusion = (f32[3072]{0:T(1024)}, bf16[512,3072]{1,0:T(8,128)(2,1)S(1)}) fusion(f32[512,3072]{1,0:T(8,128)} %copy-done.77, f32[3072]{0:T(1024)S(1)} %copy-done.62, bf16[512,768]{1,0:T(8,128)(2,1)S(1)} %get-tuple-element.55, bf16[3072,768]{1,0:T(8,128)(2,1)} %param.40), kind=kOutput, calls=%fused_computation.9 | convolution fusion | flops 2452091904 | bytes 14966784 | tf_op jit(solution)/shard_map/dot_general | solution.py:38
  139.2 3.5 multiply_reduce_fusion.2
  146.6 2.3 copy.121
  148.9 2.4 reshape.281
  151.4 6.5 multiply_reduce_fusion
  157.9 4.7 multiply_convert_fusion
  164.3 2.2 multiply_bitcast_fusion
  166.8 6.6 convolution_bitcast_fusion
  174.3 4.5 multiply_bitcast_fusion.1
  178.7 31.3 %reduce-scatter.6.cloned.1.call-done = f32[4,128,12,64]{1,3,2,0:T(8,128)} async-done(((f32[4,256,12,64]{1,3,2,0:T(8,128)}), f32[4,128,12,64]{1,3,2,0:T(8,128)}) %reduce-scatter.6.cloned.1.call-update) | async-done | bytes 1572880 | tf_op jit(solution)/shard_map/reduce_scatter | solution.py:211
  210.0 45.6 %reduce-scatter.8.cloned.1.call-done = f32[4,128,12,64]{1,3,2,0:T(8,128)} async-done(((f32[4,256,12,64]{1,3,2,0:T(8,128)}), f32[4,128,12,64]{1,3,2,0:T(8,128)}) %reduce-scatter.8.cloned.1.call-update) | async-done | bytes 1572880 | tf_op jit(solution)/shard_map/reduce_scatter | solution.py:212
  255.6 2.6 maximum_convert_fusion
  258.2 2.2 copy.124
  260.5 3.1 multiply_reduce_fusion.3
  266.4 3.2 fusion.49
  270.2 2.7 add_convert_fusion
  274.0 2.2 fusion.31
  276.1 2.3 reduce_sum.289
  281.3 2.2 fusion.45
  283.5 6.7 fusion.9
  290.9 8.9 fusion.60
  300.5 10.6 %fusion.62 = f32[3072,768]{1,0:T(8,128)} fusion(bf16[512,768]{1,0:T(8,128)(2,1)} %copy-done.26, f32[512,3072]{1,0:T(8,128)} %copy-done.77, f32[3072]{0:T(1024)S(1)} %copy-done.63), kind=kOutput, calls=%fused_computation.136 | convolution fusion | flops 2431647744 | bytes 16527360 | tf_op jit(solution)/shard_map/dot_general | solution.py:32
  312.3 2.9 fusion.72
  322.9 2.1 reduce_sum.288
  328.0 2.4 multiply_reduce_fusion.10
  330.4 42.7 %pmax.7 = f32[]{:T(128)} all-reduce(f32[]{:T(128)} %get-tuple-element.34), channel_id=1, replica_groups=mesh['dp'=16,'seq'=2] {'dp','seq'}, use_global_device_ids=true, to_apply=%region_55.56 | all-reduce | flops 1 | bytes 8 | tf_op jit(solution)/shard_map/pmax | solution.py:159
  373.2 5.7 psum.119
  378.8 42.7 %all-reduce.1 = (f32[768]{0:T(1024)}, f32[768]{0:T(1024)}, f32[768]{0:T(1024)}, f32[768]{0:T(1024)}, f32[768]{0:T(1024)}, /*index=5*/f32[3072]{0:T(1024)}, f32[7...) all-reduce(f32[768]{0:T(1024)} %reduce_sum.288, ...), channel_id=1, replica_groups=mesh['dp'=16,'seq'=2] {'dp','seq'}, use_global_device_ids=true, to_apply=%region_21.22 | all-reduce | flops 9314 | bytes 74512 | tf_op jit(solution)/shard_map/psum | solution.py:257
  424.2 173.3 %all-reduce.5.cloned.1.call-done = (f32[48,768]{1,0:T(8,128)}, f32[256,768]{1,0:T(8,128)}, f32[768,2304]{1,0:T(8,128)}, f32[768,768]{1,0:T(8,128)}, f32[768,96]{0,1:T(8,128)}) async-done(((f32[48,768]{1,0:T(8,128)}, f32[256,768]{1,0:T(8,128)}, f32[768,2304]{1,0:T(8,128)}, f32[768,768]{1,0:T(8,128)}, f32[768,96]{0,1:T(8,128)}), (f32[48,768]{1,0:T(8,128)}, f32[256,768]{1,0:T(8,128)}, f32[768,2304]{1,0:T(8,128)}, ...) | async-done | bytes 10666000 | tf_op jit(solution)/shard_map/psum | solution.py:257
  597.5 140.6 %reduce-scatter.12.cloned.1.call-done = f32[768,96]{0,1:T(8,128)} async-done(((f32[768,3072]{0,1:T(8,128)}), f32[768,96]{0,1:T(8,128)}) %reduce-scatter.12.cloned.1.call-update) | async-done | bytes 294928 | tf_op jit(solution)/shard_map/reduce_scatter | solution.py:279
  738.1 142.4 %reduce-scatter.14.cloned.1.call-done = f32[96,768]{1,0:T(8,128)} async-done(((f32[3072,768]{1,0:T(8,128)}), f32[96,768]{1,0:T(8,128)}) %reduce-scatter.14.cloned.1.call-update) | async-done | bytes 294928 | tf_op jit(solution)/shard_map/reduce_scatter | solution.py:281
  882.1 2.1 copy.207
  884.2 6.6 copy.208
  (257 shorter events, 65.6 us)
Async XLA Ops:
  7.2 16.0 %copy-start = (bf16[768,2304]{1,0:T(8,128)(2,1)S(1)}, bf16[768,2304]{1,0:T(8,128)(2,1)}, u32[]{:S(2)}) copy-start(bf16[768,2304]{1,0:T(8,128)(2,1)} %param.34) | copy-start | bytes 10616836
  7.2 9.7 %copy-start.72 = (bf16[768]{0:T(1024)(128)(2,1)S(1)}, bf16[768]{0:T(1024)(128)(2,1)}, u32[]{:S(2)}) copy-start(bf16[768]{0:T(1024)(128)(2,1)} %param.29) | copy-start | bytes 4612
  7.2 61.6 %all-gather.7.cloned.1.call-start = ((), (), s32[]{:S(2)}) async-start(), calls=%async_computation.11 | async-start | bytes 2359296 | tf_op jit(solution)/shard_map/all_gather | solution.py:113
  9.0 9.2 %collective-permute-start = (bf16[4,48]{1,0:T(4,128)(2,1)}, bf16[4,48]{1,0:T(4,128)(2,1)}, u32[]{:S(2)}, u32[]{:S(2)}) collective-permute-start(bf16[4,48]{1,0:T(4,128)(2,1)} %slice_reduce_fusion), channel_id=1, source_target_pairs={{0,1},{2,3},{4,5},{6,7},{8,9},{10,11},{12,13},{14,15},{16,17},{18,... | collective-permute-start | bytes 1160 | tf_op jit(solution)/shard_map/ppermute | solution.py:18
  14.3 3.2 copy-start.73
  14.3 3.2 copy-start.74
  19.5 3.3 copy-start.34
  40.1 8.2 copy-start.53
  41.2 57.0 %all-gather.5.cloned.1.call-start = ((), (), s32[]{:S(2)}) async-start(), calls=%async_computation.10 | async-start | bytes 2359296 | tf_op jit(solution)/shard_map/all_gather | solution.py:114
  41.2 64.7 %copy-start.58 = (f32[768]{0:T(1024)}, f32[768]{0:T(1024)S(1)}, u32[]{:S(2)}) copy-start(f32[768]{0:T(1024)S(1)} %convert_element_type.124) | copy-start | bytes 9220
  51.6 158.5 %reduce-scatter.6.cloned.1.call-start = ((), (), s32[]{:S(2)}) async-start(), calls=%async_computation.5 | async-start | bytes 4718592 | tf_op jit(solution)/shard_map/reduce_scatter | solution.py:211
  68.8 3.5 copy-start.29
  98.1 5.7 copy-start.23
  105.6 6.5 copy-start.12
  105.6 6.4 slice-start
  106.5 5.5 copy-start.64
  106.5 5.6 copy-start.61
  106.5 5.6 copy-start.70
  106.5 5.6 slice-start.1
  112.1 4.1 copy-start.77
  127.6 11.6 %slice-start.2 = ((s8[4718592]{0:T(1024)(128)(4,1)}), s8[4194304]{0:T(1024)(128)(4,1)S(1)}, s32[]{:S(2)}) async-start(s8[4718592]{0:T(1024)(128)(4,1)} %bitcast.158), calls=%async_computation.15 | async-start | bytes 8388608
  128.4 10.7 %copy-start.26 = (bf16[512,768]{1,0:T(8,128)(2,1)}, bf16[512,768]{1,0:T(8,128)(2,1)S(1)}, u32[]{:S(2)}) copy-start(bf16[512,768]{1,0:T(8,128)(2,1)S(1)} %get-tuple-element.55) | copy-start | bytes 2359300
  128.4 10.7 %copy-start.13 = (f32[512,768]{1,0:T(8,128)S(1)}, f32[512,768]{1,0:T(8,128)}, u32[]{:S(2)}) copy-start(f32[512,768]{1,0:T(8,128)} %copy-done.12) | copy-start | bytes 4718596
  128.4 10.8 %copy-start.47 = (f32[512]{0:T(512)S(1)}, f32[512]{0:T(512)}, u32[]{:S(2)}) copy-start(f32[512]{0:T(512)} %copy-done.46) | copy-start | bytes 6148
  128.4 10.8 %copy-start.59 = (f32[768]{0:T(1024)S(1)}, f32[768]{0:T(1024)}, u32[]{:S(2)}) copy-start(f32[768]{0:T(1024)} %copy-done.58) | copy-start | bytes 9220
  128.4 10.8 %copy-start.65 = (f32[512]{0:T(512)S(1)}, f32[512]{0:T(512)}, u32[]{:S(2)}) copy-start(f32[512]{0:T(512)} %copy-done.64) | copy-start | bytes 6148
  128.4 10.8 %slice-start.3 = ((s8[4718592]{0:T(1024)(128)(4,1)}), s8[524288]{0:T(1024)(128)(4,1)S(1)}, s32[]{:S(2)}) async-start(s8[4718592]{0:T(1024)(128)(4,1)} %bitcast.158), calls=%async_computation.16 | async-start | bytes 1048576
  139.2 3.6 copy-start.78
  139.2 3.5 copy-start.50
  151.4 6.5 copy-start.30
  151.4 6.5 copy-start.32
  157.9 6.4 copy-start.16
  166.5 89.1 %reduce-scatter.8.cloned.1.call-start = ((), (), s32[]{:S(2)}) async-start(), calls=%async_computation.6 | async-start | bytes 4718592 | tf_op jit(solution)/shard_map/reduce_scatter | solution.py:212
  173.4 250.8 %reduce-scatter.10.cloned.1.call-start = ((), (), s32[]{:S(2)}) async-start(), calls=%async_computation.7 | async-start | bytes 3244032 | tf_op jit(solution)/shard_map/reduce_scatter | solution.py:282
  260.4 3.1 copy-start.20
  269.6 328.0 %all-reduce.5.cloned.1.call-start = ((), (), s32[]{:S(2)}) async-start(), calls=%async_computation.12 | async-start | bytes 21331968 | tf_op jit(solution)/shard_map/psum | solution.py:257
  269.9 3.1 copy-start.18
  270.2 3.7 copy-start.11
  270.2 3.7 copy-start.15
  278.4 5.0 copy-start.27
  290.2 447.9 %reduce-scatter.12.cloned.1.call-start = ((), (), s32[]{:S(2)}) async-start(), calls=%async_computation.8 | async-start | bytes 9732096 | tf_op jit(solution)/shard_map/reduce_scatter | solution.py:279
  299.8 580.7 %reduce-scatter.14.cloned.1.call-start = ((), (), s32[]{:S(2)}) async-start(), calls=%async_computation.9 | async-start | bytes 9732096 | tf_op jit(solution)/shard_map/reduce_scatter | solution.py:281
  315.2 12.8 %copy-start.38 = (f32[4,128]{1,0:T(4,128)S(1)}, f32[4,128]{1,0:T(4,128)}, u32[]{:S(2)}) copy-start(f32[4,128]{1,0:T(4,128)} %get-tuple-element.74) | copy-start | bytes 6148
  315.2 12.8 %copy-start.43 = (f32[4,128]{1,0:T(4,128)S(1)}, f32[4,128]{1,0:T(4,128)}, u32[]{:S(2)}) copy-start(f32[4,128]{1,0:T(4,128)} %convert_element_type.113) | copy-start | bytes 6148
  315.2 63.6 %copy-start.55 = (f32[768]{0:T(1024)S(1)}, f32[768]{0:T(1024)}, u32[]{:S(2)}) copy-start(f32[768]{0:T(1024)} %get-tuple-element.23) | copy-start | bytes 9220
  315.2 63.6 %copy-start.56 = (f32[768]{0:T(1024)S(1)}, f32[768]{0:T(1024)}, u32[]{:S(2)}) copy-start(f32[768]{0:T(1024)} %get-tuple-element.29) | copy-start | bytes 9220
  318.4 8.2 collective-permute-start.1
  884.2 6.6 copy-start.19
  (45 other events, 63.8 us)
Sparse Core Ops, SparseCore 0:
  41.3 27.4 all-gather.6
  70.9 27.1 all-gather.4
  166.6 43.3 reduce-scatter.5
  212.2 43.3 reduce-scatter.7
  269.7 101.5 reduce-scatter.9
  379.2 218.2 all-reduce.4
  604.0 134.0 reduce-scatter.11
  745.6 134.8 reduce-scatter.13
where the time goes:
time: 908 us; the launch traced here: 901 us
  waiting for transfers between devices  569 us (63%)
  matrix products  106 us (12%)
  blocking collectives  91.1 us (10%)
  local copies, waits for them, and re-layouts  64.7 us (7%)
  other arithmetic  43.7 us (5%)
  between operations  18.3 us (2%)
    psum x1, waiting for transfers between devices, local(): lax.psum((grad_w_patch, grad_b_patch, grad_pos_full, grad_norm1_gain, gra...  173 us
    reduce_scatter x1, waiting for transfers between devices, local(): lax.psum_scatter(grad_w_fc2, ('dp', 'seq'), scatter_dimension=0, tiled=True)  142 us
    reduce_scatter x1, waiting for transfers between devices, local(): lax.psum_scatter(grad_w_fc1, ('dp', 'seq'), scatter_dimension=1, tiled=True)  141 us
    reduce_scatter x1, waiting for transfers between devices, local(): lax.psum_scatter(d_values, 'seq', scatter_dimension=1, tiled=True)  45.6 us
    psum x1, blocking collectives, local(): lax.psum((grad_w_patch, grad_b_patch, grad_pos_full, grad_norm1_gain, gra...  42.7 us
    pmax x1, blocking collectives, local(): top_scale = lax.pmax(local_top, ('dp', 'seq'))  42.7 us
    reduce_scatter x1, waiting for transfers between devices, local(): lax.psum_scatter(d_keys, 'seq', scatter_dimension=1, tiled=True)  31.3 us
    unnamed x177, local copies, waits for them, and re-layouts  30.4 us
  transfers between devices with their start and end apart: 10, of which 7 were waited for; matrix products, arithmetic and copies ran while one was open for 10% of the time, Pallas kernels for 0%

commit v1 on v0

v1 whole, which is shorter than its diff:
```python
import math

import jax
import jax.numpy as jnp
from jax import lax
from jax.sharding import PartitionSpec as P

HEADS = 12
EPS = 1e-05
bf16 = jnp.bfloat16
f32 = jnp.float32
AXES = ("dp", "seq")


def layer_norm(hidden, gain, offset):
    center = hidden - jnp.mean(hidden, axis=-1, keepdims=True)
    spread = jnp.mean(center * center, axis=-1, keepdims=True)
    return center * lax.rsqrt(spread + EPS) * gain + offset


def gelu_tanh(values):
    return jax.nn.gelu(values, approximate=True)


def dot(left, right, a=1, b=0):
    return lax.dot_general(
        left, right, (((a,), (b,)), ((), ())), preferred_element_type=f32
    )


class Cube:
    def __init__(self):
        self.size = lax.axis_size("dp") * lax.axis_size("seq")
        self.nbits = self.size.bit_length() - 1
        self.me = lax.axis_index("dp") * lax.axis_size("seq") + lax.axis_index("seq")
        self.bit = [(self.me >> k) & 1 for k in range(self.nbits)]

    def send(self, block, mask):
        return lax.ppermute(block, AXES, [(i, i ^ mask) for i in range(self.size)])

    def patterns(self, stage):
        out = []
        for m in range(1 << len(stage)):
            out.append({k: (m >> j) & 1 for j, k in enumerate(stage)})
        return out

    def start(self, full):
        rows = full.shape[0] // self.size
        return full.reshape((2,) * self.nbits + (rows, full.shape[1])), list(
            range(self.nbits - 1, -1, -1)
        )

    def pick(self, block, left, pattern):
        for k, m in pattern.items():
            axis = left.index(k)
            block = lax.dynamic_index_in_dim(block, self.bit[k] ^ m, axis, keepdims=False)
            left = [b for b in left if b != k]
        return block

    def scatter(self, block, left, stages):
        for stage in stages:
            total = None
            for pattern in self.patterns(stage):
                part = self.pick(block, left, pattern)
                mask = sum(m << k for k, m in pattern.items())
                if mask:
                    part = self.send(part.astype(bf16), mask).astype(f32)
                total = part if total is None else total + part
            block, left = total, [b for b in left if b not in stage]
        return block, left

    def add_up(self, block):
        for k in [1, 0] + list(range(2, self.nbits)):
            block = block + self.send(block, 1 << k)
        return block

    def gather(self, block, stages):
        order = []
        for stage in stages:
            parts = []
            for pattern in self.patterns(stage):
                mask = sum(m << k for k, m in pattern.items())
                parts.append(self.send(block, mask) if mask else block)
            block = jnp.stack(parts).reshape((2,) * len(stage) + block.shape)
            order = stage[::-1] + order
        for axis, k in enumerate(order):
            block = jnp.where(self.bit[k] == 1, jnp.flip(block, axis), block)
        want = list(range(self.nbits - 1, -1, -1))
        spots = [order.index(k) for k in want]
        rest = list(range(self.nbits, block.ndim))
        block = block.transpose(spots + rest)
        return block.reshape((self.size,) + block.shape[self.nbits :])


def split3(value):
    high = lax.reduce_precision(value, 8, 7)
    rest = value - high
    mid = lax.reduce_precision(rest, 8, 7)
    return [high, mid, rest - mid]


def local(
    patches, labels, valid_mask, class_slot, w_patch, b_patch, pos_embed, class_embed,
    norm1_gain, norm1_shift, w_qkv, w_out, norm2_gain, norm2_shift, w_fc1, b_fc1, w_fc2, b_fc2,
    final_gain, final_shift, w_head, b_head, cot_latent, cot_logdet,
):
    cube = Cube()
    seq_n = lax.axis_size("seq")
    assert seq_n == 2
    seq = lax.axis_index("seq")
    held, span, feat = patches.shape
    items = held // seq_n
    length = span * seq_n
    width = w_out.shape[0]
    head_dim = width // HEADS
    scale = 1.0 / math.sqrt(head_dim)
    rows = items * length
    classes = class_embed.shape[0]

    first = seq * items
    away = (1 - seq) * items
    packed = jnp.concatenate(
        [
            patches.transpose(0, 2, 1).astype(f32),
            cot_latent.transpose(0, 2, 1),
            jnp.broadcast_to(valid_mask.astype(f32)[:, None], (held, 8, span)),
        ],
        axis=1,
    )
    mine = lax.dynamic_slice_in_dim(packed, first, items, 0)
    came = cube.send(lax.dynamic_slice_in_dim(packed, away, items, 0), 1)
    low_half = jnp.where(seq == 0, mine, came)
    high_half = jnp.where(seq == 0, came, mine)
    whole = jnp.concatenate([low_half, high_half], axis=2).transpose(0, 2, 1)
    inputs = whole[:, :, :feat]
    cot = whole[:, :, feat : 2 * feat]
    valid_f = whole[:, :, 2 * feat : 2 * feat + 1]
    my_labels = lax.dynamic_slice_in_dim(labels, first, items, 0)
    my_det = lax.dynamic_slice_in_dim(cot_logdet, first, items, 0)
    class_rows = jnp.concatenate(
        [lax.dynamic_slice_in_dim(class_embed, my_labels[i], 1, 0) for i in range(items)]
    )
    slots = jnp.stack(
        [lax.dynamic_slice_in_dim(class_slot, my_labels[i], 1, 0)[0] for i in range(items)]
    )

    gain1, shift1 = norm1_gain.astype(f32), norm1_shift.astype(f32)
    gain2, shift2 = norm2_gain.astype(f32), norm2_shift.astype(f32)
    gainf, shiftf = final_gain.astype(f32), final_shift.astype(f32)

    shifted = jnp.concatenate(
        [jnp.zeros((items, 1, feat), f32), inputs[:, :-1]], axis=1
    ).astype(bf16)
    flat_in = shifted.reshape(rows, feat)
    hidden0 = dot(flat_in, w_patch).reshape(items, length, width)
    hidden0 = (
        hidden0
        + b_patch.astype(f32)
        + pos_embed.astype(f32)[None]
        + class_rows.astype(f32)[:, None]
    ).reshape(rows, width)
    normed1 = layer_norm(hidden0, gain1, shift1).astype(bf16)
    qkv = dot(normed1, w_qkv).astype(bf16).reshape(items, length, 3, HEADS, head_dim)
    query, keys, values = qkv[:, :, 0], qkv[:, :, 1], qkv[:, :, 2]
    allowed = jnp.arange(length)[None, :] <= jnp.arange(length)[:, None]
    scores = jnp.einsum("bqhd,bkhd->bhqk", query, keys, preferred_element_type=f32) * scale
    scores = jnp.where(allowed[None, None], scores, -1e30)
    probs = jax.nn.softmax(scores, axis=-1)
    probs_low = probs.astype(bf16)
    attended = (
        jnp.einsum("bhqk,bkhd->bqhd", probs_low, values, preferred_element_type=f32)
        .astype(bf16)
        .reshape(rows, width)
    )
    hidden1 = hidden0 + dot(attended, w_out)
    normed2 = layer_norm(hidden1, gain2, shift2).astype(bf16)
    up_values = dot(normed2, w_fc1) + b_fc1.astype(f32)
    act_values = gelu_tanh(up_values).astype(bf16)
    hidden2 = hidden1 + dot(act_values, w_fc2) + b_fc2.astype(f32)
    normed3 = layer_norm(hidden2, gainf, shiftf).astype(bf16)
    head_out = (dot(normed3, w_head) + b_head.astype(f32)).reshape(items, length, 2 * feat)
    shift_part, log_scale = head_out[..., :feat], head_out[..., feat:]
    inverse = jnp.exp(-log_scale)
    moved = (inputs - shift_part) * inverse
    latent = valid_f * moved + (1.0 - valid_f) * inputs
    logdet = -jnp.sum(valid_f * log_scale, axis=(1, 2))
    scale_count = jnp.sum(valid_f) * feat
    local_top = jnp.max(jnp.where(valid_f > 0, log_scale, -1e30))

    d_moved = valid_f * cot
    d_shift = -d_moved * inverse
    d_scale = -d_moved * moved - valid_f * my_det[:, None, None]
    d_head = jnp.concatenate([d_shift, d_scale], axis=-1).astype(bf16).reshape(rows, 2 * feat)
    grad_b_head = jnp.sum(d_head.astype(f32), axis=0)
    grad_w_head_t = dot(d_head, normed3, 0, 0)
    d_normed3 = dot(d_head, w_head, 1, 1)
    d_hidden2, g_fg, g_fs = jax.vjp(layer_norm, hidden2, gainf, shiftf)[1](d_normed3)
    d_mlp = d_hidden2.astype(bf16)
    g_b2 = jnp.sum(d_mlp.astype(f32), axis=0)
    grad_fc2 = dot(act_values, d_mlp, 0, 0)
    core = [1]
    late = [b for b in range(2, cube.nbits)]
    tail = [late[1:][i : i + 2] for i in range(0, len(late) - 1, 2)]
    singles = [[b] for b in late[1:]]
    own_fc2, _ = cube.scatter(*cube.start(grad_fc2), [core, [0], late[:1]] + singles)
    d_act = dot(d_mlp, w_fc2, 1, 1)
    d_up = jax.vjp(gelu_tanh, up_values)[1](d_act)[0].astype(bf16)
    g_b1 = jnp.sum(d_up.astype(f32), axis=0)
    grad_fc1_t = dot(d_up, normed2, 0, 0)
    own_fc1, _ = cube.scatter(*cube.start(grad_fc1_t), [core, late[:1], [0]] + singles)
    d_normed2 = dot(d_up, w_fc1, 1, 1)
    d_part1, g_n2g, g_n2s = jax.vjp(layer_norm, hidden1, gain2, shift2)[1](d_normed2)
    d_hidden1 = d_hidden2 + d_part1
    d_out = d_hidden1.astype(bf16)
    grad_out = dot(attended, d_out, 0, 0)
    d_attended = dot(d_out, w_out, 1, 1).astype(bf16).reshape(items, length, HEADS, head_dim)
    d_probs = jnp.einsum("bqhd,bkhd->bhqk", d_attended, values, preferred_element_type=f32)
    d_scores = (probs * (d_probs - jnp.sum(probs * d_probs, axis=-1, keepdims=True))).astype(bf16)
    d_query = jnp.einsum("bhqk,bkhd->bqhd", d_scores, keys, preferred_element_type=f32) * scale
    d_keys = jnp.einsum("bhqk,bqhd->bkhd", d_scores, query, preferred_element_type=f32) * scale
    d_values = jnp.einsum("bhqk,bqhd->bkhd", probs_low, d_attended, preferred_element_type=f32)
    d_qkv = jnp.stack([d_query, d_keys, d_values], axis=2).astype(bf16).reshape(rows, 3 * width)
    grad_q = dot(normed1, d_qkv[:, :width], 0, 0)
    grad_k = dot(normed1, d_qkv[:, width : 2 * width], 0, 0)
    grad_v = dot(normed1, d_qkv[:, 2 * width :], 0, 0)
    d_normed1 = dot(d_qkv, w_qkv, 1, 1)
    d_part0, g_n1g, g_n1s = jax.vjp(layer_norm, hidden0, gain1, shift1)[1](d_normed1)
    d_hidden0 = d_hidden1 + d_part0
    d_low = d_hidden0.astype(bf16)
    grad_patch = dot(flat_in, d_low, 0, 0)
    d_items = d_hidden0.reshape(items, length, width)
    pos_local = jnp.sum(d_items, axis=0)
    item_sums = jnp.sum(d_items, axis=1)
    g_bp = jnp.sum(item_sums, axis=0)
    d_shifted = dot(d_low, w_patch, 1, 1).reshape(items, length, feat)
    from_shift = jnp.concatenate([d_shifted[:, 1:], jnp.zeros((items, 1, feat), f32)], axis=1)
    grad_in = cot * (1.0 - valid_f) + d_moved * inverse + from_shift

    vectors = jnp.stack(
        [g_bp, g_n1g, g_n1s, g_n2g, g_n2s, g_b2, g_fg, g_fs]
        + [jnp.pad(grad_b_head, (0, width - 2 * feat))]
    )
    b1_rows = g_b1.reshape(-1, width)
    parts = [grad_q, grad_k, grad_v, grad_out, pos_local, grad_w_head_t, grad_patch]
    short = jnp.concatenate([vectors, b1_rows])
    short = cube.add_up(jnp.pad(short, ((0, -short.shape[0] % 8), (0, 0))))
    starts = [0]
    for part in parts:
        starts.append(starts[-1] + part.shape[0])
    chunk = -(-starts[-1] // (16 * cube.size)) * 16
    bulk = jnp.concatenate(parts + [jnp.zeros((chunk * cube.size - starts[-1], width), f32)])
    block, left = cube.start(bulk)
    half = chunk // 2
    one, left1 = cube.scatter(block[..., :half, :], left, [core, [0], late[:1]])
    two, _ = cube.scatter(block[..., half:, :], left, [core, late[:1], [0]])
    both = jnp.concatenate([one, two], axis=-2)
    own, _ = cube.scatter(both, left1, tail)

    scalars = jnp.concatenate(
        [
            jnp.stack(
                split3(jnp.sum(valid_f * log_scale))
                + split3(scale_count)
                + split3(local_top)
            ),
            (slots // 32).astype(f32),
            (slots % 32).astype(f32),
        ]
    )
    extra = jnp.concatenate(
        [item_sums, jnp.pad(scalars, (0, width - scalars.shape[0]))[None]]
    )
    extra = jnp.pad(extra, ((0, 16 - extra.shape[0]), (0, 0)))
    piece = jnp.concatenate([own, extra]).astype(bf16)
    back_tail = tail[::-1]
    gathered = cube.gather(piece, back_tail + [late[:1], [0], core]).astype(f32)
    full = gathered[:, :chunk].reshape(chunk * cube.size, width)
    got = [full[starts[i] : starts[i + 1]] for i in range(len(parts))]
    sums = gathered[:, chunk : chunk + items].reshape(-1, width)
    facts = gathered[:, chunk + items]
    scale_sum = jnp.sum(facts[:, 0] + facts[:, 1] + facts[:, 2])
    count = jnp.sum(facts[:, 3] + facts[:, 4] + facts[:, 5])
    top = jnp.max(facts[:, 6] + facts[:, 7] + facts[:, 8])
    all_slots = (facts[:, 9 : 9 + items] * 32 + facts[:, 9 + items : 9 + 2 * items]).reshape(-1)
    own_rows = classes // cube.size
    wanted = (cube.me * own_rows + jnp.arange(own_rows)).astype(f32)
    hot = (wanted[:, None] == all_slots[None, :]).astype(bf16)
    class_own = dot(hot, sums.astype(bf16))

    result = jnp.concatenate([latent, grad_in], axis=2).transpose(0, 2, 1)
    dets = jnp.broadcast_to(logdet[:, None, None], (items, 8, length))
    result = jnp.concatenate([result, dets], axis=1)
    keep = lax.dynamic_slice_in_dim(result, seq * span, span, 2)
    came = cube.send(lax.dynamic_slice_in_dim(result, (1 - seq) * span, span, 2), 1)
    out = jnp.where(
        seq == 0, jnp.concatenate([keep, came]), jnp.concatenate([came, keep])
    )
    latent_out = out[:, :feat].transpose(0, 2, 1)
    grad_out_in = out[:, feat : 2 * feat].transpose(0, 2, 1)
    logdet_out = out[:, 2 * feat, 0]
    vec = short[:9]
    ff_rows = own_fc1.shape[0]
    b1_own = lax.dynamic_slice_in_dim(short[9 : 9 + b1_rows.shape[0]].reshape(-1), cube.me * ff_rows, ff_rows, 0)
    return (
        latent_out,
        logdet_out,
        grad_out_in,
        got[6],
        vec[0],
        got[4],
        class_own,
        vec[1],
        vec[2],
        jnp.concatenate(got[:3], axis=1),
        got[3],
        vec[3],
        vec[4],
        own_fc1.T,
        b1_own,
        own_fc2,
        vec[5],
        vec[6],
        vec[7],
        got[5].T,
        vec[8, : 2 * feat],
        scale_sum / count,
        top,
    )


def solution(mesh):
    run, item, whole = P("dp", "seq", None), P("dp"), P()
    placed = (run, item, P("dp", "seq")) + (whole,) * 19 + (run, item)
    owned = P(AXES)
    return jax.shard_map(
        local,
        mesh=mesh,
        in_specs=placed,
        out_specs=(run, item, run, whole, whole, whole, P(AXES, None), whole, whole, whole, whole,
                   whole, whole, P(None, AXES), owned, P(AXES, None)) + (whole,) * 7,
        check_vma=False,
    )
```

time: 908 us -> 439 us (0.48)
  waiting for transfers between devices: 569 us -> 119 us
  blocking collectives: 91.1 us -> 0 us
  local copies, waits for them, and re-layouts: 64.7 us -> 107 us
  other arithmetic: 43.7 us -> 82.1 us
  matrix products: 106 us -> 77.6 us
  starting transfers between devices: 7.45 us -> 25.8 us
    reduce_scatter x5 -> x0, waiting for transfers between devices: 360 us -> none  [the longest x1 142 us: local(): lax.psum_scatter(grad_w_fc2, ('dp', 'seq'), scatter_dimension=0, tiled=True)]
    psum x1 -> x0, waiting for transfers between devices: 173 us -> none  [local(): lax.psum((grad_w_patch, grad_b_patch, grad_pos_full, grad_norm1_gain, gra...]
    ppermute x2 -> x32, waiting for transfers between devices: 0.01 us -> 119 us  [send(): return lax.ppermute(block, AXES, [(i, i ^ mask) for i in range(self.size)])]
    psum x2 -> x0, blocking collectives: 48.4 us -> none  [the longest x1 42.7 us: local(): lax.psum((grad_w_patch, grad_b_patch, grad_pos_full, grad_norm1_gain, gra...]
    pmax x1 -> x0, blocking collectives: 42.7 us -> none  [local(): top_scale = lax.pmax(local_top, ('dp', 'seq'))]
    all_gather x2 -> x0, waiting for transfers between devices: 36 us -> none  [the longest x1 22.1 us: local(): lax.all_gather(value_own, 'seq', axis=1, tiled=True)]
    dot_general x26 -> x27, matrix products: 106 us -> 77.6 us  [the longest x21 63.3 us: dot(): lax.dot_general(left, right, (((a,), (b,)), ((), ())), preferred_element_...]
    slice x4 -> x15, local copies, waits for them, and re-layouts: 8.21 us -> 31.4 us  [the longest x3 11.2 us: local(): got = [full[starts[i]:starts[i + 1]] for i in range(len(parts))]]
  transfers between devices with their start and end apart: 10 -> 32, of which waited for: 7 -> 18; matrix products, arithmetic and copies ran while one was open for 10% -> 19% of each run, Pallas kernels for 0% -> 0%
where the time goes in v1:
time: 439 us; the launch traced here: 432 us
  waiting for transfers between devices  119 us (27%)
  local copies, waits for them, and re-layouts  107 us (24%)
  other arithmetic  82.1 us (19%)
  matrix products  77.6 us (18%)
  starting transfers between devices  25.8 us (6%)
  between operations  19.3 us (4%)
    ppermute x32, waiting for transfers between devices, send(): return lax.ppermute(block, AXES, [(i, i ^ mask) for i in range(self.size)])  119 us
    dot_general x21, matrix products, dot(): lax.dot_general(left, right, (((a,), (b,)), ((), ())), preferred_element_...  63.3 us
    ppermute x32, starting transfers between devices, send(): return lax.ppermute(block, AXES, [(i, i ^ mask) for i in range(self.size)])  25.8 us
    unnamed x228, local copies, waits for them, and re-layouts  24.6 us
    add x15, other arithmetic, scatter(): total = part if total is None else total + part  18.2 us
    convert_element_type x16, local copies, waits for them, and re-layouts, scatter(): part = self.send(part.astype(bf16), mask).astype(f32)  16.1 us
    slice x3, local copies, waits for them, and re-layouts, local(): got = [full[starts[i]:starts[i + 1]] for i in range(len(parts))]  11.2 us
  transfers between devices with their start and end apart: 32, of which 18 were waited for; matrix products, arithmetic and copies ran while one was open for 19% of the time, Pallas kernels for 0%

profile of v1, /device:TPU:0, one launch (start us, length us, event | category | flops | bytes accessed | tf_op | source)
XLA Modules:
  0.0 431.7 jit_solution(12857752142642397163)
XLA Ops:
  5.5 2.9 collective-permute-start
  43.9 3.4 convolution_convert_fusion
  47.4 4.3 copy.90
  51.6 6.0 %reshape.347 = bf16[2,256,3,12,64]{1,0,4,3,2:T(2,128)(2,1)} reshape(bf16[512,2304]{0,1:T(8,128)(2,1)} %copy.90) | data formatting | bytes 4718592 | tf_op jit(solution)/shard_map/reshape | solution.py:163
  57.7 2.9 fusion.112
  71.9 2.7 fusion.102
  74.7 4.1 fusion.119
  87.6 2.9 multiply_reduce_fusion.1
  91.9 11.1 %convert_reduce_fusion = (f32[3072]{0:T(1024)}, bf16[512,3072]{1,0:T(8,128)(2,1)S(1)}) fusion(f32[512,3072]{1,0:T(8,128)} %copy-done.92, f32[3072]{0:T(1024)S(1)} %copy-done.77, bf16[512,768]{1,0:T(8,128)(2,1)S(1)} %get-tuple-element.49, bf16[3072,768]{1,0:T(8,128)(2,1)} %param.40), kind=kOutput, calls=%fused_computation.18 | convolution fusion | flops 2452091904 | bytes 14966784 | tf_op jit(solution)/shard_map/dot_general | solution.py:26
  103.0 3.5 multiply_reduce_fusion.2
  112.7 3.1 reshape.350
  115.8 4.2 fusion.28
  120.0 6.9 %multiply_reduce_fusion = (f32[2,12,256]{2,1,0:T(8,128)S(1)}, f32[2,12,256,256]{2,3,1,0:T(8,128)}) fusion(f32[2,12,256,256]{2,3,1,0:T(8,128)} %copy-done.30, f32[2,12,256]{2,1,0:T(8,128)S(1)} %copy-done.53, bf16[2,256,1,12,64]{1,0,4,3,2:T(2,128)(2,1)S(1)} %copy-done.42, bf16[2,256,12,64]{1,0,3,2:T(2,128)(2,1)S(1)} %copy-done.44), kind=kOutput, calls=%fused_computation.20 | convolution fusion | flops 206039040 | bytes 14204928 | tf_op jit(solution)/shard_map/bqhd,bkhd->bhqk/dot_general | solution.py:217
  126.9 4.3 %multiply_convert_fusion = bf16[2,12,256,256]{2,3,1,0:T(8,128)(2,1)S(1)} fusion(f32[2,12,256,256]{2,3,1,0:T(8,128)} %get-tuple-element.113, f32[2,12,256]{2,1,0:T(8,128)S(1)} %get-tuple-element.112, f32[2,12,256,256]{2,3,1,0:T(8,128)S(1)} %bitcast.278, f32[2,12,256]{2,1,0:T(8,128)S(1)} %copy-done.53), kind=kLoop, calls=%fused_computation.19 | loop fusion | flops 6291456 | bytes 15777792 | tf_op jit(solution)/shard_map/convert_element_type | solution.py:218
  133.2 2.5 copy.106
  137.1 3.0 multiply_reduce_fusion.3
  142.9 2.5 convolution_dynamic-update-slice_fusion.2
  154.0 7.8 %fusion.111 = (f32[2,2,2,2,2,56,768]{6,5,4,3,2,1,0:T(8,128)S(1)}, f32[2,2,2,2,2,56,768]{6,5,4,3,2,1,0:T(8,128)}) fusion(f32[2,2,2,2,2,112,768]{6,5,4,3,2,1,0:T(8,128)} %bitcast.21), kind=kLoop, calls=%fused_computation.293 | loop fusion | bytes 22020096 | tf_op jit(solution)/shard_map/slice | solution.py:255
  161.8 5.0 %fusion.27 = bf16[2,2,2,2,56,768]{5,4,1,0,2,3:T(8,128)(2,1)} fusion(f32[2,2,2,2,2,56,768]{6,5,4,3,2,1,0:T(8,128)} %get-tuple-element.65, s32[]{:T(128)S(6)} %select_n.195), kind=kLoop, calls=%fused_computation.93 | loop fusion | bytes 2752516 | tf_op jit(solution)/shard_map/convert_element_type | solution.py:67
  166.9 10.1 %fusion.104 = f32[3072,768]{1,0:T(8,128)} fusion(bf16[512,768]{1,0:T(8,128)(2,1)S(1)} %copy-done.46, f32[512,3072]{1,0:T(8,128)} %copy-done.92, f32[3072]{0:T(1024)S(1)} %copy-done.78), kind=kOutput, calls=%fused_computation.287 | convolution fusion | flops 2431647744 | bytes 16527360 | tf_op jit(solution)/shard_map/dot_general | solution.py:26
  182.4 4.2 fusion.15
  186.6 4.8 %fusion.101 = f32[3072,768]{1,0:T(8,128)S(1)} fusion(bf16[512,3072]{1,0:T(8,128)(2,1)} %copy-done.93, f32[512,768]{1,0:T(8,128)S(1)} %copy-done.16, f32[768]{0:T(1024)S(1)} %copy-done.87, f32[768]{0:T(1024)S(1)} %copy-done.74, f32[512]{0:T(512)S(1)} %copy-done.81, f32[512]{0:T(512)S(1)} %copy-done.56), kind=kOutput, calls=%fused_computation.284 | convolution fusion | flops 2417885184 | bytes 14166016 | tf_op jit(solution)/shard_map/dot_general | solution.py:26
  191.5 2.7 fusion.13
  203.5 10.1 %collective-permute-done.3 = bf16[2,2,2,56,768]{4,3,1,0,2:T(8,128)(2,1)S(1)} collective-permute-done((bf16[2,2,2,56,768]{4,3,1,0,2:T(8,128)(2,1)}, bf16[2,2,2,56,768]{4,3,1,0,2:T(8,128)(2,1)S(1)}, u32[]{:S(2)}, u32[]{:S(2)}) %collective-permute-start.3) | collective-permute-done | bytes 688160 | tf_op jit(solution)/shard_map/ppermute | solution.py:39
  218.5 6.4 %collective-permute-done.4 = bf16[2,2,56,768]{3,2,1,0:T(8,128)(2,1)S(1)} collective-permute-done((bf16[2,2,56,768]{3,2,1,0:T(8,128)(2,1)S(1)}, bf16[2,2,56,768]{3,2,1,0:T(8,128)(2,1)S(1)}, u32[]{:S(2)}, u32[]{:S(2)}) %collective-permute-start.4) | collective-permute-done | bytes 344096 | tf_op jit(solution)/shard_map/ppermute | solution.py:39
  229.0 2.6 collective-permute-start.9
  240.7 4.0 concatenate.91
  244.9 3.7 collective-permute-start.13
  249.4 5.2 %collective-permute-done.13 = bf16[128,768]{1,0:T(8,128)(2,1)S(1)} collective-permute-done((bf16[128,768]{1,0:T(8,128)(2,1)S(1)}, bf16[128,768]{1,0:T(8,128)(2,1)S(1)}, u32[]{:S(2)}, u32[]{:S(2)}) %collective-permute-start.13) | collective-permute-done | bytes 196640 | tf_op jit(solution)/shard_map/ppermute | solution.py:39
  254.6 9.2 %collective-permute-done.12 = bf16[128,768]{1,0:T(8,128)(2,1)S(1)} collective-permute-done((bf16[128,768]{1,0:T(8,128)(2,1)S(1)}, bf16[128,768]{1,0:T(8,128)(2,1)S(1)}, u32[]{:S(2)}, u32[]{:S(2)}) %collective-permute-start.12) | collective-permute-done | bytes 196640 | tf_op jit(solution)/shard_map/ppermute | solution.py:39
  267.4 15.3 %collective-permute-done.14 = bf16[2,2,128,768]{3,2,1,0:T(8,128)(2,1)S(1)} collective-permute-done((bf16[2,2,128,768]{3,2,1,0:T(8,128)(2,1)S(1)}, bf16[2,2,128,768]{3,2,1,0:T(8,128)(2,1)S(1)}, u32[]{:S(2)}, u32[]{:S(2)}) %collective-permute-start.14) | collective-permute-done | bytes 786464 | tf_op jit(solution)/shard_map/ppermute | solution.py:39
  283.6 2.5 fusion.100
  289.9 3.6 bitcast_add_fusion
  295.6 3.6 bitcast_add_fusion.1
  303.0 22.9 %collective-permute-done.1 = f32[2,104,128]{2,1,0:T(8,128)S(1)} collective-permute-done((f32[2,104,128]{2,1,0:T(8,128)S(1)}, f32[2,104,128]{2,1,0:T(8,128)S(1)}, u32[]{:S(2)}, u32[]{:S(2)}) %collective-permute-start.1) | collective-permute-done | bytes 106528 | tf_op jit(solution)/shard_map/ppermute | solution.py:39
  326.7 3.4 collective-permute-done.20
  331.1 4.1 collective-permute-done.21
  338.5 10.2 %collective-permute-done.28 = bf16[2,2,2,96,768]{4,3,0,1,2:T(8,128)(2,1)} collective-permute-done((bf16[2,2,2,96,768]{4,3,0,1,2:T(8,128)(2,1)S(1)}, bf16[2,2,2,96,768]{4,3,0,1,2:T(8,128)(2,1)}, u32[]{:S(2)}, u32[]{:S(2)}) %collective-permute-start.28) | collective-permute-done | bytes 1179680 | tf_op jit(solution)/shard_map/ppermute | solution.py:39
  354.5 8.8 %collective-permute-done.29 = bf16[2,2,96,768]{3,2,0,1:T(8,128)(2,1)S(1)} collective-permute-done((bf16[2,2,96,768]{3,2,0,1:T(8,128)(2,1)S(1)}, bf16[2,2,96,768]{3,2,0,1:T(8,128)(2,1)S(1)}, u32[]{:S(2)}, u32[]{:S(2)}) %collective-permute-start.29) | collective-permute-done | bytes 589856 | tf_op jit(solution)/shard_map/ppermute | solution.py:39
  363.5 2.7 collective-permute-done.24
  366.4 7.3 %collective-permute-done.30 = bf16[2,96,768]{2,1,0:T(8,128)(2,1)S(1)} collective-permute-done((bf16[2,96,768]{2,1,0:T(8,128)(2,1)S(1)}, bf16[2,96,768]{2,1,0:T(8,128)(2,1)S(1)}, u32[]{:S(2)}, u32[]{:S(2)}) %collective-permute-start.30) | collective-permute-done | bytes 294944 | tf_op jit(solution)/shard_map/ppermute | solution.py:39
  373.9 3.5 collective-permute-done.25
  377.7 4.0 collective-permute-done.31
  382.4 2.7 collective-permute-done.26
  387.6 2.5 pad_maximum_fusion.1
  402.0 5.2 %slice.237 = f32[32,112,768]{2,1,0:T(8,128)} slice(f32[32,128,768]{2,1,0:T(8,128)S(1)} %bitcast_convert_fusion), slice={[0:32], [0:112], [0:768]} | slice | bytes 22020096 | tf_op jit(solution)/shard_map/slice | solution.py:277
  413.3 7.6 %fusion.110 = (f32[768,768]{1,0:T(8,128)}, f32[768,768]{1,0:T(8,128)}, f32[768,768]{1,0:T(8,128)}, f32[768,768]{1,0:T(8,128)}) fusion(f32[3584,768]{1,0:T(8,128)} %bitcast.261), kind=kLoop, calls=%fused_computation.292 | loop fusion | bytes 18874368 | tf_op jit(solution)/shard_map/slice | solution.py:278
  424.3 5.7 %pad_maximum_fusion = f32[768,2304]{1,0:T(8,128)} fusion(f32[768,768]{1,0:T(8,128)} %get-tuple-element.61, f32[768,768]{1,0:T(8,128)} %get-tuple-element.62, f32[768,768]{1,0:T(8,128)} %get-tuple-element.63), kind=kLoop, calls=%fused_computation.8 | loop fusion | flops 3538944 | bytes 14155776 | tf_op jit(solution)/shard_map/concatenate | solution.py:314
  (450 shorter events, 150.8 us)
Async XLA Ops:
  0.7 43.3 %copy-start = (bf16[768,2304]{1,0:T(8,128)(2,1)S(1)}, bf16[768,2304]{1,0:T(8,128)(2,1)}, u32[]{:S(2)}) copy-start(bf16[768,2304]{1,0:T(8,128)(2,1)} %param.34) | copy-start | bytes 10616836
  5.5 29.5 %collective-permute-start = (f32[2,104,128]{2,1,0:T(8,128)}, f32[2,104,128]{2,1,0:T(8,128)}, u32[]{:S(2)}, u32[]{:S(2)}) collective-permute-start(f32[2,104,128]{2,1,0:T(8,128)} %constant_dynamic-slice_fusion.8), channel_id=1, source_target_pairs={{0,1},{1,0},{2,3},{3,2},{4,5},{5,4},{6,7},{7,6},{8,9},{9,8},{10,11... | collective-permute-start | bytes 319496 | tf_op jit(solution)/shard_map/ppermute | solution.py:39
  166.8 24.7 %collective-permute-start.2 = (bf16[2,2,2,2,56,768]{5,4,1,0,2,3:T(8,128)(2,1)}, bf16[2,2,2,2,56,768]{5,4,1,0,2,3:T(8,128)(2,1)}, u32[]{:S(2)}, u32[]{:S(2)}) collective-permute-start(bf16[2,2,2,2,56,768]{5,4,1,0,2,3:T(8,128)(2,1)} %fusion.27), channel_id=1, source_target_pairs={{0,2},{1,3},{2,0},{3,1},{4,6},{5,7},{6,4},{7,5},{8,10},{9,11},{10,... | collective-permute-start | bytes 4128776 | tf_op jit(solution)/shard_map/ppermute | solution.py:39
  166.8 19.8 %copy-start.74 = (f32[768]{0:T(1024)S(1)}, f32[768]{0:T(1024)}, u32[]{:S(2)}) copy-start(f32[768]{0:T(1024)} %convert_element_type.335) | copy-start | bytes 9220
  166.8 19.8 %copy-start.81 = (f32[512]{0:T(512)S(1)}, f32[512]{0:T(512)}, u32[]{:S(2)}) copy-start(f32[512]{0:T(512)} %copy-done.79) | copy-start | bytes 6148
  166.8 19.8 %copy-start.87 = (f32[768]{0:T(1024)S(1)}, f32[768]{0:T(1024)}, u32[]{:S(2)}) copy-start(f32[768]{0:T(1024)} %convert_element_type.336) | copy-start | bytes 9220
  178.2 17.3 %collective-permute-start.5 = (bf16[2,2,2,2,56,768]{5,4,3,2,1,0:T(8,128)(2,1)}, bf16[2,2,2,2,56,768]{5,4,3,2,1,0:T(8,128)(2,1)}, u32[]{:S(2)}, u32[]{:S(2)}) collective-permute-start(bf16[2,2,2,2,56,768]{5,4,3,2,1,0:T(8,128)(2,1)} %fusion.26), channel_id=1, source_target_pairs={{0,2},{1,3},{2,0},{3,1},{4,6},{5,7},{6,4},{7,5},{8,10},{9,11},{10,... | collective-permute-start | bytes 4128776 | tf_op jit(solution)/shard_map/ppermute | solution.py:39
  186.6 103.3 %collective-permute-start.27 = (bf16[2,2,2,2,96,768]{5,4,0,1,2,3:T(8,128)(2,1)}, bf16[2,2,2,2,96,768]{5,4,0,1,2,3:T(8,128)(2,1)}, u32[]{:S(2)}, u32[]{:S(2)}) collective-permute-start(bf16[2,2,2,2,96,768]{5,4,0,1,2,3:T(8,128)(2,1)} %fusion.15), channel_id=1, source_target_pairs={{0,2},{1,3},{2,0},{3,1},{4,6},{5,7},{6,4},{7,5},{8,10},{9,11},{10,... | collective-permute-start | bytes 7077896 | tf_op jit(solution)/shard_map/ppermute | solution.py:39
  195.5 18.1 %collective-permute-start.3 = (bf16[2,2,2,56,768]{4,3,1,0,2:T(8,128)(2,1)}, bf16[2,2,2,56,768]{4,3,1,0,2:T(8,128)(2,1)S(1)}, u32[]{:S(2)}, u32[]{:S(2)}) collective-permute-start(bf16[2,2,2,56,768]{4,3,1,0,2:T(8,128)(2,1)} %fusion.45), channel_id=1, source_target_pairs={{0,1},{1,0},{2,3},{3,2},{4,5},{5,4},{6,7},{7,6},{8,9},{9,8},{10,11... | collective-permute-start | bytes 2064392 | tf_op jit(solution)/shard_map/ppermute | solution.py:39
  199.0 18.1 %collective-permute-start.6 = (bf16[2,2,2,56,768]{4,3,2,1,0:T(8,128)(2,1)}, bf16[2,2,2,56,768]{4,3,2,1,0:T(8,128)(2,1)S(1)}, u32[]{:S(2)}, u32[]{:S(2)}) collective-permute-start(bf16[2,2,2,56,768]{4,3,2,1,0:T(8,128)(2,1)} %fusion.46), channel_id=1, source_target_pairs={{0,4},{1,5},{2,6},{3,7},{4,0},{5,1},{6,2},{7,3},{8,12},{9,13},{10,... | collective-permute-start | bytes 2064392 | tf_op jit(solution)/shard_map/ppermute | solution.py:39
  202.1 93.5 %collective-permute-start.22 = (bf16[2,2,2,2,96,768]{5,4,0,1,3,2:T(8,128)(2,1)}, bf16[2,2,2,2,96,768]{5,4,0,1,3,2:T(8,128)(2,1)}, u32[]{:S(2)}, u32[]{:S(2)}) collective-permute-start(bf16[2,2,2,2,96,768]{5,4,0,1,3,2:T(8,128)(2,1)} %fusion.14), channel_id=1, source_target_pairs={{0,2},{1,3},{2,0},{3,1},{4,6},{5,7},{6,4},{7,5},{8,10},{9,11},{10,... | collective-permute-start | bytes 7077896 | tf_op jit(solution)/shard_map/ppermute | solution.py:39
  215.1 9.8 %collective-permute-start.4 = (bf16[2,2,56,768]{3,2,1,0:T(8,128)(2,1)S(1)}, bf16[2,2,56,768]{3,2,1,0:T(8,128)(2,1)S(1)}, u32[]{:S(2)}, u32[]{:S(2)}) collective-permute-start(bf16[2,2,56,768]{3,2,1,0:T(8,128)(2,1)S(1)} %fusion.54), channel_id=1, source_target_pairs={{0,4},{1,5},{2,6},{3,7},{4,0},{5,1},{6,2},{7,3},{8,12},{9,13},{10,... | collective-permute-start | bytes 1032200 | tf_op jit(solution)/shard_map/ppermute | solution.py:39
  217.3 9.8 %collective-permute-start.7 = (bf16[2,2,56,768]{3,2,1,0:T(8,128)(2,1)S(1)}, bf16[2,2,56,768]{3,2,1,0:T(8,128)(2,1)S(1)}, u32[]{:S(2)}, u32[]{:S(2)}) collective-permute-start(bf16[2,2,56,768]{3,2,1,0:T(8,128)(2,1)S(1)} %fusion.55), channel_id=1, source_target_pairs={{0,1},{1,0},{2,3},{3,2},{4,5},{5,4},{6,7},{7,6},{8,9},{9,8},{10,11... | collective-permute-start | bytes 1032200 | tf_op jit(solution)/shard_map/ppermute | solution.py:39
  225.0 15.7 %copy-start.89 = (bf16[2]{0:T(256)(128)(2,1)S(1)}, bf16[2]{0:T(256)(128)(2,1)}, u32[]{:S(2)}) copy-start(bf16[2]{0:T(256)(128)(2,1)} %get-tuple-element.52) | copy-start | bytes 16
  225.0 15.7 %copy-start.90 = (bf16[2]{0:T(256)(128)(2,1)S(1)}, bf16[2]{0:T(256)(128)(2,1)}, u32[]{:S(2)}) copy-start(bf16[2]{0:T(256)(128)(2,1)} %fusion.94) | copy-start | bytes 16
  227.3 38.3 %copy-start.70 = (f32[768]{0:T(1024)S(1)}, f32[768]{0:T(1024)}, u32[]{:S(2)}) copy-start(f32[768]{0:T(1024)} %get-tuple-element.23) | copy-start | bytes 9220
  227.3 38.3 %copy-start.69 = (f32[768]{0:T(1024)S(1)}, f32[768]{0:T(1024)}, u32[]{:S(2)}) copy-start(f32[768]{0:T(1024)} %get-tuple-element.29) | copy-start | bytes 9220
  227.3 17.5 %collective-permute-start.8 = (bf16[112,768]{1,0:T(8,128)(2,1)S(1)}, bf16[112,768]{1,0:T(8,128)(2,1)S(1)}, u32[]{:S(2)}, u32[]{:S(2)}) collective-permute-start(bf16[112,768]{1,0:T(8,128)(2,1)S(1)} %get-tuple-element.75), channel_id=1, source_target_pairs={{0,8},{1,9},{2,10},{3,11},{4,12},{5,13},{6,14},{7,15},{8,0},{9,1},... | collective-permute-start | bytes 516104 | tf_op jit(solution)/shard_map/ppermute | solution.py:39
  229.0 15.8 %collective-permute-start.9 = (bf16[112,768]{1,0:T(8,128)(2,1)S(1)}, bf16[112,768]{1,0:T(8,128)(2,1)S(1)}, u32[]{:S(2)}, u32[]{:S(2)}) collective-permute-start(bf16[112,768]{1,0:T(8,128)(2,1)S(1)} %get-tuple-element.76), channel_id=1, source_target_pairs={{0,16},{1,17},{2,18},{3,19},{4,20},{5,21},{6,22},{7,23},{8,24},{9,... | collective-permute-start | bytes 516104 | tf_op jit(solution)/shard_map/ppermute | solution.py:39
  231.5 13.2 %collective-permute-start.10 = (bf16[112,768]{1,0:T(8,128)(2,1)S(1)}, bf16[112,768]{1,0:T(8,128)(2,1)S(1)}, u32[]{:S(2)}, u32[]{:S(2)}) collective-permute-start(bf16[112,768]{1,0:T(8,128)(2,1)S(1)} %get-tuple-element.77), channel_id=1, source_target_pairs={{0,24},{1,25},{2,26},{3,27},{4,28},{5,29},{6,30},{7,31},{8,16},{9,... | collective-permute-start | bytes 516104 | tf_op jit(solution)/shard_map/ppermute | solution.py:39
  231.8 33.9 %copy-start.75 = (f32[3072]{0:T(1024)S(1)}, f32[3072]{0:T(1024)}, u32[]{:S(2)}) copy-start(f32[3072]{0:T(1024)} %get-tuple-element.46) | copy-start | bytes 36868
  231.8 33.9 %copy-start.83 = (f32[768]{0:T(1024)S(1)}, f32[768]{0:T(1024)}, u32[]{:S(2)}) copy-start(f32[768]{0:T(1024)} %get-tuple-element.25) | copy-start | bytes 9220
  231.8 33.9 %copy-start.82 = (f32[768]{0:T(1024)S(1)}, f32[768]{0:T(1024)}, u32[]{:S(2)}) copy-start(f32[768]{0:T(1024)} %get-tuple-element.30) | copy-start | bytes 9220
  231.8 33.9 %copy-start.85 = (f32[768]{0:T(1024)S(1)}, f32[768]{0:T(1024)}, u32[]{:S(2)}) copy-start(f32[768]{0:T(1024)} %get-tuple-element.27) | copy-start | bytes 9220
  231.8 33.9 %copy-start.84 = (f32[768]{0:T(1024)S(1)}, f32[768]{0:T(1024)}, u32[]{:S(2)}) copy-start(f32[768]{0:T(1024)} %get-tuple-element.31) | copy-start | bytes 9220
  233.4 32.5 %copy-start.48 = (f32[2,256,48]{1,2,0:T(8,128)S(1)}, f32[2,256,48]{1,2,0:T(8,128)}, u32[]{:S(2)}) copy-start(f32[2,256,48]{1,2,0:T(8,128)} %get-tuple-element.78) | copy-start | bytes 294916
  244.9 9.7 %collective-permute-start.13 = (bf16[128,768]{1,0:T(8,128)(2,1)S(1)}, bf16[128,768]{1,0:T(8,128)(2,1)S(1)}, u32[]{:S(2)}, u32[]{:S(2)}) collective-permute-start(bf16[128,768]{1,0:T(8,128)(2,1)S(1)} %pad_maximum_fusion.7), channel_id=1, source_target_pairs={{0,24},{1,25},{2,26},{3,27},{4,28},{5,29},{6,30},{7,31},{8,16},{9,... | collective-permute-start | bytes 589832 | tf_op jit(solution)/shard_map/ppermute | solution.py:39
  248.6 15.2 %collective-permute-start.12 = (bf16[128,768]{1,0:T(8,128)(2,1)S(1)}, bf16[128,768]{1,0:T(8,128)(2,1)S(1)}, u32[]{:S(2)}, u32[]{:S(2)}) collective-permute-start(bf16[128,768]{1,0:T(8,128)(2,1)S(1)} %pad_maximum_fusion.7), channel_id=1, source_target_pairs={{0,16},{1,17},{2,18},{3,19},{4,20},{5,21},{6,22},{7,23},{8,24},{9,... | collective-permute-start | bytes 589832 | tf_op jit(solution)/shard_map/ppermute | solution.py:39
  248.6 15.2 %collective-permute-start.11 = (bf16[128,768]{1,0:T(8,128)(2,1)S(1)}, bf16[128,768]{1,0:T(8,128)(2,1)S(1)}, u32[]{:S(2)}, u32[]{:S(2)}) collective-permute-start(bf16[128,768]{1,0:T(8,128)(2,1)S(1)} %pad_maximum_fusion.7), channel_id=1, source_target_pairs={{0,8},{1,9},{2,10},{3,11},{4,12},{5,13},{6,14},{7,15},{8,0},{9,1},... | collective-permute-start | bytes 589832 | tf_op jit(solution)/shard_map/ppermute | solution.py:39
  263.9 18.9 %collective-permute-start.14 = (bf16[2,2,128,768]{3,2,1,0:T(8,128)(2,1)S(1)}, bf16[2,2,128,768]{3,2,1,0:T(8,128)(2,1)S(1)}, u32[]{:S(2)}, u32[]{:S(2)}) collective-permute-start(bf16[2,2,128,768]{3,2,1,0:T(8,128)(2,1)S(1)} %bitcast.283), channel_id=1, source_target_pairs={{0,4},{1,5},{2,6},{3,7},{4,0},{5,1},{6,2},{7,3},{8,12},{9,13},{10,... | collective-permute-start | bytes 2359304 | tf_op jit(solution)/shard_map/ppermute | solution.py:39
  265.9 1.3 collective-permute-start.17
  267.2 21.1 %collective-permute-start.18 = (f32[16,768]{1,0:T(8,128)S(1)}, f32[16,768]{1,0:T(8,128)S(1)}, u32[]{:S(2)}, u32[]{:S(2)}) collective-permute-start(f32[16,768]{1,0:T(8,128)S(1)} %pad_add_fusion.2), channel_id=1, source_target_pairs={{0,1},{1,0},{2,3},{3,2},{4,5},{5,4},{6,7},{7,6},{8,9},{9,8},{10,11... | collective-permute-start | bytes 147464 | tf_op jit(solution)/shard_map/ppermute | solution.py:39
  286.1 49.7 %collective-permute-start.15 = (bf16[2,2,2,128,768]{4,3,2,1,0:T(8,128)(2,1)}, bf16[2,2,2,128,768]{4,3,2,1,0:T(8,128)(2,1)}, u32[]{:S(2)}, u32[]{:S(2)}) collective-permute-start(bf16[2,2,2,128,768]{4,3,2,1,0:T(8,128)(2,1)} %get-tuple-element.72), channel_id=1, source_target_pairs={{0,1},{1,0},{2,3},{3,2},{4,5},{5,4},{6,7},{7,6},{8,9},{9,8},{10,11... | collective-permute-start | bytes 4718600 | tf_op jit(solution)/shard_map/ppermute | solution.py:39
  286.2 39.7 %collective-permute-start.1 = (f32[2,104,128]{2,1,0:T(8,128)S(1)}, f32[2,104,128]{2,1,0:T(8,128)S(1)}, u32[]{:S(2)}, u32[]{:S(2)}) collective-permute-start(f32[2,104,128]{2,1,0:T(8,128)S(1)} %get-tuple-element.90), channel_id=1, source_target_pairs={{0,1},{1,0},{2,3},{3,2},{4,5},{5,4},{6,7},{7,6},{8,9},{9,8},{10,11... | collective-permute-start | bytes 319496 | tf_op jit(solution)/shard_map/ppermute | solution.py:39
  288.3 37.6 %collective-permute-start.19 = (f32[16,768]{1,0:T(8,128)S(1)}, f32[16,768]{1,0:T(8,128)S(1)}, u32[]{:S(2)}, u32[]{:S(2)}) collective-permute-start(f32[16,768]{1,0:T(8,128)S(1)} %add.441), channel_id=1, source_target_pairs={{0,4},{1,5},{2,6},{3,7},{4,0},{5,1},{6,2},{7,3},{8,12},{9,13},{10,... | collective-permute-start | bytes 147464 | tf_op jit(solution)/shard_map/ppermute | solution.py:39
  293.6 55.1 %collective-permute-start.28 = (bf16[2,2,2,96,768]{4,3,0,1,2:T(8,128)(2,1)S(1)}, bf16[2,2,2,96,768]{4,3,0,1,2:T(8,128)(2,1)}, u32[]{:S(2)}, u32[]{:S(2)}) collective-permute-start(bf16[2,2,2,96,768]{4,3,0,1,2:T(8,128)(2,1)S(1)} %fusion.37), channel_id=1, source_target_pairs={{0,1},{1,0},{2,3},{3,2},{4,5},{5,4},{6,7},{7,6},{8,9},{9,8},{10,11... | collective-permute-start | bytes 3538952 | tf_op jit(solution)/shard_map/ppermute | solution.py:39
  302.5 49.5 %collective-permute-start.23 = (bf16[2,2,2,96,768]{4,3,0,1,2:T(8,128)(2,1)}, bf16[2,2,2,96,768]{4,3,0,1,2:T(8,128)(2,1)}, u32[]{:S(2)}, u32[]{:S(2)}) collective-permute-start(bf16[2,2,2,96,768]{4,3,0,1,2:T(8,128)(2,1)} %fusion.36), channel_id=1, source_target_pairs={{0,4},{1,5},{2,6},{3,7},{4,0},{5,1},{6,2},{7,3},{8,12},{9,13},{10,... | collective-permute-start | bytes 3538952 | tf_op jit(solution)/shard_map/ppermute | solution.py:39
  326.0 4.2 collective-permute-start.20
  330.1 5.0 %collective-permute-start.21 = (f32[16,768]{1,0:T(8,128)S(1)}, f32[16,768]{1,0:T(8,128)S(1)}, u32[]{:S(2)}, u32[]{:S(2)}) collective-permute-start(f32[16,768]{1,0:T(8,128)S(1)} %add.443), channel_id=1, source_target_pairs={{0,16},{1,17},{2,18},{3,19},{4,20},{5,21},{6,22},{7,23},{8,24},{9,... | collective-permute-start | bytes 147464 | tf_op jit(solution)/shard_map/ppermute | solution.py:39
  335.2 16.8 %slice-start.4 = ((s8[4718592]{0:T(1024)(128)(4,1)}), s8[524288]{0:T(1024)(128)(4,1)S(1)}, s32[]{:S(2)}) async-start(s8[4718592]{0:T(1024)(128)(4,1)} %bitcast.268), calls=%async_computation.4 | async-start | bytes 1048576
  335.8 16.2 %slice-start.5 = ((s8[4718592]{0:T(1024)(128)(4,1)}), s8[4194304]{0:T(1024)(128)(4,1)S(1)}, s32[]{:S(2)}) async-start(s8[4718592]{0:T(1024)(128)(4,1)} %bitcast.268), calls=%async_computation.5 | async-start | bytes 8388608
  337.8 48.1 %collective-permute-start.16 = (bf16[2,2,2,2,128,768]{5,4,3,2,1,0:T(8,128)(2,1)S(1)}, bf16[2,2,2,2,128,768]{5,4,3,2,1,0:T(8,128)(2,1)S(1)}, u32[]{:S(2)}, u32[]{:S(2)}) collective-permute-start(bf16[2,2,2,2,128,768]{5,4,3,2,1,0:T(8,128)(2,1)S(1)} %get-tuple-element.67), channel_id=1, source_target_pairs={{0,2},{1,3},{2,0},{3,1},{4,6},{5,7},{6,4},{7,5},{8,10},{9,11},{10,... | collective-permute-start | bytes 9437192 | tf_op jit(solution)/shard_map/ppermute | solution.py:39
  350.4 12.8 %collective-permute-start.29 = (bf16[2,2,96,768]{3,2,0,1:T(8,128)(2,1)S(1)}, bf16[2,2,96,768]{3,2,0,1:T(8,128)(2,1)S(1)}, u32[]{:S(2)}, u32[]{:S(2)}) collective-permute-start(bf16[2,2,96,768]{3,2,0,1:T(8,128)(2,1)S(1)} %fusion.48), channel_id=1, source_target_pairs={{0,4},{1,5},{2,6},{3,7},{4,0},{5,1},{6,2},{7,3},{8,12},{9,13},{10,... | collective-permute-start | bytes 1769480 | tf_op jit(solution)/shard_map/ppermute | solution.py:39
  353.6 12.5 %collective-permute-start.24 = (bf16[2,2,96,768]{3,2,0,1:T(8,128)(2,1)S(1)}, bf16[2,2,96,768]{3,2,0,1:T(8,128)(2,1)S(1)}, u32[]{:S(2)}, u32[]{:S(2)}) collective-permute-start(bf16[2,2,96,768]{3,2,0,1:T(8,128)(2,1)S(1)} %fusion.47), channel_id=1, source_target_pairs={{0,1},{1,0},{2,3},{3,2},{4,5},{5,4},{6,7},{7,6},{8,9},{9,8},{10,11... | collective-permute-start | bytes 1769480 | tf_op jit(solution)/shard_map/ppermute | solution.py:39
  363.4 10.3 %collective-permute-start.30 = (bf16[2,96,768]{2,1,0:T(8,128)(2,1)S(1)}, bf16[2,96,768]{2,1,0:T(8,128)(2,1)S(1)}, u32[]{:S(2)}, u32[]{:S(2)}) collective-permute-start(bf16[2,96,768]{2,1,0:T(8,128)(2,1)S(1)} %fusion.69), channel_id=1, source_target_pairs={{0,8},{1,9},{2,10},{3,11},{4,12},{5,13},{6,14},{7,15},{8,0},{9,1},... | collective-permute-start | bytes 884744 | tf_op jit(solution)/shard_map/ppermute | solution.py:39
  366.3 11.1 %collective-permute-start.25 = (bf16[2,96,768]{2,1,0:T(8,128)(2,1)S(1)}, bf16[2,96,768]{2,1,0:T(8,128)(2,1)S(1)}, u32[]{:S(2)}, u32[]{:S(2)}) collective-permute-start(bf16[2,96,768]{2,1,0:T(8,128)(2,1)S(1)} %fusion.68), channel_id=1, source_target_pairs={{0,8},{1,9},{2,10},{3,11},{4,12},{5,13},{6,14},{7,15},{8,0},{9,1},... | collective-permute-start | bytes 884744 | tf_op jit(solution)/shard_map/ppermute | solution.py:39
  373.8 7.9 %collective-permute-start.31 = (bf16[96,768]{1,0:T(8,128)(2,1)S(1)}, bf16[96,768]{1,0:T(8,128)(2,1)S(1)}, u32[]{:S(2)}, u32[]{:S(2)}) collective-permute-start(bf16[96,768]{1,0:T(8,128)(2,1)S(1)} %fusion.75), channel_id=1, source_target_pairs={{0,16},{1,17},{2,18},{3,19},{4,20},{5,21},{6,22},{7,23},{8,24},{9,... | collective-permute-start | bytes 442376 | tf_op jit(solution)/shard_map/ppermute | solution.py:39
  377.5 7.7 %collective-permute-start.26 = (bf16[96,768]{1,0:T(8,128)(2,1)S(1)}, bf16[96,768]{1,0:T(8,128)(2,1)S(1)}, u32[]{:S(2)}, u32[]{:S(2)}) collective-permute-start(bf16[96,768]{1,0:T(8,128)(2,1)S(1)} %fusion.74), channel_id=1, source_target_pairs={{0,16},{1,17},{2,18},{3,19},{4,20},{5,21},{6,22},{7,23},{8,24},{9,... | collective-permute-start | bytes 442376 | tf_op jit(solution)/shard_map/ppermute | solution.py:39
  (92 other events, 427.3 us)

commit v2 on v1

v2 whole, which is shorter than its diff:
```python
import math
from functools import partial

import jax
import jax.numpy as jnp
from jax import lax
from jax.experimental import pallas as pl
from jax.experimental.pallas import tpu as pltpu
from jax.sharding import PartitionSpec as P

HEADS = 12
EPS = 1e-05
GELU_A = math.sqrt(2.0 / math.pi)
GELU_B = 0.044715
bf16 = jnp.bfloat16
f32 = jnp.float32
AXES = ("dp", "seq")
ROW = dict(bp=0, n1g=1, n1s=2, n2g=3, n2s=4, b2=5, fg=6, fs=7, bh=8, b1=9)
VEC = dict(bp=0, n1g=1, n1s=2, n2g=3, n2s=4, b2=5, fg=6, fs=7, b1=8, cls=12)


def dot(left, right, a=1, b=0):
    return lax.dot_general(
        left, right, (((a,), (b,)), ((), ())), preferred_element_type=f32
    )


def call(body, outs, args, name, flops, limit, smem=()):
    specs = [
        pl.BlockSpec(memory_space=pltpu.SMEM if i in smem else pltpu.VMEM) for i in range(len(args))
    ]
    shapes = [jax.ShapeDtypeStruct(s, d) for s, d in outs]
    moved = sum(math.prod(s) * jnp.dtype(d).itemsize for s, d in outs)
    moved += sum(a.size * a.dtype.itemsize for a in args)
    return pl.pallas_call(
        body,
        out_shape=shapes,
        in_specs=specs,
        out_specs=[pl.BlockSpec(memory_space=pltpu.VMEM)] * len(outs),
        compiler_params=pltpu.CompilerParams(vmem_limit_bytes=limit * 2**20),
        cost_estimate=pl.CostEstimate(flops=int(flops), bytes_accessed=int(moved), transcendentals=0),
        name=name,
    )(*args)


def centered(hidden):
    center = hidden - jnp.mean(hidden, axis=-1, keepdims=True)
    spread = jnp.mean(center * center, axis=-1, keepdims=True)
    inverse = lax.rsqrt(spread + EPS)
    return center * inverse, inverse


def norm_pull(grad, unit, inverse, gain):
    scaled = grad * gain
    mean = jnp.mean(scaled, axis=-1, keepdims=True)
    along = jnp.mean(scaled * unit, axis=-1, keepdims=True)
    return inverse * (scaled - mean - unit * along)


def col_sum(values):
    return jnp.sum(values, axis=0, keepdims=True)


def both_halves(seq, own, came):
    low = jnp.where(seq == 0, own, came)
    high = jnp.where(seq == 0, came, own)
    return jnp.concatenate([low, high], axis=1)


def front_kernel(place, runs, came, vecs, pos, w_patch, w_qkv,
                 hidden0, normed1, qkv, shifted_t, attended, lse):
    seq = place[0]
    items = came.shape[0]
    feat = w_patch.shape[0]
    length = pos.shape[0]
    width = pos.shape[1]
    for i in range(items):
        rows = slice(i * length, (i + 1) * length)
        own = runs[seq * items + i].astype(f32)
        whole = both_halves(seq, own, came[i, :feat])
        lane = lax.broadcasted_iota(jnp.int32, whole.shape, 1)
        moved = jnp.where(lane == 0, 0.0, pltpu.roll(whole, 1, 1)).astype(bf16)
        shifted_t[:, rows] = moved
        base = vecs[VEC["bp"] : VEC["bp"] + 1] + vecs[VEC["cls"] + i : VEC["cls"] + i + 1]
        h0 = dot(moved, w_patch[...], 0, 0) + base + pos[...].astype(f32)
        hidden0[rows, :] = h0
        unit, _ = centered(h0)
        normed1[rows, :] = (
            unit * vecs[VEC["n1g"] : VEC["n1g"] + 1] + vecs[VEC["n1s"] : VEC["n1s"] + 1]
        ).astype(bf16)
    for j in range(3):
        cols = slice(j * width, (j + 1) * width)
        qkv[:, cols] = dot(normed1[...], w_qkv[:, cols]).astype(bf16)
    pairs = HEADS // 2
    key_at = lax.broadcasted_iota(jnp.int32, (length, length), 0)
    query_at = lax.broadcasted_iota(jnp.int32, (length, length), 1)
    allowed = key_at <= query_at

    def step(p, carry):
        for i in range(items):
            rows = slice(i * length, (i + 1) * length)
            col = pl.multiple_of(p * 128, 128)
            q = qkv[rows, pl.ds(col, 128)]
            k = qkv[rows, pl.ds(pl.multiple_of(width + p * 128, 128), 128)]
            v = qkv[rows, pl.ds(pl.multiple_of(2 * width + p * 128, 128), 128)]
            first = lax.broadcasted_iota(jnp.int32, q.shape, 1) < 64
            v_t = v.T
            outs = []
            for h in range(2):
                mine = first if h == 0 else ~first
                qh = jnp.where(mine, q * 0.125, jnp.zeros_like(q))
                s = jnp.where(allowed, dot(k, qh, 1, 1), -1e30)
                top = jnp.max(s, axis=0, keepdims=True)
                e = jnp.exp(s - top)
                total = jnp.sum(e, axis=0, keepdims=True)
                lse[i, pl.ds(p * 2 + h, 1), :] = top + jnp.log(total)
                probs = (e * (1.0 / total)).astype(bf16)
                outs.append(dot(v_t[h * 64 : (h + 1) * 64], probs))
            attended[rows, pl.ds(col, 128)] = jnp.concatenate(outs, axis=0).T.astype(bf16)
        return carry

    lax.fori_loop(0, pairs, step, 0)


def middle_kernel(place, det, hidden0, attended, w_out, vecs, w_fc1, w_fc2, w_head_t, b_head,
                  runs, cot_runs, valid_runs, came,
                  hidden1, normed2, act, slope, d_hidden2, part_in, lat_keep, lat_send,
                  short, grad_head_t, facts):
    seq = place[0]
    items = came.shape[0]
    feat = runs.shape[1]
    width = w_out.shape[0]
    span = came.shape[2]
    length = 2 * span

    def vec(name, k=0):
        return vecs[VEC[name] + k : VEC[name] + k + 1]

    hidden1[...] = hidden0[...] + dot(attended[...], w_out[...])
    for i in range(items):
        rows = slice(i * length, (i + 1) * length)
        unit, _ = centered(hidden1[rows, :])
        normed2[rows, :] = (unit * vec("n2g") + vec("n2s")).astype(bf16)
    total = None
    for j in range(w_fc1.shape[1] // width):
        cols = slice(j * width, (j + 1) * width)
        up = dot(normed2[...], w_fc1[:, cols]) + vec("b1", j)
        square = up * up
        half = 0.5 * jnp.tanh(up * (GELU_A + GELU_A * GELU_B * square)) + 0.5
        value = up * half
        act[:, cols] = value.astype(bf16)
        slope[:, cols] = (
            half + 2.0 * value * (1.0 - half) * (GELU_A + 3.0 * GELU_A * GELU_B * square)
        ).astype(bf16)
        part = dot(act[:, cols], w_fc2[cols, :])
        total = part if total is None else total + part
    hidden2 = hidden1[...] + total + vec("b2")
    unit, inverse_dev = centered(hidden2)
    normed3 = (unit * vec("fg") + vec("fs")).astype(bf16)
    head = dot(w_head_t[...], normed3, 1, 1) + b_head[...]
    short[...] = jnp.zeros(short.shape, f32)
    d_heads = []
    sums = [jnp.zeros((1, 1), f32), jnp.zeros((1, 1), f32), jnp.full((1, 1), -1e30, f32)]
    for i in range(items):
        cols = slice(i * length, (i + 1) * length)
        source = seq * items + i
        x = both_halves(seq, runs[source].astype(f32), came[i, :feat])
        cot = both_halves(seq, cot_runs[source], came[i, feat : 2 * feat])
        valid = both_halves(
            seq, valid_runs[source].astype(f32), came[i, 2 * feat : 2 * feat + 1]
        )
        shift_part = head[:feat, cols]
        log_scale = head[feat:, cols]
        inverse = jnp.exp(-log_scale)
        moved = (x - shift_part) * inverse
        latent = valid * moved + (1.0 - valid) * x
        d_moved = valid * cot
        d_heads.append(
            jnp.concatenate(
                [-d_moved * inverse, -d_moved * moved - valid * det[source]], axis=0
            ).astype(bf16)
        )
        part_in[:, cols] = cot * (1.0 - valid) + d_moved * inverse
        counted = valid * log_scale
        item_sum = jnp.sum(jnp.sum(counted, axis=1, keepdims=True), axis=0, keepdims=True)
        sums[0] = sums[0] + item_sum
        sums[1] = sums[1] + jnp.sum(valid, axis=1, keepdims=True) * feat
        tops = jnp.where(valid > 0, log_scale, -1e30)
        tops = jnp.max(jnp.max(tops, axis=1, keepdims=True), axis=0, keepdims=True)
        sums[2] = jnp.maximum(sums[2], tops)
        low, high = latent[:, :span], latent[:, span:]
        logdet = jnp.broadcast_to(-item_sum, (8, span))
        lat_keep[i, :feat] = jnp.where(seq == 0, low, high)
        lat_send[i, :feat] = jnp.where(seq == 0, high, low)
        lat_keep[i, feat:] = logdet
        lat_send[i, feat:] = logdet
    lane = lax.broadcasted_iota(jnp.int32, facts.shape, 1)
    row = jnp.zeros(facts.shape, f32)
    for k, value in enumerate(sums):
        for j in range(3):
            piece = value.astype(bf16).astype(f32)
            value = value - piece
            row = jnp.where(lane == 3 * k + j, piece, row)
    for i in range(items):
        slot = place[8 + i]
        row = jnp.where(lane == 9 + i, (slot // 32).astype(f32), row)
        row = jnp.where(lane == 9 + items + i, (slot % 32).astype(f32), row)
    facts[...] = row
    d_head = jnp.concatenate(d_heads, axis=1)
    grad_head_t[...] = dot(d_head, normed3)
    short[ROW["bh"] : ROW["bh"] + 1, : 2 * feat] = dot(
        jnp.ones((8, d_head.shape[1]), bf16), d_head, 1, 1
    )[:1]
    d_normed3 = dot(d_head, w_head_t[...], 0, 0)
    short[ROW["fg"] : ROW["fg"] + 1, :] = col_sum(d_normed3 * unit)
    short[ROW["fs"] : ROW["fs"] + 1, :] = col_sum(d_normed3)
    pulled = norm_pull(d_normed3, unit, inverse_dev, vec("fg"))
    d_hidden2[...] = pulled
    short[ROW["b2"] : ROW["b2"] + 1, :] = col_sum(pulled.astype(bf16).astype(f32))


def split_by(bit, block, keep, send, half):
    low, high = block[:half], block[half:]
    keep[...] = jnp.where(bit == 0, low, high).astype(keep.dtype)
    send[...] = jnp.where(bit == 0, high, low).astype(send.dtype)


def fc2_kernel(place, act, d_hidden2, keep, send):
    group = keep.shape[1]
    d_mlp = d_hidden2[...].astype(bf16)
    step = 384
    per = step // (2 * group)
    for j in range(act.shape[1] // step):
        block = dot(act[:, j * step : (j + 1) * step], d_mlp, 0, 0)
        for k in range(per):
            n = j * per + k
            split_by(place[1], block[2 * group * k : 2 * group * (k + 1)], keep.at[n], send.at[n], group)


def back_kernel(place, d_hidden2, w_fc2, slope, normed2, w_fc1, hidden1, vecs, attended, w_out,
                short_in, grad_head_t,
                keep, send, d_hidden1, short, out_keep, out_send, d_attended):
    group = keep.shape[1]
    width = w_out.shape[0]
    step = 384
    per = step // (2 * group)
    d_mlp = d_hidden2[...].astype(bf16)
    short[...] = short_in[...]
    gain = vecs[VEC["n2g"] : VEC["n2g"] + 1]
    total = None
    for j in range(w_fc1.shape[1] // width):
        cols = slice(j * width, (j + 1) * width)
        d_up = (dot(d_mlp, w_fc2[cols, :], 1, 1) * slope[:, cols].astype(f32)).astype(bf16)
        short[ROW["b1"] + j : ROW["b1"] + j + 1, :] = col_sum(d_up.astype(f32))
        for m in range(width // step):
            block = dot(d_up[:, m * step : (m + 1) * step], normed2[...], 0, 0)
            for k in range(per):
                n = (j * (width // step) + m) * per + k
                split_by(place[1], block[2 * group * k : 2 * group * (k + 1)], keep.at[n], send.at[n], group)
        part = dot(d_up, w_fc1[:, cols], 1, 1)
        total = part if total is None else total + part
    unit, inverse_dev = centered(hidden1[...])
    short[ROW["n2g"] : ROW["n2g"] + 1, :] = col_sum(total * unit)
    short[ROW["n2s"] : ROW["n2s"] + 1, :] = col_sum(total)
    h1 = d_hidden2[...] + norm_pull(total, unit, inverse_dev, gain)
    d_hidden1[...] = h1
    d_out = h1.astype(bf16)
    grad_out = dot(attended[...], d_out, 0, 0)
    half = out_keep.shape[0]
    rest = 2 * half - grad_out.shape[0] - grad_head_t.shape[0]
    block = jnp.concatenate([grad_out, grad_head_t[...], jnp.zeros((rest, width), f32)], axis=0)
    split_by(place[1], block, out_keep, out_send, half)
    d_attended[...] = dot(d_out, w_out[...], 1, 1).astype(bf16)


def attention_back_kernel(qkv, lse, d_attended, d_qkv):
    rows_all, width = d_attended.shape
    items = lse.shape[0]
    length = rows_all // items
    key_at = lax.broadcasted_iota(jnp.int32, (length, length), 0)
    query_at = lax.broadcasted_iota(jnp.int32, (length, length), 1)
    allowed = key_at <= query_at

    def step(p, carry):
        for i in range(items):
            rows = slice(i * length, (i + 1) * length)
            at = [pl.ds(pl.multiple_of(j * width + p * 128, 128), 128) for j in range(3)]
            q, k, v = (qkv[rows, at[j]] for j in range(3))
            q = q * 0.125
            d_o = d_attended[rows, at[0]]
            first = lax.broadcasted_iota(jnp.int32, q.shape, 1) < 64
            none = jnp.zeros_like(q)
            total = [None, None, None]
            for h in range(2):
                mine = first if h == 0 else ~first
                qh = jnp.where(mine, q, none)
                kh = jnp.where(mine, k * 0.125, none)
                dh = jnp.where(mine, d_o, none)
                s = jnp.where(allowed, dot(k, qh, 1, 1), -1e30)
                probs = jnp.exp(s - lse[i, pl.ds(p * 2 + h, 1), :])
                d_probs = dot(v, dh, 1, 1)
                delta = jnp.sum(probs * d_probs, axis=0, keepdims=True)
                d_s = (probs * (d_probs - delta)).astype(bf16)
                parts = [dot(d_s, kh, 0, 0), dot(d_s, qh), dot(probs.astype(bf16), dh)]
                total = [b if a is None else a + b for a, b in zip(total, parts)]
            for j in range(3):
                d_qkv[rows, at[j]] = total[j].astype(bf16)
        return carry

    lax.fori_loop(0, HEADS // 2, step, 0)


def qkv_kernel(place, normed1, d_qkv, keep, send):
    width = normed1.shape[1]
    half = keep.shape[0]
    core = place[1]
    step = 384
    for j in range(3):
        for m in range(width // step):
            block = dot(normed1[:, m * step : (m + 1) * step], d_qkv[:, j * width : (j + 1) * width], 0, 0)
            at = j * width + m * step
            inside = at % half

            @pl.when(core == at // half)
            def _():
                keep[inside : inside + step, :] = block

            @pl.when(core != at // half)
            def _():
                send[inside : inside + step, :] = block.astype(bf16)


def rest_kernel(place, d_qkv, w_qkv, hidden0, d_hidden1, vecs, shifted_t, w_patch, part_in, short_in, facts,
                keep, send, short, in_keep, in_send, extra):
    seq = place[0]
    width = hidden0.shape[1]
    items, feat, span = in_keep.shape
    length = 2 * span
    d_normed1 = dot(d_qkv[...], w_qkv[...], 1, 1)
    unit, inverse_dev = centered(hidden0[...])
    short[...] = short_in[...]
    short[ROW["n1g"] : ROW["n1g"] + 1, :] = col_sum(d_normed1 * unit)
    short[ROW["n1s"] : ROW["n1s"] + 1, :] = col_sum(d_normed1)
    d0 = d_hidden1[...] + norm_pull(d_normed1, unit, inverse_dev, vecs[VEC["n1g"] : VEC["n1g"] + 1])
    d_low = d0.astype(bf16)
    extra[...] = jnp.zeros(extra.shape, bf16)
    d_pos, whole = None, None
    for i in range(items):
        mine = d0[i * length : (i + 1) * length]
        d_pos = mine if d_pos is None else d_pos + mine
        item = col_sum(mine)
        whole = item if whole is None else whole + item
        extra[i : i + 1, :] = item.astype(bf16)
    extra[items : items + 1, :] = facts[...].astype(bf16)
    short[ROW["bp"] : ROW["bp"] + 1, :] = whole
    d_patch = dot(shifted_t[...], d_low)
    half = keep.shape[0]
    rest = 2 * half - d_pos.shape[0] - d_patch.shape[0]
    block = jnp.concatenate([d_pos, d_patch, jnp.zeros((rest, width), f32)], axis=0)
    split_by(place[1], block, keep, send.at[:half], half)
    short[...] = put_short(send, half, short[...])
    d_shift = dot(w_patch[...], d_low, 1, 1)
    for i in range(items):
        cols = slice(i * length, (i + 1) * length)
        moved = d_shift[:, cols]
        lane = lax.broadcasted_iota(jnp.int32, moved.shape, 1)
        back = jnp.where(lane == length - 1, 0.0, pltpu.roll(moved, length - 1, 1))
        grad = part_in[:, cols] + back
        in_keep[i] = jnp.where(seq == 0, grad[:, :span], grad[:, span:])
        in_send[i] = jnp.where(seq == 0, grad[:, span:], grad[:, :span])


def put_short(send, at, short):
    n = short.shape[0]
    high = short.astype(bf16)
    low = (short - high.astype(f32)).astype(bf16)
    send[at : at + n, :] = high
    send[at + n : at + 2 * n, :] = low
    return high.astype(f32) + low.astype(f32)


def take_short(came, at, n):
    return came[at : at + n, :].astype(f32) + came[at + n : at + 2 * n, :].astype(f32)


def add_split_kernel(bits, place, *refs):
    n = len(bits)
    for t, bit in enumerate(bits):
        keep, came, kept, send = refs[t], refs[n + t], refs[2 * n + t], refs[3 * n + t]
        mine = place[1 + bit - 1] if bit else place[0]
        for a in range(keep.shape[0]):
            kept[a] = keep[a, mine] + came[a, mine].astype(f32)
            send[a] = (keep[a, 1 - mine] + came[a, 1 - mine].astype(f32)).astype(bf16)


def add_split(place, bits, keeps, cames, name):
    outs = []
    for keep in keeps:
        a, _, b, w = keep.shape
        outs.append(((a, b, w), f32))
    for keep in keeps:
        a, _, b, w = keep.shape
        outs.append(((a, b, w), bf16))
    got = call(
        partial(add_split_kernel, bits), outs, [place] + list(keeps) + list(cames), name, 1e6, 4, smem=(0,)
    )
    return got[: len(keeps)], got[len(keeps) :]


def add_kernel(keep, came, out):
    out[...] = keep[...] + came[...].astype(f32)


def bulk0_kernel(place, qk, qc, ek, ec, lk, lc, short_in, keep_a, keep_b, send_a, send_b, short):
    x, y = place[0], place[2]
    na, nb = keep_a.shape[0], keep_b.shape[0]
    nq, ne, nl = qk.shape[0], ek.shape[0], lk.shape[0]
    ns = short.shape[0]
    total = short_in[...] + take_short(lc, nl, ns)
    mine, away = pl.ds(pl.multiple_of(x * na, na), na), pl.ds(pl.multiple_of((1 - x) * na, na), na)
    keep_a[...] = qk[mine, :] + qc[mine, :].astype(f32)
    send_a[...] = (qk[away, :] + qc[away, :].astype(f32)).astype(bf16)
    low = 2 * na
    parts = [
        qk[low:nq, :] + qc[low:nq, :].astype(f32),
        ek[...] + ec[...].astype(f32),
        lk[...] + lc[:nl, :].astype(f32),
    ]
    block = jnp.concatenate(parts, axis=0)
    split_by(y, block, keep_b, send_b.at[:nb], nb)
    short[...] = put_short(send_b, nb, total)


def bulk1_kernel(place, ka, ca, kb, cb, short_in, keep_a, keep_b, send_a, send_b, short):
    x, y = place[0], place[2]
    na, nb = keep_a.shape[0], keep_b.shape[0]
    ns = short.shape[0]
    total = short_in[...] + take_short(cb, 2 * nb, ns)
    for bit, n, k, c, keep, send in ((y, na, ka, ca, keep_a, send_a), (x, nb, kb, cb, keep_b, send_b)):
        mine, away = pl.ds(pl.multiple_of(bit * n, n), n), pl.ds(pl.multiple_of((1 - bit) * n, n), n)
        keep[...] = k[mine, :] + c[mine, :].astype(f32)
        send[:n, :] = (k[away, :] + c[away, :].astype(f32)).astype(bf16)
    short[...] = put_short(send_b, nb, total)


def bulk2_kernel(place, ka, ca, kb, cb, short_in, keep, send1, send2, send3, short):
    z = place[3] + 2 * place[4]
    na, nb = ka.shape[0] // 4, kb.shape[0] // 4
    ns = short.shape[0]
    total = short_in[...] + take_short(cb, 4 * nb, ns)
    for m, out in enumerate((keep, send1, send2, send3)):
        at = z ^ m
        ra = pl.ds(pl.multiple_of(at * na, na), na)
        rb = pl.ds(pl.multiple_of(at * nb, nb), nb)
        out[:na, :] = (ka[ra, :] + ca[ra, :].astype(f32)).astype(out.dtype)
        out[na : na + nb, :] = (kb[rb, :] + cb[rb, :].astype(f32)).astype(out.dtype)
        if m:
            short[...] = put_short(out, na + nb, total)


def bulk3_kernel(keep, c1, c2, c3, short_in, extra, piece, short):
    n = keep.shape[0]
    ns = short.shape[0]
    total = keep[...]
    for c in (c1, c2, c3):
        total = total + c[:n, :].astype(f32)
    piece[:n, :] = total.astype(bf16)
    piece[n:, :] = extra[...]
    short[...] = (short_in[...] + take_short(c1, n, ns)) + (take_short(c2, n, ns) + take_short(c3, n, ns))


def join0_kernel(place, own, c1, c2, c3, part_a, part_b):
    z = place[3] + 2 * place[4]
    na, nb = part_a.shape[0] // 4, part_b.shape[0] // 4
    for m, c in enumerate((own, c1, c2, c3)):
        at = z ^ m
        part_a[pl.ds(pl.multiple_of(at * na, na), na), :] = c[:na, :]
        part_b[pl.ds(pl.multiple_of(at * nb, nb), nb), :] = c[na:, :]


def join1_kernel(place, own_a, came_a, own_b, came_b, part_a, part_b):
    x, y = place[0], place[2]
    n = own_a.shape[0]
    for bit, own, came, part in ((y, own_a, came_a, part_a), (x, own_b, came_b, part_b)):
        part[pl.ds(pl.multiple_of(bit * n, n), n), :] = own[...]
        part[pl.ds(pl.multiple_of((1 - bit) * n, n), n), :] = came[...]


def last_kernel(geo, place, *refs):
    quarters = refs[:8]
    g_qkv, g_out, g_pos, g_head, g_patch, extras, full = refs[8:]
    x, core, y = place[0], place[1], place[2]
    nb, ne = geo["nb"], geo["extra"]
    n = quarters[0].shape[0]
    for c in range(2):
        which = core if c == 0 else 1 - core
        for t, (bit, other) in enumerate(((x, 1 - x), (y, 1 - y))):
            own, came = quarters[4 * c + 2 * t], quarters[4 * c + 2 * t + 1]
            full[which, t, bit] = own[...]
            full[which, t, other] = came[...]
    width = g_out.shape[0]
    na = 2 * n

    def rows_b(c):
        out = []
        for k in range(2):
            for j in range(8):
                block = full[c, 1, k, j * (nb + ne) : (j + 1) * (nb + ne), :]
                out.append(block[:nb])
                extras[c, k * 8 + j] = block[nb:]
        return jnp.concatenate(out, axis=0)

    flat_b = [rows_b(c) for c in range(2)]
    half_q = geo["half_q"]
    left = half_q - na
    for c in range(2):
        for at in range(0, half_q, 128):
            q = c * half_q + at
            third, row = q // width, q % width
            if at < na:
                block = full[c, 0, at // n, at % n : at % n + 128, :]
            else:
                block = flat_b[c][at - na : at - na + 128]
            g_qkv[row : row + 128, third * width : (third + 1) * width] = block.astype(f32)
    half_e, half_l = geo["half_e"], geo["half_l"]
    early = [flat_b[c][left : left + half_e].astype(f32) for c in range(2)]
    later = [flat_b[c][left + half_e : left + half_e + half_l].astype(f32) for c in range(2)]
    g_out[:half_e, :] = early[0]
    g_out[half_e:, :] = early[1][: width - half_e]
    g_head[...] = early[1][width - half_e : width - half_e + g_head.shape[0]]
    length, feat = g_pos.shape[0], g_patch.shape[0]
    g_pos[:half_l, :] = later[0]
    g_pos[half_l:, :] = later[1][: length - half_l]
    g_patch[...] = later[1][length - half_l : length - half_l + feat]


class Cube:
    def __init__(self):
        self.size = lax.axis_size("dp") * lax.axis_size("seq")
        self.nbits = self.size.bit_length() - 1
        self.me = lax.axis_index("dp") * lax.axis_size("seq") + lax.axis_index("seq")
        self.bit = [(self.me >> k) & 1 for k in range(self.nbits)]

    def send(self, block, mask):
        return lax.ppermute(block, AXES, [(i, i ^ mask) for i in range(self.size)])

    def start(self, full, bits):
        rows = full.shape[0] >> len(bits)
        return full.reshape((2,) * len(bits) + (rows, full.shape[1])), list(bits)

    def scatter(self, block, left):
        for bit in list(left):
            axis = left.index(bit)
            mine = lax.dynamic_index_in_dim(block, self.bit[bit], axis, keepdims=False)
            away = lax.dynamic_index_in_dim(block, 1 - self.bit[bit], axis, keepdims=False)
            block = mine + self.send(away.astype(bf16), 1 << bit).astype(f32)
            left = [b for b in left if b != bit]
        return block

    def add_up(self, block, bits):
        for k in bits:
            block = block + self.send(block, 1 << k)
        return block

    def gather(self, block, bits):
        for k in reversed(bits):
            came = self.send(block, 1 << k)
            block = jnp.where(self.bit[k] == 0, jnp.stack([block, came]), jnp.stack([came, block]))
        return block


def tie(value, *others):
    return lax.optimization_barrier((value,) + others)[0]


def local(
    patches, labels, valid_mask, class_slot, w_patch, b_patch, pos_embed, class_embed,
    norm1_gain, norm1_shift, w_qkv, w_out, norm2_gain, norm2_shift, w_fc1, b_fc1, w_fc2, b_fc2,
    final_gain, final_shift, w_head, b_head, cot_latent, cot_logdet,
):
    cube = Cube()
    seq_n = lax.axis_size("seq")
    assert seq_n == 2
    seq = lax.axis_index("seq")
    held, span, feat = patches.shape
    items = held // seq_n
    length = span * seq_n
    width = w_out.shape[0]
    ff = w_fc1.shape[1]
    rows = items * length
    classes = class_embed.shape[0]
    chunk = ff // cube.size
    group = 2 * chunk
    fast = cube.size == 32

    runs = patches.transpose(0, 2, 1)
    cot_runs = cot_latent.transpose(0, 2, 1)
    first = seq * items
    away = (1 - seq) * items
    packed = jnp.concatenate(
        [
            lax.dynamic_slice_in_dim(runs, away, items, 0).astype(f32),
            lax.dynamic_slice_in_dim(cot_runs, away, items, 0),
            jnp.broadcast_to(
                lax.dynamic_slice_in_dim(valid_mask, away, items, 0).astype(f32)[:, None],
                (items, 8, span),
            ),
        ],
        axis=1,
    )
    came = cube.send(packed, 1)
    my_labels = [lax.dynamic_index_in_dim(labels, first + i, 0, keepdims=False) for i in range(items)]
    slots = [lax.dynamic_index_in_dim(class_slot, at, 0, keepdims=False) for at in my_labels]
    bits = (cube.bit + [0] * 8)[:8]
    place = jnp.stack([jnp.asarray(v, jnp.int32) for v in bits + slots])
    vectors = [b_patch, norm1_gain, norm1_shift, norm2_gain, norm2_shift, b_fc2, final_gain, final_shift]
    vecs = jnp.concatenate(
        [v[None] for v in vectors]
        + [b_fc1.reshape(-1, width)]
        + [lax.dynamic_slice_in_dim(class_embed, at, 1, 0) for at in my_labels]
    )
    vecs = jnp.pad(vecs.astype(f32), ((0, -vecs.shape[0] % 8), (0, 0)))
    w_head_t = w_head.T
    b_head_col = b_head.astype(f32)[:, None]
    valid_runs = valid_mask[:, None, :]

    big = 2.0 * rows * width * ff
    hidden0, normed1, qkv, shifted_t, attended, lse = call(
        front_kernel,
        [((rows, width), f32), ((rows, width), bf16), ((rows, 3 * width), bf16), ((feat, rows), bf16),
         ((rows, width), bf16), ((items, HEADS, length), f32)],
        [place, runs, came, vecs, pos_embed, w_patch, w_qkv],
        "front", big, 16, smem=(0,),
    )
    n_short = 16
    (hidden1, normed2, act, slope, d_hidden2, part_in, lat_keep, lat_send, short, grad_head_t, facts) = call(
        middle_kernel,
        [((rows, width), f32), ((rows, width), bf16), ((rows, ff), bf16), ((rows, ff), bf16),
         ((rows, width), f32), ((feat, rows), f32), ((items, feat + 8, span), f32),
         ((items, feat + 8, span), f32), ((n_short, width), f32), ((2 * feat, width), f32),
         ((1, width), f32)],
        [place, cot_logdet, hidden0, attended, w_out, vecs, w_fc1, w_fc2, w_head_t, b_head_col,
         runs, cot_runs, valid_runs, came],
        "middle", 2.5 * big, 24, smem=(0, 1),
    )
    groups = ff // (2 * group)
    keep2, send2 = call(
        fc2_kernel, [((groups, group, width), f32), ((groups, group, width), bf16)],
        [place, act, d_hidden2], "fc2", big, 12, smem=(0,),
    )
    came2 = cube.send(send2, 2)
    half_e, half_l, half_q = 448, 192, 3 * width // 2
    keep1, send1, d_hidden1, short, ekeep, esend, d_attended = call(
        back_kernel,
        [((groups, group, width), f32), ((groups, group, width), bf16), ((rows, width), f32),
         ((n_short, width), f32), ((half_e, width), f32), ((half_e, width), bf16), ((rows, width), bf16)],
        [place, d_hidden2, w_fc2, slope, normed2, w_fc1, hidden1, vecs, attended, w_out, short, grad_head_t],
        "back", 3.5 * big, 24, smem=(0,),
    )
    came1 = cube.send(send1, 2)
    ecame = cube.send(esend, 2)
    if fast:
        (k2,), (s2,) = add_split(
            place, (0,), [keep2.reshape(8, 2, chunk, width)], [came2.reshape(8, 2, chunk, width)], "fc2_core"
        )
        c2 = cube.send(s2, 1)
        d_attended = tie(d_attended, s2)
    (d_qkv,) = call(
        attention_back_kernel, [((rows, 3 * width), bf16)], [qkv, lse, d_attended],
        "attention_back", big, 16,
    )
    qkeep, qsend = call(
        qkv_kernel, [((half_q, width), f32), ((half_q, width), bf16)], [place, normed1, d_qkv],
        "qkv_grad", 0.75 * big, 12, smem=(0,),
    )
    qcame = cube.send(qsend, 2)
    if fast:
        (k1,), (s1,) = add_split(
            place, (2,), [keep1.reshape(4, 2, group, width)], [came1.reshape(4, 2, group, width)], "fc1_core"
        )
        c1 = cube.send(s1, 4)
    lkeep, lsend, short, in_keep, in_send, extra = call(
        rest_kernel,
        [((half_l, width), f32), ((half_l + 2 * n_short, width), bf16), ((n_short, width), f32),
         ((items, feat, span), f32), ((items, feat, span), f32), ((16, width), bf16)],
        [place, d_qkv, w_qkv, hidden0, d_hidden1, vecs, shifted_t, w_patch, part_in, short, facts],
        "rest", 0.9 * big, 16, smem=(0,),
    )
    lcame = cube.send(lsend, 2)

    back_send = jnp.concatenate([lat_send, in_send], axis=1)
    back_keep = jnp.concatenate([lat_keep, in_keep], axis=1)
    back_came = cube.send(back_send, 1)

    if fast:
        na, nb = 512, 384
        ns2 = 2 * n_short
        ka, kb, sa, sb, short = call(
            bulk0_kernel,
            [((na, width), f32), ((nb, width), f32), ((na, width), bf16), ((nb + ns2, width), bf16),
             ((n_short, width), f32)],
            [place, qkeep, qcame, ekeep, ecame, lkeep, lcame, short], "bulk0", 1e6, 8, smem=(0,),
        )
        ca, cb = cube.send(sa, 1), cube.send(sb, 4)
        na, nb = 256, 192
        ka, kb, sa, sb, short = call(
            bulk1_kernel,
            [((na, width), f32), ((nb, width), f32), ((na, width), bf16), ((nb + ns2, width), bf16),
             ((n_short, width), f32)],
            [place, ka, ca, kb, cb, short], "bulk1", 1e6, 6, smem=(0,),
        )
        ca, cb = cube.send(sa, 4), cube.send(sb, 1)
        na, nb = 64, 48
        n = na + nb
        keep, z1, z2, z3, short = call(
            bulk2_kernel,
            [((n, width), f32)] + [((n + ns2, width), bf16)] * 3 + [((n_short, width), f32)],
            [place, ka, ca, kb, cb, short], "bulk2", 1e6, 6, smem=(0,),
        )
        z1, z2, z3 = cube.send(z1, 8), cube.send(z2, 16), cube.send(z3, 24)
        (k2, k1), (s2, s1) = add_split(
            place, (2, 0),
            [k2.reshape(4, 2, chunk, width), k1.reshape(4, 2, chunk, width)],
            [c2.reshape(4, 2, chunk, width), c1.reshape(4, 2, chunk, width)], "fc_second",
        )
        c2, c1 = cube.send(s2, 4), cube.send(s1, 1)
        piece, short = call(
            bulk3_kernel, [((n + 16, width), bf16), ((n_short, width), f32)],
            [keep, z1, z2, z3, short, extra], "bulk3", 1e6, 4,
        )
        g1, g2, g3 = cube.send(piece, 8), cube.send(piece, 16), cube.send(piece, 24)
        (kf,), (sf,) = add_split_pair(place, 3, k2, k1, c2, c1, "fc_third")
        cf = cube.send(sf, 8)
        part_a, part_b = call(
            join0_kernel, [((4 * na, width), bf16), ((4 * (nb + 16), width), bf16)],
            [place, piece, g1, g2, g3], "join0", 1e6, 4, smem=(0,),
        )
        ca, cb = cube.send(part_a, 4), cube.send(part_b, 1)
        part_a, part_b = call(
            join1_kernel, [((8 * na, width), bf16), ((8 * (nb + 16), width), bf16)],
            [place, part_a, ca, part_b, cb], "join1", 1e6, 4, smem=(0,),
        )
        (kf,), (sf,) = add_split(
            place, (4,), [kf.reshape(1, 2, 2 * chunk, width)], [cf.reshape(1, 2, 2 * chunk, width)], "fc_fourth"
        )
        cf = cube.send(sf, 16)
        ca, cb = cube.send(part_a, 1), cube.send(part_b, 4)
        quarters = [part_a, ca, part_b, cb]
        quarters = quarters + [cube.send(q, 2) for q in quarters]
        geo = dict(nb=nb, extra=16, half_q=half_q, half_e=half_e, half_l=half_l)
        g_qkv, g_out, g_pos, g_head_t, g_patch, extras = last_call(
            geo, place, quarters, width, length, feat
        )
        (own,) = call(add_kernel, [((1, 2 * chunk, width), f32)], [kf, cf], "fc_last", 1e6, 4)
        own_fc2, own_fc1 = own[0, :chunk], own[0, chunk:]
        extras = extras.reshape(2, 2, 2, 4, 16, width)[:, :, :, :, : items + 1]
        extras = extras.transpose(3, 1, 0, 2, 4, 5).reshape(cube.size, items + 1, width).astype(f32)
    else:
        rest = [0] + list(range(2, cube.nbits))
        upper = list(range(cube.nbits - 1, 1, -1)) + [0]

        def owned(keep, came):
            total = (keep + came.astype(f32)).reshape(-1, width)
            return cube.scatter(*cube.start(total, upper))

        own_fc2, own_fc1 = owned(keep2, came2), owned(keep1, came1)
        full = jnp.concatenate(
            [qkeep + qcame.astype(f32), ekeep + ecame.astype(f32), lkeep + lcame[:half_l].astype(f32)]
        )
        n_full = full.shape[0]
        full = jnp.pad(full, ((0, -n_full % (cube.size * 8)), (0, 0)))
        own = cube.scatter(*cube.start(full, upper))
        n_own = own.shape[0]
        got = cube.gather(jnp.concatenate([own.astype(bf16), extra]), [1] + upper)
        halves = got[..., :n_own, :].reshape(2, -1, width)[:, :n_full].astype(f32)
        short = cube.add_up(short, [1] + rest)
        q = halves[:, :half_q].reshape(3, width, width)
        g_qkv = jnp.concatenate([q[0], q[1], q[2]], axis=1)
        e = halves[:, half_q : half_q + half_e].reshape(-1, width)
        g_out, g_head_t = e[:width], e[width : width + 2 * feat]
        later = halves[:, half_q + half_e :].reshape(-1, width)
        g_pos, g_patch = later[:length], later[length : length + feat]
        extras = got[..., n_own : n_own + items + 1, :]
        extras = jnp.moveaxis(extras, 0, cube.nbits - 2)
        extras = extras.reshape(cube.size, items + 1, width).astype(f32)

    sums = extras[:, :items].reshape(-1, width)
    facts = extras[:, items]
    scale_sum = jnp.sum(facts[:, 0] + facts[:, 1] + facts[:, 2])
    count = jnp.sum(facts[:, 3] + facts[:, 4] + facts[:, 5])
    top = jnp.max(facts[:, 6] + facts[:, 7] + facts[:, 8])
    all_slots = (facts[:, 9 : 9 + items] * 32 + facts[:, 9 + items : 9 + 2 * items]).reshape(-1)
    own_rows = classes // cube.size
    wanted = (cube.me * own_rows + jnp.arange(own_rows)).astype(f32)
    hot = (wanted[:, None] == all_slots[None, :]).astype(bf16)
    class_own = dot(hot, sums.astype(bf16))

    out = jnp.where(
        seq == 0, jnp.concatenate([back_keep, back_came]), jnp.concatenate([back_came, back_keep])
    )
    latent_out = out[:, :feat].transpose(0, 2, 1)
    logdet_out = out[:, feat, 0]
    grad_in_out = out[:, feat + 8 :].transpose(0, 2, 1)
    b1_all = short[ROW["b1"] : ROW["b1"] + ff // width].reshape(-1)
    b1_own = lax.dynamic_slice_in_dim(b1_all, cube.me * chunk, chunk, 0)
    vec = {name: short[at] for name, at in ROW.items()}
    return (
        latent_out, logdet_out, grad_in_out, g_patch, vec["bp"], g_pos, class_own,
        vec["n1g"], vec["n1s"], g_qkv, g_out, vec["n2g"], vec["n2s"], own_fc1.T, b1_own, own_fc2,
        vec["b2"], vec["fg"], vec["fs"], g_head_t.T, vec["bh"][: 2 * feat], scale_sum / count, top,
    )


def pair_kernel(bit, place, ka, kb, ca, cb, kept, send):
    mine = place[bit]
    n = ka.shape[2]
    for t, (k, c) in enumerate(((ka, ca), (kb, cb))):
        for a in range(k.shape[0]):
            kept[a, t * n : (t + 1) * n] = k[a, mine] + c[a, mine].astype(f32)
            send[a, t * n : (t + 1) * n] = (k[a, 1 - mine] + c[a, 1 - mine].astype(f32)).astype(bf16)


def add_split_pair(place, bit, ka, kb, ca, cb, name):
    n, w = ka.shape[1:]
    args = [v.reshape(2, 2, n, w) for v in (ka, kb, ca, cb)]
    kept, send = call(
        partial(pair_kernel, bit), [((2, 2 * n, w), f32), ((2, 2 * n, w), bf16)], [place] + args, name, 1e6, 4,
        smem=(0,),
    )
    return (kept,), (send,)


def last_call(geo, place, quarters, width, length, feat):
    n = quarters[0].shape[0]
    outs = [
        ((width, 3 * width), f32), ((width, width), f32), ((length, width), f32),
        ((2 * feat, width), f32), ((feat, width), f32), ((2, 16, geo["extra"], width), bf16),
    ]
    return pl.pallas_call(
        partial(last_kernel, geo),
        out_shape=[jax.ShapeDtypeStruct(s, d) for s, d in outs],
        in_specs=[pl.BlockSpec(memory_space=pltpu.SMEM)] + [pl.BlockSpec(memory_space=pltpu.VMEM)] * 8,
        out_specs=[pl.BlockSpec(memory_space=pltpu.VMEM)] * len(outs),
        scratch_shapes=[pltpu.VMEM((2, 2, 2, n, width), bf16)],
        compiler_params=pltpu.CompilerParams(vmem_limit_bytes=24 * 2**20),
        cost_estimate=pl.CostEstimate(flops=10**6, bytes_accessed=20 * 10**6, transcendentals=0),
        name="last",
    )(place, *quarters)


def solution(mesh):
    run, item, whole = P("dp", "seq", None), P("dp"), P()
    placed = (run, item, P("dp", "seq")) + (whole,) * 19 + (run, item)
    owned = P(AXES)
    return jax.shard_map(
        local,
        mesh=mesh,
        in_specs=placed,
        out_specs=(run, item, run, whole, whole, whole, P(AXES, None), whole, whole, whole, whole,
                   whole, whole, P(None, AXES), owned, P(AXES, None)) + (whole,) * 7,
        check_vma=False,
    )
```

time: 439 us -> 261 us (0.59)
  other arithmetic: 82.1 us -> 3.88 us
  matrix products: 77.6 us -> 0.84 us
  Pallas kernels: 0 us -> 69.9 us
  local copies, waits for them, and re-layouts: 107 us -> 40.8 us
  waiting for transfers between devices: 119 us -> 95.4 us
  starting transfers between devices: 25.8 us -> 37.4 us
  between operations: 19.3 us -> 7.99 us
    pallas_call x0 -> x20, Pallas kernels: none -> 69.9 us  [the longest x19 63.4 us: call(): pl.pallas_call(body, out_shape=shapes, in_specs=specs, out_specs=[pl.Bloc...]
    dot_general x21 -> x1, matrix products: 63.3 us -> 0.84 us  [dot(): lax.dot_general(left, right, (((a,), (b,)), ((), ())), preferred_element_...]
    slice x15 -> x5, local copies, waits for them, and re-layouts: 31.4 us -> 1.87 us  [the longest x1 0.66 us: local(): vec = {name: short[at] for name, at in ROW.items()}]
    convert_element_type x22 -> x2, other arithmetic: 28.1 us -> 1.43 us  [the longest x1 0.74 us: local(): lax.dynamic_slice_in_dim(runs, away, items, 0).astype(f32)]
    ppermute x32 -> x31, waiting for transfers between devices: 119 us -> 95.4 us  [send(): return lax.ppermute(block, AXES, [(i, i ^ mask) for i in range(self.size)])]
    convert_element_type x20 -> x2, local copies, waits for them, and re-layouts: 24.1 us -> 0.12 us  [local(): extras.transpose(3, 1, 0, 2, 4, 5).reshape(cube.size, items + 1, width)]
    add x22 -> x0, other arithmetic: 20.1 us -> none  [the longest x15 18.2 us: scatter(): total = part if total is None else total + part]
    dot_general x6 -> x0, matrix products: 14.3 us -> none  [the longest x1 6.86 us: local(): jnp.einsum('bqhd,bkhd->bhqk', d_attended, values, preferred_element_type=...]
  transfers between devices with their start and end apart: 32 -> 31, of which waited for: 18 -> 12; matrix products, arithmetic and copies ran while one was open for 19% -> 7% of each run, Pallas kernels for 0% -> 14%
where the time goes in v2:
time: 261 us; the launch traced here: 256 us
  waiting for transfers between devices  95.4 us (37%)
  Pallas kernels  69.9 us (27%)
  local copies, waits for them, and re-layouts  40.8 us (16%)
  starting transfers between devices  37.4 us (14%)
  between operations  7.99 us (3%)
  other arithmetic  3.88 us (1%)
    ppermute x31, waiting for transfers between devices, send(): return lax.ppermute(block, AXES, [(i, i ^ mask) for i in range(self.size)])  95.4 us
    pallas_call x19, Pallas kernels, call(): pl.pallas_call(body, out_shape=shapes, in_specs=specs, out_specs=[pl.Bloc...  63.4 us
    ppermute x31, starting transfers between devices, send(): return lax.ppermute(block, AXES, [(i, i ^ mask) for i in range(self.size)])  37.4 us
    unnamed x72, local copies, waits for them, and re-layouts  23.8 us
    pallas_call x1, Pallas kernels, last_call(): pl.pallas_call(partial(last_kernel, geo), out_shape=[jax.ShapeDtypeStruct...  6.52 us
    broadcast_in_dim x8, local copies, waits for them, and re-layouts, local(): v[None]  5.48 us
  transfers between devices with their start and end apart: 31, of which 12 were waited for; matrix products, arithmetic and copies ran while one was open for 7% of the time, Pallas kernels for 14%

profile of v2, /device:TPU:0, one launch (start us, length us, event | category | flops | bytes accessed | tf_op | source)
XLA Modules:
  0.0 256.3 jit_solution(1082784828381675190)
XLA Ops:
  2.9 3.0 %collective-permute-start = (f32[2,104,128]{2,1,0:T(8,128)S(1)}, f32[2,104,128]{2,1,0:T(8,128)S(1)}, u32[]{:S(2)}, u32[]{:S(2)}) collective-permute-start(f32[2,104,128]{2,1,0:T(8,128)S(1)} %pad_maximum_fusion), channel_id=1, source_target_pairs={{0,1},{1,0},{2,3},{3,2},{4,5},{5,4},{6,7},{7,6},{8,9},{9,8},{10,11... | collective-permute-start | bytes 319496 | tf_op jit(solution)/shard_map/ppermute | solution.py:545
  5.9 1.3 fusion.9
  17.3 1.4 fusion.8
  20.2 1.4 stack.25.place
  21.7 2.0 copy-done
  26.4 12.4 %front.1 = (f32[512,768]{1,0:T(8,128)S(1)}, bf16[512,768]{1,0:T(8,128)(2,1)S(1)}, bf16[512,2304]{1,0:T(8,128)(2,1)S(1)}, bf16[48,512]{1,0:T(8,128)(2,1)S(1)}, bf...) custom-call(s32[10]{0:T(128)S(1)} %stack.25.place, bf16[4,48,128]{2,1,0:T(8,128)(2,1)S(1)} %bitcast.68, ...), custom_call_target="tpu_custom_call" | custom-call | flops 2415919104 | bytes 9789480 | tf_op jit(solution)/shard_map/front/pallas_call | solution.py:35
  38.9 1.4 copy-done.25
  41.2 2.6 %copy-done.18 = bf16[3072,768]{1,0:T(8,128)(2,1)S(1)} copy-done((bf16[3072,768]{1,0:T(8,128)(2,1)S(1)}, bf16[3072,768]{1,0:T(8,128)(2,1)}, u32[]{:S(2)}) %copy-start.18) | copy-done | bytes 4718616
  43.8 10.9 %middle.1 = (f32[512,768]{1,0:T(8,128)S(1)}, bf16[512,768]{1,0:T(8,128)(2,1)S(1)}, bf16[512,3072]{1,0:T(8,128)(2,1)S(1)}, bf16[512,3072]{1,0:T(8,128)(2,1)S(1)},...) custom-call(s32[10]{0:T(128)S(1)} %stack.25.place, ...), custom_call_target="tpu_custom_call" | custom-call | flops 6039797760 | bytes 24212920 | tf_op jit(solution)/shard_map/middle/pallas_call | solution.py:35
  54.7 1.7 copy-done.31
  56.4 3.2 %fc2.1 = (f32[8,192,768]{2,1,0:T(8,128)S(1)}, bf16[8,192,768]{2,1,0:T(8,128)(2,1)S(1)}) custom-call(s32[10]{0:T(128)S(1)} %stack.25.place, bf16[512,3072]{1,0:T(8,128)(2,1)S(1)} %get-tuple-element.109.act, f32[512,768]{1,0:T(8,128)S(1)} %get-tuple-element.102.d_hidden2), custom_call_target="tpu_custom_call" | custom-call | flops 2415919104 | bytes 11796520 | tf_op jit(solution)/shard_map/fc2/pallas_call | solution.py:35
  59.8 2.3 copy-done.17
  62.1 2.3 copy-done.19
  64.5 1.4 copy-done.28
  65.9 1.9 copy-done.32
  67.7 10.9 %back.1 = (f32[8,192,768]{2,1,0:T(8,128)S(1)}, bf16[8,192,768]{2,1,0:T(8,128)(2,1)S(1)}, f32[512,768]{1,0:T(8,128)S(1)}, f32[16,768]{1,0:T(8,128)S(1)}, f32[448,...) custom-call(s32[10]{0:T(128)S(1)} %stack.25.place, f32[512,768]{1,0:T(8,128)S(1)} %copy-done.28, ...), custom_call_target="tpu_custom_call" | custom-call | flops 8455716864 | bytes 30425128 | tf_op jit(solution)/shard_map/back/pallas_call | solution.py:35
  78.7 1.1 copy-done.2
  81.9 7.6 %attention_back.1.d_qkv = bf16[512,2304]{1,0:T(8,128)(2,1)S(1)} custom-call(bf16[512,2304]{1,0:T(8,128)(2,1)S(1)} %copy-done.26, f32[2,12,256]{2,1,0:T(8,128)S(1)} %get-tuple-element.101.lse, bf16[512,768]{1,0:T(8,128)(2,1)S(1)} %get-tuple-element.113.d_attended), custom_call_target="tpu_custom_call" | custom-call | flops 2415919104 | bytes 5529600 | tf_op jit(solution)/shard_map/attention_back/pallas_call | solution.py:35
  89.5 4.7 %qkv_grad.1 = (f32[1152,768]{1,0:T(8,128)S(1)}, bf16[1152,768]{1,0:T(8,128)(2,1)S(1)}) custom-call(s32[10]{0:T(128)S(1)} %stack.25.place, bf16[512,768]{1,0:T(8,128)(2,1)S(1)} %copy-done.30, bf16[512,2304]{1,0:T(8,128)(2,1)S(1)} %attention_back.1.d_qkv), custom_call_target="tpu_custom_call" | custom-call | flops 1811939328 | bytes 8454184 | tf_op jit(solution)/shard_map/qkv_grad/pallas_call | solution.py:35
  94.8 4.2 %rest.1 = (f32[192,768]{1,0:T(8,128)S(1)}, bf16[224,768]{1,0:T(8,128)(2,1)S(1)}, f32[16,768]{1,0:T(8,128)S(1)}, f32[2,48,128]{2,1,0:T(8,128)S(1)}, f32[2,48,128]...) custom-call(s32[10]{0:T(128)S(1)} %stack.25.place, bf16[512,2304]{1,0:T(8,128)(2,1)S(1)} %attention_back.1.d_qkv, ...), custom_call_target="tpu_custom_call" | custom-call | flops 2174327296 | bytes 10472488 | tf_op jit(solution)/shard_map/rest/pallas_call | solution.py:35
  100.3 1.6 collective-permute-done.5.lc
  101.9 1.1 bulk0.1
  103.2 2.0 collective-permute-start.7
  105.2 1.5 collective-permute-start.25
  108.2 12.3 %collective-permute-done.7.cb = bf16[416,768]{1,0:T(8,128)(2,1)S(1)} collective-permute-done((bf16[416,768]{1,0:T(8,128)(2,1)S(1)}, bf16[416,768]{1,0:T(8,128)(2,1)S(1)}, u32[]{:S(2)}, u32[]{:S(2)}) %collective-permute-start.7) | collective-permute-done | bytes 639008 | tf_op jit(solution)/shard_map/ppermute | solution.py:545
  120.4 3.1 %collective-permute-done.6.ca = bf16[512,768]{1,0:T(8,128)(2,1)S(1)} collective-permute-done((bf16[512,768]{1,0:T(8,128)(2,1)S(1)}, bf16[512,768]{1,0:T(8,128)(2,1)S(1)}, u32[]{:S(2)}, u32[]{:S(2)}) %collective-permute-start.6) | collective-permute-done | bytes 786464 | tf_op jit(solution)/shard_map/ppermute | solution.py:545
  124.3 1.6 collective-permute-start.8
  126.4 28.9 %collective-permute-done.9.cb = bf16[224,768]{1,0:T(8,128)(2,1)S(1)} collective-permute-done((bf16[224,768]{1,0:T(8,128)(2,1)S(1)}, bf16[224,768]{1,0:T(8,128)(2,1)S(1)}, u32[]{:S(2)}, u32[]{:S(2)}) %collective-permute-start.9) | collective-permute-done | bytes 344096 | tf_op jit(solution)/shard_map/ppermute | solution.py:545
  156.1 1.7 collective-permute-start.10
  157.7 2.6 %collective-permute-start.11 = (bf16[144,768]{1,0:T(8,128)(2,1)S(1)}, bf16[144,768]{1,0:T(8,128)(2,1)S(1)}, u32[]{:S(2)}, u32[]{:S(2)}) collective-permute-start(bf16[144,768]{1,0:T(8,128)(2,1)S(1)} %get-tuple-element.142), channel_id=1, source_target_pairs={{0,16},{1,17},{2,18},{3,19},{4,20},{5,21},{6,22},{7,23},{8,24},{9,... | collective-permute-start | bytes 663560 | tf_op jit(solution)/shard_map/ppermute | solution.py:545
  160.5 5.9 %collective-permute-done.10.c1 = bf16[144,768]{1,0:T(8,128)(2,1)S(1)} collective-permute-done((bf16[144,768]{1,0:T(8,128)(2,1)S(1)}, bf16[144,768]{1,0:T(8,128)(2,1)S(1)}, u32[]{:S(2)}, u32[]{:S(2)}) %collective-permute-start.10) | collective-permute-done | bytes 221216 | tf_op jit(solution)/shard_map/ppermute | solution.py:545
  166.4 10.1 %collective-permute-done.11.c2 = bf16[144,768]{1,0:T(8,128)(2,1)S(1)} collective-permute-done((bf16[144,768]{1,0:T(8,128)(2,1)S(1)}, bf16[144,768]{1,0:T(8,128)(2,1)S(1)}, u32[]{:S(2)}, u32[]{:S(2)}) %collective-permute-start.11) | collective-permute-done | bytes 221216 | tf_op jit(solution)/shard_map/ppermute | solution.py:545
  177.2 3.3 %collective-permute-start.13 = (bf16[128,768]{1,0:T(8,128)(2,1)S(1)}, bf16[128,768]{1,0:T(8,128)(2,1)S(1)}, u32[]{:S(2)}, u32[]{:S(2)}) collective-permute-start(bf16[128,768]{1,0:T(8,128)(2,1)S(1)} %get-tuple-element.146.own), channel_id=1, source_target_pairs={{0,8},{1,9},{2,10},{3,11},{4,12},{5,13},{6,14},{7,15},{8,0},{9,1},... | collective-permute-start | bytes 589832 | tf_op jit(solution)/shard_map/ppermute | solution.py:545
  180.5 1.0 collective-permute-start.14
  181.5 1.5 collective-permute-start.15
  183.9 1.6 collective-permute-start.27
  186.4 10.2 %collective-permute-done.14.c2 = bf16[128,768]{1,0:T(8,128)(2,1)S(1)} collective-permute-done((bf16[128,768]{1,0:T(8,128)(2,1)S(1)}, bf16[128,768]{1,0:T(8,128)(2,1)S(1)}, u32[]{:S(2)}, u32[]{:S(2)}) %collective-permute-start.14) | collective-permute-done | bytes 196640 | tf_op jit(solution)/shard_map/ppermute | solution.py:545
  197.3 1.6 collective-permute-start.16
  199.4 5.9 %collective-permute-done.16.came_a = bf16[256,768]{1,0:T(8,128)(2,1)S(1)} collective-permute-done((bf16[256,768]{1,0:T(8,128)(2,1)S(1)}, bf16[256,768]{1,0:T(8,128)(2,1)S(1)}, u32[]{:S(2)}, u32[]{:S(2)}) %collective-permute-start.16) | collective-permute-done | bytes 393248 | tf_op jit(solution)/shard_map/ppermute | solution.py:545
  205.3 2.1 collective-permute-done.17.came_b
  209.2 1.5 fc_third.1
  210.7 2.7 %collective-permute-start.29 = (bf16[2,192,768]{2,1,0:T(8,128)(2,1)}, bf16[2,192,768]{2,1,0:T(8,128)(2,1)}, u32[]{:S(2)}, u32[]{:S(2)}) collective-permute-start(bf16[2,192,768]{2,1,0:T(8,128)(2,1)} %get-tuple-element.167), channel_id=1, source_target_pairs={{0,8},{1,9},{2,10},{3,11},{4,12},{5,13},{6,14},{7,15},{8,0},{9,1},... | collective-permute-start | bytes 1769480 | tf_op jit(solution)/shard_map/ppermute | solution.py:545
  215.1 1.5 collective-permute-start.2
  217.5 8.3 %collective-permute-done.2 = f32[2,104,128]{2,1,0:T(8,128)S(1)} collective-permute-done((f32[2,104,128]{2,1,0:T(8,128)S(1)}, f32[2,104,128]{2,1,0:T(8,128)S(1)}, u32[]{:S(2)}, u32[]{:S(2)}) %collective-permute-start.2) | collective-permute-done | bytes 106528 | tf_op jit(solution)/shard_map/ppermute | solution.py:545
  225.8 1.2 fc_fourth.1
  227.0 6.0 %collective-permute-start.30 = (bf16[1,192,768]{2,1,0:T(8,128)(2,1)S(1)}, bf16[1,192,768]{2,1,0:T(8,128)(2,1)S(1)}, u32[]{:S(2)}, u32[]{:S(2)}) collective-permute-start(bf16[1,192,768]{2,1,0:T(8,128)(2,1)S(1)} %get-tuple-element.169), channel_id=1, source_target_pairs={{0,16},{1,17},{2,18},{3,19},{4,20},{5,21},{6,22},{7,23},{8,24},{9,... | collective-permute-start | bytes 884744 | tf_op jit(solution)/shard_map/ppermute | solution.py:545
  235.4 6.6 %collective-permute-done.30.came = bf16[1,192,768]{2,1,0:T(8,128)(2,1)S(1)} collective-permute-done((bf16[1,192,768]{2,1,0:T(8,128)(2,1)S(1)}, bf16[1,192,768]{2,1,0:T(8,128)(2,1)S(1)}, u32[]{:S(2)}, u32[]{:S(2)}) %collective-permute-start.30) | collective-permute-done | bytes 294944 | tf_op jit(solution)/shard_map/ppermute | solution.py:545
  244.7 6.5 %last.1 = (f32[768,2304]{1,0:T(8,128)}, f32[768,768]{1,0:T(8,128)}, f32[256,768]{1,0:T(8,128)}, f32[96,768]{1,0:T(8,128)}, f32[48,768]{1,0:T(8,128)}, /*index=5*/bf16[2,16,16,768]{3,2,1,0:T(8,128)(2,1)S(1)}) custom-call(s32[10]{0:T(128)S(1)} %stack.25.place, bf16[512,768]{1,0:T(8,128)(2,1)S(1)} %get-tuple-element.149.refs_0_, ...), custom_call_target="tpu_custom_call" | custom-call | flops 1000000 | bytes 20000000 | tf_op jit(solution)/shard_map/last/pallas_call | solution.py:839
  (150 shorter events, 36.7 us)
Async XLA Ops:
  2.9 18.7 %collective-permute-start = (f32[2,104,128]{2,1,0:T(8,128)S(1)}, f32[2,104,128]{2,1,0:T(8,128)S(1)}, u32[]{:S(2)}, u32[]{:S(2)}) collective-permute-start(f32[2,104,128]{2,1,0:T(8,128)S(1)} %pad_maximum_fusion), channel_id=1, source_target_pairs={{0,1},{1,0},{2,3},{3,2},{4,5},{5,4},{6,7},{7,6},{8,9},{9,8},{10,11... | collective-permute-start | bytes 319496 | tf_op jit(solution)/shard_map/ppermute | solution.py:545
  26.4 14.8 %copy-start.12 = (f32[4,128,48]{1,2,0:T(8,128)S(1)}, f32[4,128,48]{1,2,0:T(8,128)}, u32[]{:S(2)}) copy-start(f32[4,128,48]{1,2,0:T(8,128)} %param.46) | copy-start | bytes 294916
  26.4 14.8 %copy-start.14 = (bf16[4,128,48]{1,2,0:T(8,128)(2,1)S(1)}, bf16[4,128,48]{1,2,0:T(8,128)(2,1)}, u32[]{:S(2)}) copy-start(bf16[4,128,48]{1,2,0:T(8,128)(2,1)} %param.24) | copy-start | bytes 147460
  26.4 14.8 %copy-start.15 = (s32[4,128]{1,0:T(4,128)S(1)}, s32[4,128]{1,0:T(4,128)}, u32[]{:S(2)}) copy-start(s32[4,128]{1,0:T(4,128)} %param.26) | copy-start | bytes 6148
  26.4 14.8 %copy-start.16 = (bf16[768,3072]{1,0:T(8,128)(2,1)S(1)}, bf16[768,3072]{1,0:T(8,128)(2,1)}, u32[]{:S(2)}) copy-start(bf16[768,3072]{1,0:T(8,128)(2,1)} %w_fc1.3) | copy-start | bytes 14155780
  26.4 14.8 %copy-start.20 = (bf16[768,768]{1,0:T(8,128)(2,1)S(1)}, bf16[768,768]{1,0:T(8,128)(2,1)}, u32[]{:S(2)}) copy-start(bf16[768,768]{1,0:T(8,128)(2,1)} %w_out.3) | copy-start | bytes 3538948
  26.4 14.8 %copy-start.23 = (bf16[768,96]{0,1:T(8,128)(2,1)S(1)}, bf16[768,96]{0,1:T(8,128)(2,1)}, u32[]{:S(2)}) copy-start(bf16[768,96]{0,1:T(8,128)(2,1)} %param.44) | copy-start | bytes 442372
  26.4 14.8 %copy-start.24 = (f32[4]{0:T(128)S(1)}, f32[4]{0:T(128)}, u32[]{:S(2)}) copy-start(f32[4]{0:T(128)} %det.1) | copy-start | bytes 52
  41.1 13.6 %copy-start.33 = (bf16[512,768]{1,0:T(8,128)(2,1)}, bf16[512,768]{1,0:T(8,128)(2,1)S(1)}, u32[]{:S(2)}) copy-start(bf16[512,768]{1,0:T(8,128)(2,1)S(1)} %get-tuple-element.98.attended) | copy-start | bytes 2359300
  56.4 3.3 %copy-start.7 = (f32[2,56,128]{2,1,0:T(8,128)}, f32[2,56,128]{2,1,0:T(8,128)S(1)}, u32[]{:S(2)}) copy-start(f32[2,56,128]{2,1,0:T(8,128)S(1)} %get-tuple-element.120) | copy-start | bytes 172036
  56.4 3.3 %copy-start.27 = (f32[512,768]{1,0:T(8,128)}, f32[512,768]{1,0:T(8,128)S(1)}, u32[]{:S(2)}) copy-start(f32[512,768]{1,0:T(8,128)S(1)} %get-tuple-element.102.d_hidden2) | copy-start | bytes 4718596
  56.4 3.4 %copy-start.21 = (bf16[768,768]{1,0:T(8,128)(2,1)S(1)}, bf16[768,768]{1,0:T(8,128)(2,1)}, u32[]{:S(2)}) copy-start(bf16[768,768]{1,0:T(8,128)(2,1)} %w_out.3) | copy-start | bytes 3538948
  56.4 3.4 %copy-start.34 = (bf16[512,768]{1,0:T(8,128)(2,1)S(1)}, bf16[512,768]{1,0:T(8,128)(2,1)}, u32[]{:S(2)}) copy-start(bf16[512,768]{1,0:T(8,128)(2,1)} %copy-done.33) | copy-start | bytes 2359300
  59.7 20.5 %collective-permute-start.1 = (bf16[8,192,768]{2,1,0:T(8,128)(2,1)S(1)}, bf16[8,192,768]{2,1,0:T(8,128)(2,1)S(1)}, u32[]{:S(2)}, u32[]{:S(2)}) collective-permute-start(bf16[8,192,768]{2,1,0:T(8,128)(2,1)S(1)} %get-tuple-element.111), channel_id=1, source_target_pairs={{0,2},{1,3},{2,0},{3,1},{4,6},{5,7},{6,4},{7,5},{8,10},{9,11},{10,... | collective-permute-start | bytes 7077896 | tf_op jit(solution)/shard_map/ppermute | solution.py:545
  79.7 27.0 %collective-permute-start.24 = (bf16[8,192,768]{2,1,0:T(8,128)(2,1)S(1)}, bf16[8,192,768]{2,1,0:T(8,128)(2,1)S(1)}, u32[]{:S(2)}, u32[]{:S(2)}) collective-permute-start(bf16[8,192,768]{2,1,0:T(8,128)(2,1)S(1)} %get-tuple-element.159), channel_id=1, source_target_pairs={{0,2},{1,3},{2,0},{3,1},{4,6},{5,7},{6,4},{7,5},{8,10},{9,11},{10,... | collective-permute-start | bytes 7077896 | tf_op jit(solution)/shard_map/ppermute | solution.py:545
  81.9 7.6 %copy-start.30 = (bf16[512,768]{1,0:T(8,128)(2,1)S(1)}, bf16[512,768]{1,0:T(8,128)(2,1)}, u32[]{:S(2)}) copy-start(bf16[512,768]{1,0:T(8,128)(2,1)} %copy-done.29) | copy-start | bytes 2359300
  89.4 5.3 %copy-start.1 = (bf16[768,2304]{1,0:T(8,128)(2,1)S(1)}, bf16[768,2304]{1,0:T(8,128)(2,1)}, u32[]{:S(2)}) copy-start(bf16[768,2304]{1,0:T(8,128)(2,1)} %w_qkv.3) | copy-start | bytes 10616836
  89.4 5.3 %copy-start.5 = (bf16[48,768]{1,0:T(8,128)(2,1)S(1)}, bf16[48,768]{1,0:T(8,128)(2,1)}, u32[]{:S(2)}) copy-start(bf16[48,768]{1,0:T(8,128)(2,1)} %w_patch.3) | copy-start | bytes 221188
  94.2 7.7 %collective-permute-start.3 = (bf16[1152,768]{1,0:T(8,128)(2,1)S(1)}, bf16[1152,768]{1,0:T(8,128)(2,1)S(1)}, u32[]{:S(2)}, u32[]{:S(2)}) collective-permute-start(bf16[1152,768]{1,0:T(8,128)(2,1)S(1)} %get-tuple-element.124), channel_id=1, source_target_pairs={{0,2},{1,3},{2,0},{3,1},{4,6},{5,7},{6,4},{7,5},{8,10},{9,11},{10,... | collective-permute-start | bytes 5308424 | tf_op jit(solution)/shard_map/ppermute | solution.py:545
  94.3 6.1 %collective-permute-start.4 = (bf16[448,768]{1,0:T(8,128)(2,1)S(1)}, bf16[448,768]{1,0:T(8,128)(2,1)S(1)}, u32[]{:S(2)}, u32[]{:S(2)}) collective-permute-start(bf16[448,768]{1,0:T(8,128)(2,1)S(1)} %get-tuple-element.126), channel_id=1, source_target_pairs={{0,2},{1,3},{2,0},{3,1},{4,6},{5,7},{6,4},{7,5},{8,10},{9,11},{10,... | collective-permute-start | bytes 2064392 | tf_op jit(solution)/shard_map/ppermute | solution.py:545
  94.8 7.1 %copy-start.3 = (f32[448,768]{1,0:T(8,128)S(1)}, f32[448,768]{1,0:T(8,128)}, u32[]{:S(2)}) copy-start(f32[448,768]{1,0:T(8,128)} %copy-done.2) | copy-start | bytes 4128772
  100.3 1.7 collective-permute-start.5
  103.1 20.4 %collective-permute-start.6 = (bf16[512,768]{1,0:T(8,128)(2,1)S(1)}, bf16[512,768]{1,0:T(8,128)(2,1)S(1)}, u32[]{:S(2)}, u32[]{:S(2)}) collective-permute-start(bf16[512,768]{1,0:T(8,128)(2,1)S(1)} %get-tuple-element.131), channel_id=1, source_target_pairs={{0,1},{1,0},{2,3},{3,2},{4,5},{5,4},{6,7},{7,6},{8,9},{9,8},{10,11... | collective-permute-start | bytes 2359304 | tf_op jit(solution)/shard_map/ppermute | solution.py:545
  103.2 17.3 %collective-permute-start.7 = (bf16[416,768]{1,0:T(8,128)(2,1)S(1)}, bf16[416,768]{1,0:T(8,128)(2,1)S(1)}, u32[]{:S(2)}, u32[]{:S(2)}) collective-permute-start(bf16[416,768]{1,0:T(8,128)(2,1)S(1)} %get-tuple-element.133), channel_id=1, source_target_pairs={{0,4},{1,5},{2,6},{3,7},{4,0},{5,1},{6,2},{7,3},{8,12},{9,13},{10,... | collective-permute-start | bytes 1916936 | tf_op jit(solution)/shard_map/ppermute | solution.py:545
  105.2 77.8 %collective-permute-start.25 = (bf16[8,96,768]{2,1,0:T(8,128)(2,1)S(1)}, bf16[8,96,768]{2,1,0:T(8,128)(2,1)S(1)}, u32[]{:S(2)}, u32[]{:S(2)}) collective-permute-start(bf16[8,96,768]{2,1,0:T(8,128)(2,1)S(1)} %get-tuple-element.112), channel_id=1, source_target_pairs={{0,1},{1,0},{2,3},{3,2},{4,5},{5,4},{6,7},{7,6},{8,9},{9,8},{10,11... | collective-permute-start | bytes 3538952 | tf_op jit(solution)/shard_map/ppermute | solution.py:545
  107.6 75.4 %collective-permute-start.26 = (bf16[4,192,768]{2,1,0:T(8,128)(2,1)S(1)}, bf16[4,192,768]{2,1,0:T(8,128)(2,1)S(1)}, u32[]{:S(2)}, u32[]{:S(2)}) collective-permute-start(bf16[4,192,768]{2,1,0:T(8,128)(2,1)S(1)} %get-tuple-element.161), channel_id=1, source_target_pairs={{0,4},{1,5},{2,6},{3,7},{4,0},{5,1},{6,2},{7,3},{8,12},{9,13},{10,... | collective-permute-start | bytes 3538952 | tf_op jit(solution)/shard_map/ppermute | solution.py:545
  124.3 31.1 %collective-permute-start.8 = (bf16[256,768]{1,0:T(8,128)(2,1)S(1)}, bf16[256,768]{1,0:T(8,128)(2,1)S(1)}, u32[]{:S(2)}, u32[]{:S(2)}) collective-permute-start(bf16[256,768]{1,0:T(8,128)(2,1)S(1)} %get-tuple-element.136), channel_id=1, source_target_pairs={{0,4},{1,5},{2,6},{3,7},{4,0},{5,1},{6,2},{7,3},{8,12},{9,13},{10,... | collective-permute-start | bytes 1179656 | tf_op jit(solution)/shard_map/ppermute | solution.py:545
  125.9 29.5 %collective-permute-start.9 = (bf16[224,768]{1,0:T(8,128)(2,1)S(1)}, bf16[224,768]{1,0:T(8,128)(2,1)S(1)}, u32[]{:S(2)}, u32[]{:S(2)}) collective-permute-start(bf16[224,768]{1,0:T(8,128)(2,1)S(1)} %get-tuple-element.138), channel_id=1, source_target_pairs={{0,1},{1,0},{2,3},{3,2},{4,5},{5,4},{6,7},{7,6},{8,9},{9,8},{10,11... | collective-permute-start | bytes 1032200 | tf_op jit(solution)/shard_map/ppermute | solution.py:545
  156.1 10.3 %collective-permute-start.10 = (bf16[144,768]{1,0:T(8,128)(2,1)S(1)}, bf16[144,768]{1,0:T(8,128)(2,1)S(1)}, u32[]{:S(2)}, u32[]{:S(2)}) collective-permute-start(bf16[144,768]{1,0:T(8,128)(2,1)S(1)} %get-tuple-element.141), channel_id=1, source_target_pairs={{0,8},{1,9},{2,10},{3,11},{4,12},{5,13},{6,14},{7,15},{8,0},{9,1},... | collective-permute-start | bytes 663560 | tf_op jit(solution)/shard_map/ppermute | solution.py:545
  157.7 18.7 %collective-permute-start.11 = (bf16[144,768]{1,0:T(8,128)(2,1)S(1)}, bf16[144,768]{1,0:T(8,128)(2,1)S(1)}, u32[]{:S(2)}, u32[]{:S(2)}) collective-permute-start(bf16[144,768]{1,0:T(8,128)(2,1)S(1)} %get-tuple-element.142), channel_id=1, source_target_pairs={{0,16},{1,17},{2,18},{3,19},{4,20},{5,21},{6,22},{7,23},{8,24},{9,... | collective-permute-start | bytes 663560 | tf_op jit(solution)/shard_map/ppermute | solution.py:545
  160.3 16.2 %collective-permute-start.12 = (bf16[144,768]{1,0:T(8,128)(2,1)S(1)}, bf16[144,768]{1,0:T(8,128)(2,1)S(1)}, u32[]{:S(2)}, u32[]{:S(2)}) collective-permute-start(bf16[144,768]{1,0:T(8,128)(2,1)S(1)} %get-tuple-element.143), channel_id=1, source_target_pairs={{0,24},{1,25},{2,26},{3,27},{4,28},{5,29},{6,30},{7,31},{8,16},{9,... | collective-permute-start | bytes 663560 | tf_op jit(solution)/shard_map/ppermute | solution.py:545
  177.2 9.2 %collective-permute-start.13 = (bf16[128,768]{1,0:T(8,128)(2,1)S(1)}, bf16[128,768]{1,0:T(8,128)(2,1)S(1)}, u32[]{:S(2)}, u32[]{:S(2)}) collective-permute-start(bf16[128,768]{1,0:T(8,128)(2,1)S(1)} %get-tuple-element.146.own), channel_id=1, source_target_pairs={{0,8},{1,9},{2,10},{3,11},{4,12},{5,13},{6,14},{7,15},{8,0},{9,1},... | collective-permute-start | bytes 589832 | tf_op jit(solution)/shard_map/ppermute | solution.py:545
  180.5 16.1 %collective-permute-start.14 = (bf16[128,768]{1,0:T(8,128)(2,1)S(1)}, bf16[128,768]{1,0:T(8,128)(2,1)S(1)}, u32[]{:S(2)}, u32[]{:S(2)}) collective-permute-start(bf16[128,768]{1,0:T(8,128)(2,1)S(1)} %get-tuple-element.146.own), channel_id=1, source_target_pairs={{0,16},{1,17},{2,18},{3,19},{4,20},{5,21},{6,22},{7,23},{8,24},{9,... | collective-permute-start | bytes 589832 | tf_op jit(solution)/shard_map/ppermute | solution.py:545
  181.5 15.1 %collective-permute-start.15 = (bf16[128,768]{1,0:T(8,128)(2,1)S(1)}, bf16[128,768]{1,0:T(8,128)(2,1)S(1)}, u32[]{:S(2)}, u32[]{:S(2)}) collective-permute-start(bf16[128,768]{1,0:T(8,128)(2,1)S(1)} %get-tuple-element.146.own), channel_id=1, source_target_pairs={{0,24},{1,25},{2,26},{3,27},{4,28},{5,29},{6,30},{7,31},{8,16},{9,... | collective-permute-start | bytes 589832 | tf_op jit(solution)/shard_map/ppermute | solution.py:545
  183.9 25.3 %collective-permute-start.27 = (bf16[4,96,768]{2,1,0:T(8,128)(2,1)S(1)}, bf16[4,96,768]{2,1,0:T(8,128)(2,1)S(1)}, u32[]{:S(2)}, u32[]{:S(2)}) collective-permute-start(bf16[4,96,768]{2,1,0:T(8,128)(2,1)S(1)} %get-tuple-element.164), channel_id=1, source_target_pairs={{0,4},{1,5},{2,6},{3,7},{4,0},{5,1},{6,2},{7,3},{8,12},{9,13},{10,... | collective-permute-start | bytes 1769480 | tf_op jit(solution)/shard_map/ppermute | solution.py:545
  185.5 23.7 %collective-permute-start.28 = (bf16[4,96,768]{2,1,0:T(8,128)(2,1)S(1)}, bf16[4,96,768]{2,1,0:T(8,128)(2,1)S(1)}, u32[]{:S(2)}, u32[]{:S(2)}) collective-permute-start(bf16[4,96,768]{2,1,0:T(8,128)(2,1)S(1)} %get-tuple-element.165), channel_id=1, source_target_pairs={{0,1},{1,0},{2,3},{3,2},{4,5},{5,4},{6,7},{7,6},{8,9},{9,8},{10,11... | collective-permute-start | bytes 1769480 | tf_op jit(solution)/shard_map/ppermute | solution.py:545
  197.3 8.0 %collective-permute-start.16 = (bf16[256,768]{1,0:T(8,128)(2,1)S(1)}, bf16[256,768]{1,0:T(8,128)(2,1)S(1)}, u32[]{:S(2)}, u32[]{:S(2)}) collective-permute-start(bf16[256,768]{1,0:T(8,128)(2,1)S(1)} %get-tuple-element.147.own_a), channel_id=1, source_target_pairs={{0,4},{1,5},{2,6},{3,7},{4,0},{5,1},{6,2},{7,3},{8,12},{9,13},{10,... | collective-permute-start | bytes 1179656 | tf_op jit(solution)/shard_map/ppermute | solution.py:545
  198.9 8.6 %collective-permute-start.17 = (bf16[256,768]{1,0:T(8,128)(2,1)S(1)}, bf16[256,768]{1,0:T(8,128)(2,1)S(1)}, u32[]{:S(2)}, u32[]{:S(2)}) collective-permute-start(bf16[256,768]{1,0:T(8,128)(2,1)S(1)} %get-tuple-element.148.own_b), channel_id=1, source_target_pairs={{0,1},{1,0},{2,3},{3,2},{4,5},{5,4},{6,7},{7,6},{8,9},{9,8},{10,11... | collective-permute-start | bytes 1179656 | tf_op jit(solution)/shard_map/ppermute | solution.py:545
  208.1 26.1 %collective-permute-start.18 = (bf16[512,768]{1,0:T(8,128)(2,1)S(1)}, bf16[512,768]{1,0:T(8,128)(2,1)S(1)}, u32[]{:S(2)}, u32[]{:S(2)}) collective-permute-start(bf16[512,768]{1,0:T(8,128)(2,1)S(1)} %get-tuple-element.149.refs_0_), channel_id=1, source_target_pairs={{0,1},{1,0},{2,3},{3,2},{4,5},{5,4},{6,7},{7,6},{8,9},{9,8},{10,11... | collective-permute-start | bytes 2359304 | tf_op jit(solution)/shard_map/ppermute | solution.py:545
  208.7 25.5 %collective-permute-start.19 = (bf16[512,768]{1,0:T(8,128)(2,1)S(1)}, bf16[512,768]{1,0:T(8,128)(2,1)}, u32[]{:S(2)}, u32[]{:S(2)}) collective-permute-start(bf16[512,768]{1,0:T(8,128)(2,1)S(1)} %get-tuple-element.150.refs_2_), channel_id=1, source_target_pairs={{0,4},{1,5},{2,6},{3,7},{4,0},{5,1},{6,2},{7,3},{8,12},{9,13},{10,... | collective-permute-start | bytes 2359304 | tf_op jit(solution)/shard_map/ppermute | solution.py:545
  210.7 15.1 %collective-permute-start.29 = (bf16[2,192,768]{2,1,0:T(8,128)(2,1)}, bf16[2,192,768]{2,1,0:T(8,128)(2,1)}, u32[]{:S(2)}, u32[]{:S(2)}) collective-permute-start(bf16[2,192,768]{2,1,0:T(8,128)(2,1)} %get-tuple-element.167), channel_id=1, source_target_pairs={{0,8},{1,9},{2,10},{3,11},{4,12},{5,13},{6,14},{7,15},{8,0},{9,1},... | collective-permute-start | bytes 1769480 | tf_op jit(solution)/shard_map/ppermute | solution.py:545
  215.1 10.7 %collective-permute-start.2 = (f32[2,104,128]{2,1,0:T(8,128)S(1)}, f32[2,104,128]{2,1,0:T(8,128)S(1)}, u32[]{:S(2)}, u32[]{:S(2)}) collective-permute-start(f32[2,104,128]{2,1,0:T(8,128)S(1)} %pad_maximum_fusion.1), channel_id=1, source_target_pairs={{0,1},{1,0},{2,3},{3,2},{4,5},{5,4},{6,7},{7,6},{8,9},{9,8},{10,11... | collective-permute-start | bytes 319496 | tf_op jit(solution)/shard_map/ppermute | solution.py:545
  227.0 15.9 %copy-start.11 = (f32[16,768]{1,0:T(8,128)S(1)}, f32[16,768]{1,0:T(8,128)}, u32[]{:S(2)}) copy-start(f32[16,768]{1,0:T(8,128)} %copy-done.10) | copy-start | bytes 147460
  227.0 15.0 %collective-permute-start.30 = (bf16[1,192,768]{2,1,0:T(8,128)(2,1)S(1)}, bf16[1,192,768]{2,1,0:T(8,128)(2,1)S(1)}, u32[]{:S(2)}, u32[]{:S(2)}) collective-permute-start(bf16[1,192,768]{2,1,0:T(8,128)(2,1)S(1)} %get-tuple-element.169), channel_id=1, source_target_pairs={{0,16},{1,17},{2,18},{3,19},{4,20},{5,21},{6,22},{7,23},{8,24},{9,... | collective-permute-start | bytes 884744 | tf_op jit(solution)/shard_map/ppermute | solution.py:545
  233.7 11.0 %collective-permute-start.20 = (bf16[512,768]{1,0:T(8,128)(2,1)S(1)}, bf16[512,768]{1,0:T(8,128)(2,1)S(1)}, u32[]{:S(2)}, u32[]{:S(2)}) collective-permute-start(bf16[512,768]{1,0:T(8,128)(2,1)S(1)} %get-tuple-element.149.refs_0_), channel_id=1, source_target_pairs={{0,2},{1,3},{2,0},{3,1},{4,6},{5,7},{6,4},{7,5},{8,10},{9,11},{10,... | collective-permute-start | bytes 2359304 | tf_op jit(solution)/shard_map/ppermute | solution.py:545
  233.7 11.0 %collective-permute-start.22 = (bf16[512,768]{1,0:T(8,128)(2,1)S(1)}, bf16[512,768]{1,0:T(8,128)(2,1)}, u32[]{:S(2)}, u32[]{:S(2)}) collective-permute-start(bf16[512,768]{1,0:T(8,128)(2,1)S(1)} %get-tuple-element.150.refs_2_), channel_id=1, source_target_pairs={{0,2},{1,3},{2,0},{3,1},{4,6},{5,7},{6,4},{7,5},{8,10},{9,11},{10,... | collective-permute-start | bytes 2359304 | tf_op jit(solution)/shard_map/ppermute | solution.py:545
  234.2 10.5 %collective-permute-start.21 = (bf16[512,768]{1,0:T(8,128)(2,1)S(1)}, bf16[512,768]{1,0:T(8,128)(2,1)}, u32[]{:S(2)}, u32[]{:S(2)}) collective-permute-start(bf16[512,768]{1,0:T(8,128)(2,1)S(1)} %collective-permute-done.18.refs_1_), channel_id=1, source_target_pairs={{0,2},{1,3},{2,0},{3,1},{4,6},{5,7},{6,4},{7,5},{8,10},{9,11},{10,... | collective-permute-start | bytes 2359304 | tf_op jit(solution)/shard_map/ppermute | solution.py:545
  234.2 10.5 %collective-permute-start.23 = (bf16[512,768]{1,0:T(8,128)(2,1)}, bf16[512,768]{1,0:T(8,128)(2,1)}, u32[]{:S(2)}, u32[]{:S(2)}) collective-permute-start(bf16[512,768]{1,0:T(8,128)(2,1)} %collective-permute-done.19.refs_3_), channel_id=1, source_target_pairs={{0,2},{1,3},{2,0},{3,1},{4,6},{5,7},{6,4},{7,5},{8,10},{9,11},{10,... | collective-permute-start | bytes 2359304 | tf_op jit(solution)/shard_map/ppermute | solution.py:545
  (18 other events, 27.1 us)

commit v3 on v2

v3 whole, which is shorter than its diff:
```python
import math
from functools import partial

import jax
import jax.numpy as jnp
from jax import lax
from jax.experimental import pallas as pl
from jax.experimental.pallas import tpu as pltpu
from jax.sharding import PartitionSpec as P

HEADS = 12
EPS = 1e-05
GELU_A = math.sqrt(2.0 / math.pi)
GELU_B = 0.044715
bf16 = jnp.bfloat16
f32 = jnp.float32
AXES = ("dp", "seq")
ROW = dict(bp=0, n1g=1, n1s=2, n2g=3, n2s=4, b2=5, fg=6, fs=7, bh=8, b1=9)


def dot(left, right, a=1, b=0):
    return lax.dot_general(
        left, right, (((a,), (b,)), ((), ())), preferred_element_type=f32
    )


SMEM, VMEM, ANY, HBM = pltpu.SMEM, pltpu.VMEM, pl.ANY, pltpu.HBM


class Line:
    def __init__(self):
        self.last = None

    def call(self, body, outs, args, name, flops, limit, places=None, scratch=(), after=()):
        places = places or {}
        args = list(args)
        after = tuple(after) + ((self.last,) if self.last is not None else ())
        if after:
            at = max(i for i in range(len(args)) if places.get(i, VMEM) is VMEM)
            args[at] = tie(args[at], *after)
        specs = [pl.BlockSpec(memory_space=places.get(i, VMEM)) for i in range(len(args))]
        for i, place in places.items():
            if place is HBM:
                args[i] = pltpu.with_memory_space_constraint(args[i], HBM)
        got = pl.pallas_call(
            body,
            out_shape=[jax.ShapeDtypeStruct(s, d) for s, d in outs],
            in_specs=specs,
            out_specs=[pl.BlockSpec(memory_space=VMEM)] * len(outs),
            scratch_shapes=list(scratch),
            compiler_params=pltpu.CompilerParams(vmem_limit_bytes=int(limit * 2**20)),
            cost_estimate=pl.CostEstimate(flops=int(flops), bytes_accessed=1, transcendentals=0),
            name=name,
        )(*args)
        self.last = got[0]
        return got


def tie(value, *others):
    return lax.optimization_barrier((value,) + others)[0]


def where():
    dp = lax.axis_index("dp")
    return lax.axis_index("seq"), dp & 1, (dp >> 1) & 1, dp >> 2


def my_bit(bit):
    return lax.axis_index("seq") if bit == 0 else (lax.axis_index("dp") >> (bit - 1)) & 1


def row_of(ref):
    return ref[...].reshape(1, ref.shape[0]).astype(f32)


def centered(hidden):
    center = hidden - jnp.mean(hidden, axis=-1, keepdims=True)
    spread = jnp.mean(center * center, axis=-1, keepdims=True)
    inverse = lax.rsqrt(spread + EPS)
    return center * inverse, inverse


def norm_pull(grad, unit, inverse, gain):
    scaled = grad * gain
    mean = jnp.mean(scaled, axis=-1, keepdims=True)
    along = jnp.mean(scaled * unit, axis=-1, keepdims=True)
    return inverse * (scaled - mean - unit * along)


def col_sum(values):
    return jnp.sum(values, axis=0, keepdims=True)


def both_halves(seq, own, came):
    low = jnp.where(seq == 0, own, came)
    high = jnp.where(seq == 0, came, own)
    return jnp.concatenate([low, high], axis=1)


def prep_kernel(runs, cot_runs, valid, out, part, mask, sems):
    x, _, _, _ = where()
    items = out.shape[0]
    feat, span = runs.shape[1:]
    theirs = pl.ds((1 - x) * items, items)
    copies = [
        pltpu.make_async_copy(runs.at[theirs], part, sems.at[0]),
        pltpu.make_async_copy(cot_runs.at[theirs], out.at[:, feat : 2 * feat], sems.at[1]),
        pltpu.make_async_copy(valid, mask, sems.at[2]),
    ]
    for copy in copies:
        copy.start()
    for copy in copies:
        copy.wait()
    out[:, :feat] = part[...].astype(f32)
    for i in range(items):
        row = mask[pl.ds((1 - x) * items + i, 1), :].astype(f32)
        out[i, 2 * feat :] = jnp.broadcast_to(row, (out.shape[1] - 2 * feat, span))


def front_kernel(labels, came, runs_in, class_embed, b_patch_in, gain_in, shift_in, pos_in, w_patch_in, w_qkv_in,
                 w_out_in, w_fc1_in, w_fc2_in,
                 hidden0, normed1, qkv, shifted_t, attended, lse, w_qkv, w_out, w_fc1, w_fc2,
                 class_rows, runs, b_patch, gain, shift, pos, w_patch, sems):
    x, _, _, _ = where()
    items = came.shape[0]
    feat = w_patch.shape[0]
    length, width = pos.shape
    copies = []

    def fetch(source, target):
        copies.append(pltpu.make_async_copy(source, target, sems.at[len(copies)]))
        copies[-1].start()

    fetch(runs_in.at[pl.ds(x * items, items)], runs)
    for i in range(items):
        tile = pl.multiple_of(labels[x * items + i] // 16 * 16, 16)
        fetch(class_embed.at[pl.ds(tile, 16)], class_rows.at[i])
    for source, target in ((b_patch_in, b_patch), (gain_in, gain), (shift_in, shift), (w_patch_in, w_patch),
                           (pos_in, pos), (w_qkv_in, w_qkv)):
        fetch(source, target)
    small = len(copies) - 1
    for copy in copies[:small]:
        copy.wait()
    gain_row, shift_row, bias = row_of(gain), row_of(shift), row_of(b_patch)
    at_row = lax.broadcasted_iota(jnp.int32, (16, width), 0)
    for i in range(items):
        rows = slice(i * length, (i + 1) * length)
        whole = both_halves(x, runs[i].astype(f32), came[i, :feat])
        lane = lax.broadcasted_iota(jnp.int32, whole.shape, 1)
        moved = jnp.where(lane == 0, 0.0, pltpu.roll(whole, 1, 1)).astype(bf16)
        shifted_t[:, rows] = moved
        mine = at_row == labels[x * items + i] % 16
        base = bias + col_sum(jnp.where(mine, class_rows[i].astype(f32), 0.0))
        h0 = dot(moved, w_patch[...], 0, 0) + base + pos[...].astype(f32)
        hidden0[rows, :] = h0
        unit, _ = centered(h0)
        normed1[rows, :] = (unit * gain_row + shift_row).astype(bf16)
    copies[small].wait()
    for source, target in ((w_out_in, w_out), (w_fc1_in, w_fc1), (w_fc2_in, w_fc2)):
        fetch(source, target)
    for j in range(3):
        cols = slice(j * width, (j + 1) * width)
        qkv[:, cols] = dot(normed1[...], w_qkv[:, cols]).astype(bf16)
    key_at = lax.broadcasted_iota(jnp.int32, (length, length), 0)
    query_at = lax.broadcasted_iota(jnp.int32, (length, length), 1)
    allowed = key_at <= query_at

    def step(p, carry):
        for i in range(items):
            rows = slice(i * length, (i + 1) * length)
            at = [pl.ds(pl.multiple_of(j * width + p * 128, 128), 128) for j in range(3)]
            q, k, v = (qkv[rows, at[j]] for j in range(3))
            first = lax.broadcasted_iota(jnp.int32, q.shape, 1) < 64
            v_t = v.T
            outs = []
            for h in range(2):
                mine = first if h == 0 else ~first
                qh = jnp.where(mine, q * 0.125, jnp.zeros_like(q))
                s = jnp.where(allowed, dot(k, qh, 1, 1), -1e30)
                top = jnp.max(s, axis=0, keepdims=True)
                e = jnp.exp(s - top)
                total = jnp.sum(e, axis=0, keepdims=True)
                lse[i, pl.ds(p * 2 + h, 1), :] = top + jnp.log(total)
                probs = (e * (1.0 / total)).astype(bf16)
                outs.append(dot(v_t[h * 64 : (h + 1) * 64], probs))
            attended[rows, at[0]] = jnp.concatenate(outs, axis=0).T.astype(bf16)
        return carry

    lax.fori_loop(0, HEADS // 2, step, 0)
    for copy in copies[small + 1 :]:
        copy.wait()


def middle_kernel(det, labels, class_slot, hidden0, attended, w_out, gain2, shift2, w_fc1, b_fc1, w_fc2, b_fc2,
                  gainf, shiftf, w_head_t, b_head, runs, cot_runs, valid_runs, came,
                  hidden1, normed2, act, slope, d_hidden2, part_in, lat_keep, lat_send,
                  short, grad_head_t, facts):
    x, _, _, _ = where()
    items = came.shape[0]
    feat = runs.shape[1]
    width = w_out.shape[0]
    span = came.shape[2]
    length = 2 * span
    hidden1[...] = hidden0[...] + dot(attended[...], w_out[...])
    gain, shift = row_of(gain2), row_of(shift2)
    for i in range(items):
        rows = slice(i * length, (i + 1) * length)
        unit, _ = centered(hidden1[rows, :])
        normed2[rows, :] = (unit * gain + shift).astype(bf16)
    total = None
    for j in range(w_fc1.shape[1] // width):
        cols = slice(j * width, (j + 1) * width)
        up = dot(normed2[...], w_fc1[:, cols]) + b_fc1[cols].reshape(1, width).astype(f32)
        square = up * up
        half = 0.5 * jnp.tanh(up * (GELU_A + GELU_A * GELU_B * square)) + 0.5
        value = up * half
        act[:, cols] = value.astype(bf16)
        slope[:, cols] = (
            half + 2.0 * value * (1.0 - half) * (GELU_A + 3.0 * GELU_A * GELU_B * square)
        ).astype(bf16)
        part = dot(act[:, cols], w_fc2[cols, :])
        total = part if total is None else total + part
    hidden2 = hidden1[...] + total + row_of(b_fc2)
    unit, inverse_dev = centered(hidden2)
    gain = row_of(gainf)
    normed3 = (unit * gain + row_of(shiftf)).astype(bf16)
    bias = jnp.broadcast_to(row_of(b_head), (8, 2 * feat)).T[:, :1]
    head = dot(w_head_t[...], normed3, 1, 1) + bias
    short[...] = jnp.zeros(short.shape, f32)
    d_heads = []
    sums = [jnp.zeros((1, 1), f32), jnp.zeros((1, 1), f32), jnp.full((1, 1), -1e30, f32)]
    for i in range(items):
        cols = slice(i * length, (i + 1) * length)
        source = x * items + i
        given = both_halves(x, runs[source].astype(f32), came[i, :feat])
        cot = both_halves(x, cot_runs[source], came[i, feat : 2 * feat])
        valid = both_halves(
            x, valid_runs[source].astype(f32), came[i, 2 * feat : 2 * feat + 1]
        )
        shift_part = head[:feat, cols]
        log_scale = head[feat:, cols]
        inverse = jnp.exp(-log_scale)
        moved = (given - shift_part) * inverse
        latent = valid * moved + (1.0 - valid) * given
        d_moved = valid * cot
        d_heads.append(
            jnp.concatenate(
                [-d_moved * inverse, -d_moved * moved - valid * det[source]], axis=0
            ).astype(bf16)
        )
        part_in[:, cols] = cot * (1.0 - valid) + d_moved * inverse
        counted = valid * log_scale
        item_sum = jnp.sum(jnp.sum(counted, axis=1, keepdims=True), axis=0, keepdims=True)
        sums[0] = sums[0] + item_sum
        sums[1] = sums[1] + jnp.sum(valid, axis=1, keepdims=True) * feat
        tops = jnp.where(valid > 0, log_scale, -1e30)
        tops = jnp.max(jnp.max(tops, axis=1, keepdims=True), axis=0, keepdims=True)
        sums[2] = jnp.maximum(sums[2], tops)
        low, high = latent[:, :span], latent[:, span:]
        logdet = jnp.broadcast_to(-item_sum, (8, span))
        lat_keep[i, :feat] = jnp.where(x == 0, low, high)
        lat_send[i, :feat] = jnp.where(x == 0, high, low)
        lat_keep[i, feat:] = logdet
        lat_send[i, feat:] = logdet
    lane = lax.broadcasted_iota(jnp.int32, facts.shape, 1)
    row = jnp.zeros(facts.shape, f32)
    for k, value in enumerate(sums):
        for j in range(3):
            piece = value.astype(bf16).astype(f32)
            value = value - piece
            row = jnp.where(lane == 3 * k + j, piece, row)
    for i in range(items):
        slot = class_slot[labels[x * items + i]]
        row = jnp.where(lane == 9 + i, (slot // 32).astype(f32), row)
        row = jnp.where(lane == 9 + items + i, (slot % 32).astype(f32), row)
    facts[...] = row
    d_head = jnp.concatenate(d_heads, axis=1)
    grad_head_t[...] = dot(d_head, normed3)
    short[ROW["bh"] : ROW["bh"] + 1, : 2 * feat] = dot(
        jnp.ones((8, d_head.shape[1]), bf16), d_head, 1, 1
    )[:1]
    d_normed3 = dot(d_head, w_head_t[...], 0, 0)
    short[ROW["fg"] : ROW["fg"] + 1, :] = col_sum(d_normed3 * unit)
    short[ROW["fs"] : ROW["fs"] + 1, :] = col_sum(d_normed3)
    pulled = norm_pull(d_normed3, unit, inverse_dev, gain)
    d_hidden2[...] = pulled
    short[ROW["b2"] : ROW["b2"] + 1, :] = col_sum(pulled.astype(bf16).astype(f32))


def split_by(bit, block, keep, send, half):
    low, high = block[:half], block[half:]
    keep[...] = jnp.where(bit == 0, low, high).astype(keep.dtype)
    send[...] = jnp.where(bit == 0, high, low).astype(send.dtype)


def split_groups(core, block, first, keep, send):
    group = keep.shape[1]
    for k in range(block.shape[0] // (2 * group)):
        rows = block[2 * group * k : 2 * group * (k + 1)]
        split_by(core, rows, keep.at[first + k], send.at[first + k], group)


STEP = 384


def fc2_kernel(half, act, d_hidden2, keep, send):
    _, core, _, _ = where()
    d_mlp = d_hidden2[...].astype(bf16)
    count = act.shape[1] // 2 // STEP
    for j in range(count):
        at = (half * count + j) * STEP
        block = dot(act[:, at : at + STEP], d_mlp, 0, 0)
        split_groups(core, block, j * STEP // (2 * keep.shape[1]), keep, send)


def fc1_kernel(half, d_hidden2, w_fc2, slope, normed2, w_fc1, *refs):
    before, (keep, send, total_out, bias) = refs[:-4], refs[-4:]
    _, core, _, _ = where()
    width = normed2.shape[1]
    d_mlp = d_hidden2[...].astype(bf16)
    total = before[0][...] if before else None
    count = w_fc1.shape[1] // 2 // width
    for j in range(count):
        at = (half * count + j) * width
        cols = slice(at, at + width)
        d_up = (dot(d_mlp, w_fc2[cols, :], 1, 1) * slope[:, cols].astype(f32)).astype(bf16)
        bias[j : j + 1, :] = col_sum(d_up.astype(f32))
        for m in range(width // STEP):
            block = dot(d_up[:, m * STEP : (m + 1) * STEP], normed2[...], 0, 0)
            split_groups(core, block, (j * width + m * STEP) // (2 * keep.shape[1]), keep, send)
        part = dot(d_up, w_fc1[:, cols], 1, 1)
        total = part if total is None else total + part
    total_out[...] = total


def back_kernel(d_hidden2, total_in, hidden1, gain2, attended, w_out, short_in, bias_a, bias_b, grad_head_t,
                d_hidden1, short, out_keep, out_send, d_attended):
    _, core, _, _ = where()
    width = w_out.shape[0]
    short[...] = short_in[...]
    n = bias_a.shape[0]
    short[ROW["b1"] : ROW["b1"] + n, :] = bias_a[...]
    short[ROW["b1"] + n : ROW["b1"] + 2 * n, :] = bias_b[...]
    unit, inverse_dev = centered(hidden1[...])
    total = total_in[...]
    short[ROW["n2g"] : ROW["n2g"] + 1, :] = col_sum(total * unit)
    short[ROW["n2s"] : ROW["n2s"] + 1, :] = col_sum(total)
    h1 = d_hidden2[...] + norm_pull(total, unit, inverse_dev, row_of(gain2))
    d_hidden1[...] = h1
    d_out = h1.astype(bf16)
    d_attended[...] = dot(d_out, w_out[...], 1, 1).astype(bf16)
    grad_out = dot(attended[...], d_out, 0, 0)
    half = out_keep.shape[0]
    rest = 2 * half - grad_out.shape[0] - grad_head_t.shape[0]
    block = jnp.concatenate([grad_out, grad_head_t[...], jnp.zeros((rest, width), f32)], axis=0)
    split_by(core, block, out_keep, out_send, half)


def attention_back_kernel(qkv, lse, d_attended, d_qkv):
    rows_all, width = d_attended.shape
    items = lse.shape[0]
    length = rows_all // items
    key_at = lax.broadcasted_iota(jnp.int32, (length, length), 0)
    query_at = lax.broadcasted_iota(jnp.int32, (length, length), 1)
    allowed = key_at <= query_at

    def step(p, carry):
        for i in range(items):
            rows = slice(i * length, (i + 1) * length)
            at = [pl.ds(pl.multiple_of(j * width + p * 128, 128), 128) for j in range(3)]
            q, k, v = (qkv[rows, at[j]] for j in range(3))
            q = q * 0.125
            d_o = d_attended[rows, at[0]]
            first = lax.broadcasted_iota(jnp.int32, q.shape, 1) < 64
            none = jnp.zeros_like(q)
            total = [None, None, None]
            for h in range(2):
                mine = first if h == 0 else ~first
                qh = jnp.where(mine, q, none)
                kh = jnp.where(mine, k * 0.125, none)
                dh = jnp.where(mine, d_o, none)
                s = jnp.where(allowed, dot(k, qh, 1, 1), -1e30)
                probs = jnp.exp(s - lse[i, pl.ds(p * 2 + h, 1), :])
                d_probs = dot(v, dh, 1, 1)
                delta = jnp.sum(probs * d_probs, axis=0, keepdims=True)
                d_s = (probs * (d_probs - delta)).astype(bf16)
                parts = [dot(d_s, kh, 0, 0), dot(d_s, qh), dot(probs.astype(bf16), dh)]
                total = [b if a is None else a + b for a, b in zip(total, parts)]
            for j in range(3):
                d_qkv[rows, at[j]] = total[j].astype(bf16)
        return carry

    lax.fori_loop(0, HEADS // 2, step, 0)


def qkv_kernel(normed1, d_qkv, keep, send):
    _, core, _, _ = where()
    width = normed1.shape[1]
    half = keep.shape[0]
    for m in range(width // STEP):
        block = dot(normed1[:, m * STEP : (m + 1) * STEP], d_qkv[...], 0, 0)
        for j in range(3):
            part = block[:, j * width : (j + 1) * width]
            at = j * width + m * STEP
            inside = at % half

            @pl.when(core == at // half)
            def _():
                keep[inside : inside + STEP, :] = part

            @pl.when(core != at // half)
            def _():
                send[inside : inside + STEP, :] = part.astype(bf16)


def rest_kernel(d_qkv, w_qkv, hidden0, d_hidden1, gain1, shifted_t, w_patch, part_in, short_in, facts, lat_keep, lat_send,
                keep, send, short, in_keep, in_send, extra):
    x, core, _, _ = where()
    width = hidden0.shape[1]
    items, done, span = lat_keep.shape
    feat = w_patch.shape[0]
    length = 2 * span
    in_keep[:, :done] = lat_keep[...]
    in_send[:, :done] = lat_send[...]
    d_normed1 = dot(d_qkv[...], w_qkv[...], 1, 1)
    unit, inverse_dev = centered(hidden0[...])
    short[...] = short_in[...]
    short[ROW["n1g"] : ROW["n1g"] + 1, :] = col_sum(d_normed1 * unit)
    short[ROW["n1s"] : ROW["n1s"] + 1, :] = col_sum(d_normed1)
    d0 = d_hidden1[...] + norm_pull(d_normed1, unit, inverse_dev, row_of(gain1))
    d_low = d0.astype(bf16)
    extra[...] = jnp.zeros(extra.shape, bf16)
    d_pos, whole = None, None
    for i in range(items):
        mine = d0[i * length : (i + 1) * length]
        d_pos = mine if d_pos is None else d_pos + mine
        item = col_sum(mine)
        whole = item if whole is None else whole + item
        extra[i : i + 1, :] = item.astype(bf16)
    extra[items : items + 1, :] = facts[...].astype(bf16)
    short[ROW["bp"] : ROW["bp"] + 1, :] = whole
    d_patch = dot(shifted_t[...], d_low)
    half = keep.shape[0]
    rest = 2 * half - d_pos.shape[0] - d_patch.shape[0]
    block = jnp.concatenate([d_pos, d_patch, jnp.zeros((rest, width), f32)], axis=0)
    split_by(core, block, keep, send.at[:half], half)
    short[...] = put_short(send, half, short[...])
    d_shift = dot(w_patch[...], d_low, 1, 1)
    for i in range(items):
        cols = slice(i * length, (i + 1) * length)
        moved = d_shift[:, cols]
        lane = lax.broadcasted_iota(jnp.int32, moved.shape, 1)
        back = jnp.where(lane == length - 1, 0.0, pltpu.roll(moved, length - 1, 1))
        grad = part_in[:, cols] + back
        in_keep[i, done:] = jnp.where(x == 0, grad[:, :span], grad[:, span:])
        in_send[i, done:] = jnp.where(x == 0, grad[:, span:], grad[:, :span])


def put_short(send, at, short):
    n = short.shape[0]
    high = short.astype(bf16)
    low = (short - high.astype(f32)).astype(bf16)
    send[at : at + n, :] = high
    send[at + n : at + 2 * n, :] = low
    return high.astype(f32) + low.astype(f32)


def take_short(came, at, n):
    return came[at : at + n, :].astype(f32) + came[at + n : at + 2 * n, :].astype(f32)


def split_sum(bit, pairs, kept, send):
    mine = my_bit(bit)
    n = 0
    for keep, came in pairs:
        for a in range(keep.shape[0]):
            kept[n] = keep[a, mine] + came[a, mine].astype(f32)
            send[n] = (keep[a, 1 - mine] + came[a, 1 - mine].astype(f32)).astype(bf16)
            n += 1


def stage_kernel(bits, counts, *refs):
    n = 2 * sum(counts)
    ins, outs = refs[:n], refs[n:]
    for i, (bit, count) in enumerate(zip(bits, counts)):
        pairs = [(ins[2 * j], ins[2 * j + 1]) for j in range(count)]
        ins = ins[2 * count :]
        split_sum(bit, pairs, outs[2 * i], outs[2 * i + 1])


def stage(line, name, *parts, after=()):
    outs, args = [], []
    for bit, pairs in parts:
        _, _, b, w = pairs[0][0].shape
        total = sum(keep.shape[0] for keep, _ in pairs)
        outs += [((total, b, w), f32), ((total, b, w), bf16)]
        for pair in pairs:
            args += list(pair)
    bits, counts = tuple(p[0] for p in parts), tuple(len(p[1]) for p in parts)
    return line.call(partial(stage_kernel, bits, counts), outs, args, name, 1, 8, after=after)


def add_kernel(keep, came, *outs):
    at = 0
    for out in outs:
        n = out.shape[0]
        out[...] = keep[at : at + n, :] + came[at : at + n, :].astype(f32)
        at += n


def bulk0_kernel(qk, qc, ek, ec, lk, lc, short_in, keep_a, keep_b, send_a, send_b, short):
    x, _, y, _ = where()
    na, nb = keep_a.shape[0], keep_b.shape[0]
    nq, nl = qk.shape[0], lk.shape[0]
    ns = short.shape[0]
    total = short_in[...] + take_short(lc, nl, ns)
    mine, away = pl.ds(pl.multiple_of(x * na, na), na), pl.ds(pl.multiple_of((1 - x) * na, na), na)
    keep_a[...] = qk[mine, :] + qc[mine, :].astype(f32)
    send_a[...] = (qk[away, :] + qc[away, :].astype(f32)).astype(bf16)
    low = 2 * na
    parts = [
        qk[low:nq, :] + qc[low:nq, :].astype(f32),
        ek[...] + ec[...].astype(f32),
        lk[...] + lc[:nl, :].astype(f32),
    ]
    block = jnp.concatenate(parts, axis=0)
    split_by(y, block, keep_b, send_b.at[:nb], nb)
    short[...] = put_short(send_b, nb, total)


def bulk1_kernel(ka, ca, kb, cb, short_in, keep_a, keep_b, send_a, send_b, short):
    x, _, y, _ = where()
    na, nb = keep_a.shape[0], keep_b.shape[0]
    ns = short.shape[0]
    total = short_in[...] + take_short(cb, 2 * nb, ns)
    for bit, n, k, c, keep, send in ((y, na, ka, ca, keep_a, send_a), (x, nb, kb, cb, keep_b, send_b)):
        mine, away = pl.ds(pl.multiple_of(bit * n, n), n), pl.ds(pl.multiple_of((1 - bit) * n, n), n)
        keep[...] = k[mine, :] + c[mine, :].astype(f32)
        send[:n, :] = (k[away, :] + c[away, :].astype(f32)).astype(bf16)
    short[...] = put_short(send_b, nb, total)


def bulk2_kernel(ka, ca, kb, cb, short_in, keep, send1, send2, send3, short):
    _, _, _, z = where()
    na, nb = ka.shape[0] // 4, kb.shape[0] // 4
    ns = short.shape[0]
    total = short_in[...] + take_short(cb, 4 * nb, ns)
    for m, out in enumerate((keep, send1, send2, send3)):
        at = z ^ m
        ra = pl.ds(pl.multiple_of(at * na, na), na)
        rb = pl.ds(pl.multiple_of(at * nb, nb), nb)
        out[:na, :] = (ka[ra, :] + ca[ra, :].astype(f32)).astype(out.dtype)
        out[na : na + nb, :] = (kb[rb, :] + cb[rb, :].astype(f32)).astype(out.dtype)
        if m:
            short[...] = put_short(out, na + nb, total)


def bulk3_kernel(keep, c1, c2, c3, short_in, extra, piece, short):
    n = keep.shape[0]
    ns = short.shape[0]
    total = keep[...]
    for c in (c1, c2, c3):
        total = total + c[:n, :].astype(f32)
    piece[:n, :] = total.astype(bf16)
    piece[n:, :] = extra[...]
    short[...] = (short_in[...] + take_short(c1, n, ns)) + (take_short(c2, n, ns) + take_short(c3, n, ns))


def join0_kernel(own, c1, c2, c3, part_a, part_b):
    _, _, _, z = where()
    na, nb = part_a.shape[0] // 4, part_b.shape[0] // 4
    for m, c in enumerate((own, c1, c2, c3)):
        at = z ^ m
        part_a[pl.ds(pl.multiple_of(at * na, na), na), :] = c[:na, :]
        part_b[pl.ds(pl.multiple_of(at * nb, nb), nb), :] = c[na:, :]


def join1_kernel(own_a, came_a, own_b, came_b, part_a, part_b):
    x, _, y, _ = where()
    n = own_a.shape[0]
    for bit, own, came, part in ((y, own_a, came_a, part_a), (x, own_b, came_b, part_b)):
        part[pl.ds(pl.multiple_of(bit * n, n), n), :] = own[...]
        part[pl.ds(pl.multiple_of((1 - bit) * n, n), n), :] = came[...]


def write_kernel(geo, first, jobs, *refs):
    n_out = 5
    quarters = refs[: len(jobs)]
    refs = refs[len(jobs) :]
    if not first:
        refs = refs[n_out:]
    g_qkv, g_out, g_pos, g_head, g_patch, wide, sems = refs
    x, core, y, _ = where()
    width = g_out.shape[0]
    half_q, half_e, half_l = geo["half_q"], geo["half_e"], geo["half_l"]
    nb, ne = geo["nb"], geo["extra"]
    feat = g_patch.shape[0]
    at, sem = 0, 0
    waits = []

    def copy(rows, target):
        nonlocal sem
        c = pltpu.make_async_copy(wide.at[rows], target, sems.at[sem])
        sem += 1
        return c

    for quarter, (part, other_core, other_half) in zip(quarters, jobs):
        c = 1 - core if other_core else core
        n = quarter.shape[0]
        if part == "a":
            h = 1 - x if other_half else x
            wide[at : at + n, :] = quarter[...].astype(f32)
            for k in range(0, n, 128):
                q = c * half_q + h * n + k
                third, row = q // width, q % width
                target = g_qkv.at[
                    pl.ds(pl.multiple_of(row, 128), 128),
                    pl.ds(pl.multiple_of(third * width, 128), width),
                ]
                waits.append((None, copy(slice(at + k, at + k + 128), target)))
                waits[-1][1].start()
            at += n
        else:
            h = 1 - y if other_half else y
            for k in range(n // (nb + ne)):
                wide[at + k * nb : at + (k + 1) * nb, :] = quarter[
                    k * (nb + ne) : k * (nb + ne) + nb, :
                ].astype(f32)
            left = half_q - 2 * geo["na"]
            rows = n // (nb + ne) * nb
            for case_c in range(2):
                for case_h in range(2):
                    spans = []
                    if case_h == 0:
                        spans.append((0, left, "q", case_c * half_q + 2 * geo["na"]))
                        spans.append((left, rows - left, "e", case_c * half_e))
                    else:
                        spans.append((0, half_e - (rows - left), "e", case_c * half_e + rows - left))
                        spans.append((half_e - (rows - left), half_l, "l", case_c * half_l))
                    moves = []
                    for start, size, kind, place in spans:
                        pieces = {
                            "q": [(case_c * half_q + 2 * geo["na"], left, g_qkv)],
                            "e": [(0, width, g_out), (width, 2 * feat, g_head)],
                            "l": [(0, g_pos.shape[0], g_pos), (g_pos.shape[0], feat, g_patch)],
                        }[kind]
                        for low, long, ref in pieces:
                            a, b = max(place, low), min(place + size, low + long)
                            if a >= b:
                                continue
                            source = slice(at + start + a - place, at + start + b - place)
                            if kind == "q":
                                third, row = a // width, a % width
                                target = g_qkv.at[row : row + b - a, third * width : (third + 1) * width]
                            else:
                                target = ref.at[a - low : b - low]
                            moves.append(copy(source, target))
                    taken = (c == case_c) & (h == case_h)

                    @pl.when(taken)
                    def _(moves=moves):
                        for move in moves:
                            move.start()

                    waits += [(taken, move) for move in moves]
            at += rows
    for taken, move in waits:
        if taken is None:
            move.wait()
        else:
            pl.when(taken)(move.wait)


def class_kernel(geo, q0, q1, q2, q3, class_own, scalars, facts):
    x, core, y, _ = where()
    nb, ne, items = geo["nb"], geo["extra"], geo["items"]
    rows = class_own.shape[0]
    me = lax.axis_index("dp") * 2 + x
    want = (me * rows + lax.broadcasted_iota(jnp.int32, (rows, 1), 0)).astype(f32)
    total = jnp.zeros(class_own.shape, f32)
    for q, c, h in ((q0, core, y), (q1, core, 1 - y), (q2, 1 - core, y), (q3, 1 - core, 1 - y)):
        for k in range(8):
            block = q[k * (nb + ne) + nb : (k + 1) * (nb + ne), :].astype(f32)
            fact = block[items : items + 1]
            facts[pl.ds((c * 2 + h) * 8 + k, 1), :] = fact
            for i in range(items):
                slot = fact[:, 9 + i : 10 + i] * 32 + fact[:, 9 + items + i : 10 + items + i]
                total = total + jnp.where(want == slot, 1.0, 0.0) * block[i : i + 1]
    class_own[...] = total
    every = facts[...]
    summed = col_sum(every)
    scale_sum = summed[:, 0:1] + summed[:, 1:2] + summed[:, 2:3]
    count = summed[:, 3:4] + summed[:, 4:5] + summed[:, 5:6]
    tops = every[:, 6:7] + every[:, 7:8] + every[:, 8:9]
    lane = lax.broadcasted_iota(jnp.int32, scalars.shape, 1)
    scalars[...] = jnp.where(lane == 0, scale_sum / count, jnp.max(tops, axis=0, keepdims=True))


class Cube:
    def __init__(self):
        self.size = lax.axis_size("dp") * lax.axis_size("seq")
        self.nbits = self.size.bit_length() - 1
        self.me = lax.axis_index("dp") * lax.axis_size("seq") + lax.axis_index("seq")
        self.bit = [(self.me >> k) & 1 for k in range(self.nbits)]

    def send(self, block, mask):
        return lax.ppermute(block, AXES, [(i, i ^ mask) for i in range(self.size)])

    def start(self, full, bits):
        rows = full.shape[0] >> len(bits)
        return full.reshape((2,) * len(bits) + (rows, full.shape[1])), list(bits)

    def scatter(self, block, left):
        for bit in list(left):
            axis = left.index(bit)
            mine = lax.dynamic_index_in_dim(block, self.bit[bit], axis, keepdims=False)
            away = lax.dynamic_index_in_dim(block, 1 - self.bit[bit], axis, keepdims=False)
            block = mine + self.send(away.astype(bf16), 1 << bit).astype(f32)
            left = [b for b in left if b != bit]
        return block

    def add_up(self, block, bits):
        for k in bits:
            block = block + self.send(block, 1 << k)
        return block

    def gather(self, block, bits):
        for k in reversed(bits):
            came = self.send(block, 1 << k)
            block = jnp.where(self.bit[k] == 0, jnp.stack([block, came]), jnp.stack([came, block]))
        return block


def local(
    patches, labels, valid_mask, class_slot, w_patch, b_patch, pos_embed, class_embed,
    norm1_gain, norm1_shift, w_qkv, w_out, norm2_gain, norm2_shift, w_fc1, b_fc1, w_fc2, b_fc2,
    final_gain, final_shift, w_head, b_head, cot_latent, cot_logdet,
):
    cube = Cube()
    line = Line()
    seq_n = lax.axis_size("seq")
    assert seq_n == 2
    seq = lax.axis_index("seq")
    held, span, feat = patches.shape
    items = held // seq_n
    length = span * seq_n
    width = w_out.shape[0]
    ff = w_fc1.shape[1]
    rows = items * length
    classes = class_embed.shape[0]
    chunk = ff // cube.size
    group = 2 * chunk
    fast = cube.size == 32

    runs = patches.transpose(0, 2, 1)
    cot_runs = cot_latent.transpose(0, 2, 1)
    valid_runs = valid_mask[:, None, :]
    w_head_t = w_head.T
    (packed,) = line.call(
        prep_kernel, [((items, 2 * feat + 8, span), f32)], [runs, cot_runs, valid_mask], "prep", 1, 1,
        places={0: HBM, 1: HBM, 2: HBM},
        scratch=[pltpu.VMEM((items, feat, span), bf16), pltpu.VMEM((held, span), jnp.int32),
                 pltpu.SemaphoreType.DMA((3,))],
    )
    came = cube.send(packed, 1)
    big = 2.0 * rows * width * ff
    vector = pltpu.VMEM((width,), bf16)
    hidden0, normed1, qkv, shifted_t, attended, lse, w_qkv, w_out, w_fc1, w_fc2 = line.call(
        front_kernel,
        [((rows, width), f32), ((rows, width), bf16), ((rows, 3 * width), bf16), ((feat, rows), bf16),
         ((rows, width), bf16), ((items, HEADS, length), f32)]
        + [(w.shape, bf16) for w in (w_qkv, w_out, w_fc1, w_fc2)],
        [labels, came, runs, class_embed, b_patch, norm1_gain, norm1_shift, pos_embed, w_patch, w_qkv, w_out,
         w_fc1, w_fc2],
        "front", 1, 6, places={0: SMEM} | {i: HBM for i in range(2, 13)},
        scratch=[pltpu.VMEM((items, 16, width), bf16), pltpu.VMEM((items, feat, span), bf16), vector, vector,
                 vector, pltpu.VMEM((length, width), bf16), pltpu.VMEM((feat, width), bf16),
                 pltpu.SemaphoreType.DMA((items + 10,))],
    )
    n_short = 16
    (hidden1, normed2, act, slope, d_hidden2, part_in, lat_keep, lat_send, short, grad_head_t, facts) = line.call(
        middle_kernel,
        [((rows, width), f32), ((rows, width), bf16), ((rows, ff), bf16), ((rows, ff), bf16),
         ((rows, width), f32), ((feat, rows), f32), ((items, feat + 8, span), f32),
         ((items, feat + 8, span), f32), ((n_short, width), f32), ((2 * feat, width), f32),
         ((1, width), f32)],
        [cot_logdet, labels, class_slot, hidden0, attended, w_out, norm2_gain, norm2_shift, w_fc1, b_fc1,
         w_fc2, b_fc2, final_gain, final_shift, w_head_t, b_head, runs, cot_runs, valid_runs, came],
        "middle", 1, 8, places={0: SMEM, 1: SMEM, 2: SMEM},
    )
    groups = ff // (4 * group)
    pieces = [((groups, group, width), f32), ((groups, group, width), bf16)]

    def fc2_half(h):
        return line.call(partial(fc2_kernel, h), pieces, [act, d_hidden2], "fc2", 1, 4)

    def fc1_half(h, before):
        return line.call(
            partial(fc1_kernel, h),
            pieces + [((rows, width), f32), ((ff // width // 2, width), f32)],
            [d_hidden2, w_fc2, slope, normed2, w_fc1] + before, "fc1", 1, 6,
        )

    def four(block):
        return block.reshape(groups, 2, chunk, width)

    half_e, half_l, half_q = 448, 192, 3 * width // 2
    keep20, send20 = fc2_half(0)
    came20 = cube.send(send20, 2)
    keep21, send21 = fc2_half(1)
    came21 = cube.send(send21, 2)
    keep10, send10, total, bias0 = fc1_half(0, [])
    came10 = cube.send(send10, 2)
    if fast:
        k20, s20 = stage(line, "fc2_core", (0, [(four(keep20), four(came20))]))
        c20 = cube.send(s20, 1)
    keep11, send11, total, bias1 = fc1_half(1, [total])
    came11 = cube.send(send11, 2)
    if fast:
        k21, s21 = stage(line, "fc2_core", (0, [(four(keep21), four(came21))]))
    d_hidden1, short, ekeep, esend, d_attended = line.call(
        back_kernel,
        [((rows, width), f32), ((n_short, width), f32), ((half_e, width), f32), ((half_e, width), bf16),
         ((rows, width), bf16)],
        [d_hidden2, total, hidden1, norm2_gain, attended, w_out, short, bias0, bias1, grad_head_t],
        "back", 1, 6,
    )
    ecame = cube.send(esend, 2)

    def by_y(block):
        return block.reshape(2, 2, group, width)

    if fast:
        k10, s10 = stage(line, "fc1_core", (2, [(by_y(keep10), by_y(came10))]))
        c10 = cube.send(s10, 4)
        k11, s11 = stage(line, "fc1_core", (2, [(by_y(keep11), by_y(came11))]))
    (d_qkv,) = line.call(
        attention_back_kernel, [((rows, 3 * width), bf16)], [qkv, lse, d_attended],
        "attention_back", 1, 4,
    )
    qkeep, qsend = line.call(
        qkv_kernel, [((half_q, width), f32), ((half_q, width), bf16)], [normed1, d_qkv],
        "qkv_grad", 1, 6, after=[c20] if fast else [],
    )
    qcame = cube.send(qsend, 2)
    lkeep, lsend, short, back_keep, back_send, extra = line.call(
        rest_kernel,
        [((half_l, width), f32), ((half_l + 2 * n_short, width), bf16), ((n_short, width), f32),
         ((items, 2 * feat + 8, span), f32), ((items, 2 * feat + 8, span), f32), ((16, width), bf16)],
        [d_qkv, w_qkv, hidden0, d_hidden1, norm1_gain, shifted_t, w_patch, part_in, short, facts,
         lat_keep, lat_send],
        "rest", 3e10, 6, after=[c10] if fast else [],
    )
    lcame = cube.send(lsend, 2)

    if fast:
        ns2 = 2 * n_short

        def two(na, nb):
            return [((na, width), f32), ((nb, width), f32), ((na, width), bf16), ((nb + ns2, width), bf16),
                    ((n_short, width), f32)]

        ka, kb, sa, sb, short = line.call(
            bulk0_kernel, two(512, 384), [qkeep, qcame, ekeep, ecame, lkeep, lcame, short], "bulk0", 1, 10,
        )
        ca, cb = cube.send(sa, 1), cube.send(sb, 4)
        back_came = cube.send(back_send, 1)
        ka, kb, sa, sb, short = line.call(
            bulk1_kernel, two(256, 192), [ka, ca, kb, cb, short], "bulk1", 1, 6, after=[back_came]
        )
        ca, cb = cube.send(sa, 4), cube.send(sb, 1)
        na, nb, ne = 64, 48, 16
        n = na + nb
        keep, z1, z2, z3, short = line.call(
            bulk2_kernel,
            [((n, width), f32)] + [((n + ns2, width), bf16)] * 3 + [((n_short, width), f32)],
            [ka, ca, kb, cb, short], "bulk2", 1, 4,
        )
        z1, z2, z3 = cube.send(z1, 8), cube.send(z2, 16), cube.send(z3, 24)
        c21, c11 = cube.send(tie(s21, keep), 1), cube.send(tie(s11, keep), 4)
        piece, short = line.call(
            bulk3_kernel, [((n + ne, width), bf16), ((n_short, width), f32)],
            [keep, z1, z2, z3, short, extra], "bulk3", 1, 4, after=[c21, c11],
        )
        g1, g2, g3 = cube.send(piece, 8), cube.send(piece, 16), cube.send(piece, 24)
        def next_y(block):
            return block.reshape(2, 2, chunk, width)

        k2, s2, k1, s1 = stage(
            line, "fc_second",
            (2, [(next_y(k20), next_y(c20)), (next_y(k21), next_y(c21))]),
            (0, [(next_y(k10), next_y(c10)), (next_y(k11), next_y(c11))]),
        )
        c2, c1 = cube.send(s2, 4), cube.send(s1, 1)
        kf, sf = stage(
            line, "fc_third", (3, [(next_y(k2), next_y(c2)), (next_y(k1), next_y(c1))])
        )

        part_a, part_b = line.call(
            join0_kernel, [((4 * na, width), bf16), ((4 * (nb + ne), width), bf16)],
            [piece, g1, g2, g3], "join0", 1, 4,
        )
        ca, cb = cube.send(part_a, 4), cube.send(part_b, 1)
        cf = cube.send(tie(sf, g1, g2, g3), 8)
        part_a, part_b = line.call(
            join1_kernel, [((8 * na, width), bf16), ((8 * (nb + ne), width), bf16)],
            [part_a, ca, part_b, cb], "join1", 1, 5,
        )
        ca, cb = cube.send(part_a, 1), cube.send(part_b, 4)
        xa, xb = cube.send(part_a, 2), cube.send(part_b, 2)
        geo = dict(na=8 * na, nb=nb, extra=ne, half_q=half_q, half_e=half_e, half_l=half_l, items=items)
        grads = write(line, geo, [("a", 0, 0), ("b", 0, 0)], [part_a, part_b], None, width, length, feat)

        kf, sf = stage(line, "fc_fourth", (4, [(next_y(kf), next_y(cf))]))
        cf = cube.send(sf, 16)
        ya, yb = cube.send(ca, 2), cube.send(cb, 2)
        grads = write(
            line, geo, [("a", 1, 0), ("b", 1, 0), ("a", 0, 1), ("b", 0, 1)], [xa, xb, ca, cb], grads,
            width, length, feat,
        )
        own_fc2, own_fc1 = line.call(
            add_kernel, [((chunk, width), f32)] * 2,
            [kf.reshape(2 * chunk, width), cf.reshape(2 * chunk, width)], "fc_last", 1, 3,
        )
        grads = write(line, geo, [("a", 1, 1), ("b", 1, 1)], [ya, yb], grads, width, length, feat)
        g_qkv, g_out, g_pos, g_head_t, g_patch = grads
        class_own, scalars = line.call(
            partial(class_kernel, geo), [((classes // cube.size, width), f32), ((1, 128), f32)],
            [part_b, cb, xb, yb], "classes", 1, 5, scratch=[pltpu.VMEM((cube.size, width), f32)],
        )
        mean, top = scalars[0, 0], scalars[0, 1]
    else:
        rest = [0] + list(range(2, cube.nbits))
        upper = list(range(cube.nbits - 1, 1, -1)) + [0]
        back_came = cube.send(back_send, 1)

        def owned(*parts):
            total = jnp.concatenate([k + c.astype(f32) for k, c in parts]).reshape(-1, width)
            return cube.scatter(*cube.start(total, upper))

        own_fc2 = owned((keep20, came20), (keep21, came21))
        own_fc1 = owned((keep10, came10), (keep11, came11))
        full = jnp.concatenate(
            [qkeep + qcame.astype(f32), ekeep + ecame.astype(f32), lkeep + lcame[:half_l].astype(f32)]
        )
        n_full = full.shape[0]
        full = jnp.pad(full, ((0, -n_full % (cube.size * 8)), (0, 0)))
        own = cube.scatter(*cube.start(full, upper))
        n_own = own.shape[0]
        got = cube.gather(jnp.concatenate([own.astype(bf16), extra]), [1] + upper)
        halves = got[..., :n_own, :].reshape(2, -1, width)[:, :n_full].astype(f32)
        short = cube.add_up(short, [1] + rest)
        q = halves[:, :half_q].reshape(3, width, width)
        g_qkv = jnp.concatenate([q[0], q[1], q[2]], axis=1)
        e = halves[:, half_q : half_q + half_e].reshape(-1, width)
        g_out, g_head_t = e[:width], e[width : width + 2 * feat]
        later = halves[:, half_q + half_e :].reshape(-1, width)
        g_pos, g_patch = later[:length], later[length : length + feat]
        extras = got[..., n_own : n_own + items + 1, :].reshape(cube.size, items + 1, width).astype(f32)
        sums = extras[:, :items].reshape(-1, width)
        facts = extras[:, items]
        mean = jnp.sum(facts[:, :3]) / jnp.sum(facts[:, 3:6])
        top = jnp.max(facts[:, 6] + facts[:, 7] + facts[:, 8])
        all_slots = (facts[:, 9 : 9 + items] * 32 + facts[:, 9 + items : 9 + 2 * items]).reshape(-1)
        own_rows = classes // cube.size
        wanted = (cube.me * own_rows + jnp.arange(own_rows)).astype(f32)
        hot = (wanted[:, None] == all_slots[None, :]).astype(bf16)
        class_own = dot(hot, sums.astype(bf16))

    out = jnp.where(
        seq == 0, jnp.concatenate([back_keep, back_came]), jnp.concatenate([back_came, back_keep])
    )
    latent_out = out[:, :feat].transpose(0, 2, 1)
    logdet_out = out[:, feat, 0]
    grad_in_out = out[:, feat + 8 :].transpose(0, 2, 1)
    b1_all = short[ROW["b1"] : ROW["b1"] + ff // width].reshape(-1)
    b1_own = lax.dynamic_slice_in_dim(b1_all, cube.me * chunk, chunk, 0)
    vec = {name: short[at] for name, at in ROW.items()}
    return (
        latent_out, logdet_out, grad_in_out, g_patch, vec["bp"], g_pos, class_own,
        vec["n1g"], vec["n1s"], g_qkv, g_out, vec["n2g"], vec["n2s"], own_fc1.T, b1_own, own_fc2,
        vec["b2"], vec["fg"], vec["fs"], g_head_t.T, vec["bh"][: 2 * feat], mean, top,
    )


def write(line, geo, jobs, quarters, grads, width, length, feat):
    shapes = [(width, 3 * width), (width, width), (length, width), (2 * feat, width), (feat, width)]
    n = len(quarters)
    args = list(quarters)
    args[0] = tie(args[0], line.last)
    aliases = {}
    if grads is not None:
        aliases = {n + i: i for i in range(len(shapes))}
        args += list(grads)
    grads = pl.pallas_call(
        partial(write_kernel, geo, grads is None, jobs),
        out_shape=[jax.ShapeDtypeStruct(s, f32) for s in shapes],
        in_specs=[pl.BlockSpec(memory_space=VMEM)] * n + [pl.BlockSpec(memory_space=ANY)] * len(aliases),
        out_specs=[pl.BlockSpec(memory_space=ANY)] * len(shapes),
        scratch_shapes=[pltpu.VMEM((512 * n, width), f32), pltpu.SemaphoreType.DMA((16 * n,))],
        input_output_aliases=aliases,
        compiler_params=pltpu.CompilerParams(vmem_limit_bytes=(2 * n + 4) * 2**20),
        cost_estimate=pl.CostEstimate(flops=10**10, bytes_accessed=1, transcendentals=0),
        name="write",
    )(*args)
    line.last = grads[-1]
    return grads


def solution(mesh):
    run, item, whole = P("dp", "seq", None), P("dp"), P()
    placed = (run, item, P("dp", "seq")) + (whole,) * 19 + (run, item)
    owned = P(AXES)
    return jax.shard_map(
        local,
        mesh=mesh,
        in_specs=placed,
        out_specs=(run, item, run, whole, whole, whole, P(AXES, None), whole, whole, whole, whole,
                   whole, whole, P(None, AXES), owned, P(AXES, None)) + (whole,) * 7,
        check_vma=False,
    )
```

time: 261 us -> 194 us (0.74)
  local copies, waits for them, and re-layouts: 40.8 us -> 12.3 us
  waiting for transfers between devices: 95.4 us -> 71.7 us
  between operations: 7.99 us -> 1.59 us
  other arithmetic: 3.88 us -> 1.07 us
  Pallas kernels: 69.9 us -> 67.1 us
    ppermute x31 -> x35, waiting for transfers between devices: 95.4 us -> 71.7 us  [send(): return lax.ppermute(block, AXES, [(i, i ^ mask) for i in range(self.size)])]
    unnamed x72 -> x52, local copies, waits for them, and re-layouts: 23.8 us -> 6.17 us
    broadcast_in_dim x10 -> x0, local copies, waits for them, and re-layouts: 5.59 us -> none  [the longest x8 5.48 us: local(): v[None]]
    dynamic_slice x4 -> x0, local copies, waits for them, and re-layouts: 4.21 us -> none  [the longest x1 1.36 us: local(): lax.dynamic_index_in_dim(class_slot, at, 0, keepdims=False)]
    pallas_call x20 -> x29, Pallas kernels: 69.9 us -> 67.1 us  [the longest x26 60.3 us: call(): pl.pallas_call(body, out_shape=[jax.ShapeDtypeStruct(s, d) for s, d in ou...]
    ppermute x31 -> x35, starting transfers between devices: 37.4 us -> 36.1 us  [send(): return lax.ppermute(block, AXES, [(i, i ^ mask) for i in range(self.size)])]
  transfers between devices with their start and end apart: 31 -> 35, of which waited for: 12 -> 18; matrix products, arithmetic and copies ran while one was open for 7% -> 3% of each run, Pallas kernels for 14% -> 18%
where the time goes in v3:
time: 194 us; the launch traced here: 190 us
  waiting for transfers between devices  71.7 us (37%)
  Pallas kernels  67.1 us (35%)
  starting transfers between devices  36.1 us (19%)
  local copies, waits for them, and re-layouts  12.3 us (6%)
    ppermute x35, waiting for transfers between devices, send(): return lax.ppermute(block, AXES, [(i, i ^ mask) for i in range(self.size)])  71.7 us
    pallas_call x26, Pallas kernels, call(): pl.pallas_call(body, out_shape=[jax.ShapeDtypeStruct(s, d) for s, d in ou...  60.3 us
    ppermute x35, starting transfers between devices, send(): return lax.ppermute(block, AXES, [(i, i ^ mask) for i in range(self.size)])  36.1 us
    pallas_call x3, Pallas kernels, write(): pl.pallas_call(partial(write_kernel, geo, grads is None, jobs), out_shape...  6.79 us
    unnamed x52, local copies, waits for them, and re-layouts  6.17 us
  transfers between devices with their start and end apart: 35, of which 18 were waited for; matrix products, arithmetic and copies ran while one was open for 3% of the time, Pallas kernels for 18%

profile of v3, /device:TPU:0, one launch (start us, length us, event | category | flops | bytes accessed | tf_op | source)
XLA Modules:
  0.0 189.9 jit_solution(15127807757004381294)
XLA Ops:
  1.7 3.0 %collective-permute-start = (f32[2,104,128]{2,1,0:T(8,128)S(1)}, f32[2,104,128]{2,1,0:T(8,128)S(1)}, u32[]{:S(2)}, u32[]{:S(2)}) collective-permute-start(f32[2,104,128]{2,1,0:T(8,128)S(1)} %prep.1), channel_id=1, source_target_pairs={{0,1},{1,0},{2,3},{3,2},{4,5},{5,4},{6,7},{7,6},{8,9},{9,8},{10,11... | collective-permute-start | bytes 319496 | tf_op jit(solution)/shard_map/ppermute | solution.py:707
  4.7 3.0 %collective-permute-done.came = f32[2,104,128]{2,1,0:T(8,128)S(1)} collective-permute-done((f32[2,104,128]{2,1,0:T(8,128)S(1)}, f32[2,104,128]{2,1,0:T(8,128)S(1)}, u32[]{:S(2)}, u32[]{:S(2)}) %collective-permute-start) | collective-permute-done | bytes 106528 | tf_op jit(solution)/shard_map/ppermute | solution.py:707
  8.3 14.0 %front.1 = (f32[512,768]{1,0:T(8,128)S(1)}, bf16[512,768]{1,0:T(8,128)(2,1)S(1)}, bf16[512,2304]{1,0:T(8,128)(2,1)S(1)}, bf16[48,512]{1,0:T(8,128)(2,1)S(1)}, bf...) custom-call(s32[4]{0:T(128)S(1)} %copy-done.21, ...), custom_call_target="tpu_custom_call" | custom-call | flops 1 | bytes 1 | tf_op jit(solution)/shard_map/front/pallas_call | solution.py:45
  22.5 10.9 %middle.1 = (f32[512,768]{1,0:T(8,128)S(1)}, bf16[512,768]{1,0:T(8,128)(2,1)S(1)}, bf16[512,3072]{1,0:T(8,128)(2,1)S(1)}, bf16[512,3072]{1,0:T(8,128)(2,1)S(1)},...) custom-call(f32[4]{0:T(128)S(1)} %copy-done.22, ...), custom_call_target="tpu_custom_call" | custom-call | flops 1 | bytes 1 | tf_op jit(solution)/shard_map/middle/pallas_call | solution.py:45
  33.4 1.4 fc2.2
  34.9 1.4 fc2.3
  36.9 4.6 %fc1.2 = (f32[4,192,768]{2,1,0:T(8,128)S(1)}, bf16[4,192,768]{2,1,0:T(8,128)(2,1)S(1)}, f32[512,768]{1,0:T(8,128)S(1)}, f32[2,768]{1,0:T(2,128)S(1)}) custom-call(f32[512,768]{1,0:T(8,128)S(1)} %get-tuple-element.172.d_hidden2, bf16[3072,768]{1,0:T(8,128)(2,1)S(1)} %get-tuple-element.163.w_fc2, bf16[512,3072]{1,0:T(8,128)(2,1)S(1)} %get-tuple-element.166.slope, ...), custom_call_target="tpu_custom_call" | custom-call | flops 1 | bytes 1 | tf_op jit(solution)/shard_map/fc1/pallas_call | solution.py:45
  41.8 4.0 %fc1.3 = (f32[4,192,768]{2,1,0:T(8,128)S(1)}, bf16[4,192,768]{2,1,0:T(8,128)(2,1)S(1)}, f32[512,768]{1,0:T(8,128)S(1)}, f32[2,768]{1,0:T(2,128)S(1)}) custom-call(f32[512,768]{1,0:T(8,128)S(1)} %get-tuple-element.172.d_hidden2, bf16[3072,768]{1,0:T(8,128)(2,1)S(1)} %get-tuple-element.163.w_fc2, bf16[512,3072]{1,0:T(8,128)(2,1)S(1)} %get-tuple-element.166.slope, ...), custom_call_target="tpu_custom_call" | custom-call | flops 1 | bytes 1 | tf_op jit(solution)/shard_map/fc1/pallas_call | solution.py:45
  46.5 1.8 collective-permute-start.6
  48.4 2.3 %back.1 = (f32[512,768]{1,0:T(8,128)S(1)}, f32[16,768]{1,0:T(8,128)S(1)}, f32[448,768]{1,0:T(8,128)S(1)}, bf16[448,768]{1,0:T(8,128)(2,1)S(1)}, bf16[512,768]{1,0:T(8,128)(2,1)S(1)}) custom-call(f32[512,768]{1,0:T(8,128)S(1)} %get-tuple-element.172.d_hidden2, f32[512,768]{1,0:T(8,128)S(1)} %get-tuple-element.181.total_in, ...), custom_call_target="tpu_custom_call" | custom-call | flops 1 | bytes 1 | tf_op jit(solution)/shard_map/back/pallas_call | solution.py:45
  50.9 1.6 collective-permute-start.5
  52.7 7.6 %attention_back.1.d_qkv = bf16[512,2304]{1,0:T(8,128)(2,1)S(1)} custom-call(bf16[512,2304]{1,0:T(8,128)(2,1)S(1)} %get-tuple-element.157.qkv, f32[2,12,256]{2,1,0:T(8,128)S(1)} %get-tuple-element.158.lse, bf16[512,768]{1,0:T(8,128)(2,1)S(1)} %get-tuple-element.199.d_attended), custom_call_target="tpu_custom_call" | custom-call | flops 1 | bytes 1 | tf_op jit(solution)/shard_map/attention_back/pallas_call | solution.py:45
  60.3 1.6 collective-permute-done.6
  61.9 3.1 %qkv_grad.1 = (f32[1152,768]{1,0:T(8,128)S(1)}, bf16[1152,768]{1,0:T(8,128)(2,1)S(1)}) custom-call(bf16[512,768]{1,0:T(8,128)(2,1)S(1)} %get-tuple-element.208.normed1, bf16[512,2304]{1,0:T(8,128)(2,1)S(1)} %attention_back.1.d_qkv), custom_call_target="tpu_custom_call" | custom-call | flops 1 | bytes 1 | tf_op jit(solution)/shard_map/qkv_grad/pallas_call | solution.py:45
  66.0 3.6 %rest.1 = (f32[192,768]{1,0:T(8,128)S(1)}, bf16[224,768]{1,0:T(8,128)(2,1)S(1)}, f32[16,768]{1,0:T(8,128)S(1)}, f32[2,104,128]{2,1,0:T(8,128)S(1)}, f32[2,104,12...) custom-call(bf16[512,2304]{1,0:T(8,128)(2,1)S(1)} %attention_back.1.d_qkv, bf16[768,2304]{1,0:T(8,128)(2,1)S(1)} %get-tuple-element.200.w_qkv, ...), custom_call_target="tpu_custom_call" | custom-call | flops 30000001024 | bytes 1 | tf_op jit(solution)/shard_map/rest/pallas_call | solution.py:45
  70.7 1.3 collective-permute-done.10.lc
  73.5 1.5 collective-permute-start.12
  75.0 1.2 collective-permute-start.7
  76.2 18.5 %collective-permute-done.7 = f32[2,104,128]{2,1,0:T(8,128)S(1)} collective-permute-done((f32[2,104,128]{2,1,0:T(8,128)S(1)}, f32[2,104,128]{2,1,0:T(8,128)S(1)}, u32[]{:S(2)}, u32[]{:S(2)}) %collective-permute-start.7) | collective-permute-done | bytes 106528 | tf_op jit(solution)/shard_map/ppermute | solution.py:707
  95.4 1.5 collective-permute-start.13
  97.7 8.4 %collective-permute-done.14.cb = bf16[224,768]{1,0:T(8,128)(2,1)S(1)} collective-permute-done((bf16[224,768]{1,0:T(8,128)(2,1)S(1)}, bf16[224,768]{1,0:T(8,128)(2,1)S(1)}, u32[]{:S(2)}, u32[]{:S(2)}) %collective-permute-start.14) | collective-permute-done | bytes 344096 | tf_op jit(solution)/shard_map/ppermute | solution.py:707
  106.3 1.4 collective-permute-start.19
  108.5 1.6 collective-permute-start.15
  110.1 2.6 %collective-permute-start.16 = (bf16[144,768]{1,0:T(8,128)(2,1)S(1)}, bf16[144,768]{1,0:T(8,128)(2,1)S(1)}, u32[]{:S(2)}, u32[]{:S(2)}) collective-permute-start(bf16[144,768]{1,0:T(8,128)(2,1)S(1)} %get-tuple-element.236), channel_id=1, source_target_pairs={{0,16},{1,17},{2,18},{3,19},{4,20},{5,21},{6,22},{7,23},{8,24},{9,... | collective-permute-start | bytes 663560 | tf_op jit(solution)/shard_map/ppermute | solution.py:707
  112.9 7.1 %collective-permute-done.19 = bf16[2,192,768]{2,1,0:T(8,128)(2,1)S(1)} collective-permute-done((bf16[2,192,768]{2,1,0:T(8,128)(2,1)S(1)}, bf16[2,192,768]{2,1,0:T(8,128)(2,1)S(1)}, u32[]{:S(2)}, u32[]{:S(2)}) %collective-permute-start.19) | collective-permute-done | bytes 589856 | tf_op jit(solution)/shard_map/ppermute | solution.py:707
  120.1 1.2 collective-permute-done.18
  121.3 6.7 %collective-permute-done.16.c2 = bf16[144,768]{1,0:T(8,128)(2,1)S(1)} collective-permute-done((bf16[144,768]{1,0:T(8,128)(2,1)S(1)}, bf16[144,768]{1,0:T(8,128)(2,1)S(1)}, u32[]{:S(2)}, u32[]{:S(2)}) %collective-permute-start.16) | collective-permute-done | bytes 221216 | tf_op jit(solution)/shard_map/ppermute | solution.py:707
  128.8 1.4 fc_second.1
  130.3 1.2 collective-permute-start.24
  132.0 1.1 maximum_select_fusion
  133.0 2.0 %collective-permute-start.22 = (bf16[128,768]{1,0:T(8,128)(2,1)}, bf16[128,768]{1,0:T(8,128)(2,1)S(1)}, u32[]{:S(2)}, u32[]{:S(2)}) collective-permute-start(bf16[128,768]{1,0:T(8,128)(2,1)} %copy-done.6), channel_id=1, source_target_pairs={{0,24},{1,25},{2,26},{3,27},{4,28},{5,29},{6,30},{7,31},{8,16},{9,... | collective-permute-start | bytes 589832 | tf_op jit(solution)/shard_map/ppermute | solution.py:707
  135.1 4.2 %collective-permute-start.20 = (bf16[128,768]{1,0:T(8,128)(2,1)}, bf16[128,768]{1,0:T(8,128)(2,1)S(1)}, u32[]{:S(2)}, u32[]{:S(2)}) collective-permute-start(bf16[128,768]{1,0:T(8,128)(2,1)} %copy-done.6), channel_id=1, source_target_pairs={{0,8},{1,9},{2,10},{3,11},{4,12},{5,13},{6,14},{7,15},{8,0},{9,1},... | collective-permute-start | bytes 589832 | tf_op jit(solution)/shard_map/ppermute | solution.py:707
  142.4 1.1 copy-done.1
  143.4 1.1 copy-done.3
  144.8 6.3 %collective-permute-done.21.c2 = bf16[128,768]{1,0:T(8,128)(2,1)S(1)} collective-permute-done((bf16[128,768]{1,0:T(8,128)(2,1)}, bf16[128,768]{1,0:T(8,128)(2,1)S(1)}, u32[]{:S(2)}, u32[]{:S(2)}) %collective-permute-start.21) | collective-permute-done | bytes 196640 | tf_op jit(solution)/shard_map/ppermute | solution.py:707
  152.1 1.5 collective-permute-start.25
  155.6 1.7 slice_reduce_fusion
  157.3 1.2 slice_bitcast_fusion.2
  160.0 1.3 collective-permute-start.27
  161.5 1.5 collective-permute-start.33
  163.0 1.9 %write.3 = (f32[768,2304]{1,0:T(8,128)}, f32[768,768]{1,0:T(8,128)}, f32[256,768]{1,0:T(8,128)}, f32[96,768]{1,0:T(8,128)}, f32[48,768]{1,0:T(8,128)}) custom-call(bf16[512,768]{1,0:T(8,128)(2,1)S(1)} %get-tuple-element.260.refs_0_, bf16[512,768]{1,0:T(8,128)(2,1)S(1)} %get-tuple-element.261.refs_1_.q0), custom_call_target="tpu_custom_call" | custom-call | flops 10000000000 | bytes 1 | tf_op jit(solution)/shard_map/write/pallas_call | solution.py:995
  164.9 6.3 %collective-permute-done.29 = bf16[4,96,768]{2,1,0:T(8,128)(2,1)S(1)} collective-permute-done((bf16[4,96,768]{2,1,0:T(8,128)(2,1)}, bf16[4,96,768]{2,1,0:T(8,128)(2,1)S(1)}, u32[]{:S(2)}, u32[]{:S(2)}) %collective-permute-start.29) | collective-permute-done | bytes 589856 | tf_op jit(solution)/shard_map/ppermute | solution.py:707
  171.3 2.1 %collective-permute-start.30 = (bf16[2,96,768]{2,1,0:T(8,128)(2,1)S(1)}, bf16[2,96,768]{2,1,0:T(8,128)(2,1)S(1)}, u32[]{:S(2)}, u32[]{:S(2)}) collective-permute-start(bf16[2,96,768]{2,1,0:T(8,128)(2,1)S(1)} %get-tuple-element.265), channel_id=1, source_target_pairs={{0,16},{1,17},{2,18},{3,19},{4,20},{5,21},{6,22},{7,23},{8,24},{9,... | collective-permute-start | bytes 884744 | tf_op jit(solution)/shard_map/ppermute | solution.py:707
  173.4 6.6 %collective-permute-done.27.refs_2_ = bf16[512,768]{1,0:T(8,128)(2,1)S(1)} collective-permute-done((bf16[512,768]{1,0:T(8,128)(2,1)S(1)}, bf16[512,768]{1,0:T(8,128)(2,1)S(1)}, u32[]{:S(2)}, u32[]{:S(2)}) %collective-permute-start.27) | collective-permute-done | bytes 786464 | tf_op jit(solution)/shard_map/ppermute | solution.py:707
  180.0 1.3 collective-permute-done.33.refs_3_.q1
  181.3 3.1 %write.4 = (f32[768,2304]{1,0:T(8,128)}, f32[768,768]{1,0:T(8,128)}, f32[256,768]{1,0:T(8,128)}, f32[96,768]{1,0:T(8,128)}, f32[48,768]{1,0:T(8,128)}) custom-call(bf16[512,768]{1,0:T(8,128)(2,1)S(1)} %collective-permute-done.31.refs_0_, ...), custom_call_target="tpu_custom_call", output_to_operand_aliasing={{0}: (4, {}), {1}: (5, {}), {2}: (6, {}), {3}: (7, {}), {4}... | custom-call | flops 10000000000 | bytes 1 | tf_op jit(solution)/shard_map/write/pallas_call | solution.py:995
  185.2 1.8 write.5
  187.0 1.9 classes.1
  (112 shorter events, 20.9 us)
Async XLA Ops:
  0.7 21.7 %copy-start.22 = (f32[4]{0:T(128)S(1)}, f32[4]{0:T(128)}, u32[]{:S(2)}) copy-start(f32[4]{0:T(128)} %det.1) | copy-start | bytes 52
  0.7 21.7 %copy-start.23 = (bf16[96]{0:T(256)(128)(2,1)S(1)}, bf16[96]{0:T(256)(128)(2,1)}, u32[]{:S(2)}) copy-start(bf16[96]{0:T(256)(128)(2,1)} %b_head.1) | copy-start | bytes 580
  1.5 20.8 %copy-start.4 = (bf16[4,128,48]{1,2,0:T(8,128)(2,1)S(1)}, bf16[4,128,48]{1,2,0:T(8,128)(2,1)}, u32[]{:S(2)}) copy-start(bf16[4,128,48]{1,2,0:T(8,128)(2,1)} %param.24) | copy-start | bytes 147460
  1.6 20.8 %copy-start.5 = (f32[4,128,48]{1,2,0:T(8,128)S(1)}, f32[4,128,48]{1,2,0:T(8,128)}, u32[]{:S(2)}) copy-start(f32[4,128,48]{1,2,0:T(8,128)} %param.46) | copy-start | bytes 294916
  1.6 20.8 %copy-start.8 = (bf16[768,96]{0,1:T(8,128)(2,1)S(1)}, bf16[768,96]{0,1:T(8,128)(2,1)}, u32[]{:S(2)}) copy-start(bf16[768,96]{0,1:T(8,128)(2,1)} %param.44) | copy-start | bytes 442372
  1.6 20.8 %copy-start.12 = (s32[4,128]{1,0:T(4,128)S(1)}, s32[4,128]{1,0:T(4,128)}, u32[]{:S(2)}) copy-start(s32[4,128]{1,0:T(4,128)} %valid.1) | copy-start | bytes 6148
  1.6 20.8 %copy-start.13 = (bf16[768]{0:T(1024)(128)(2,1)S(1)}, bf16[768]{0:T(1024)(128)(2,1)}, u32[]{:S(2)}) copy-start(bf16[768]{0:T(1024)(128)(2,1)} %gain2.3) | copy-start | bytes 4612
  1.6 20.8 %copy-start.14 = (bf16[3072]{0:T(1024)(128)(2,1)S(1)}, bf16[3072]{0:T(1024)(128)(2,1)}, u32[]{:S(2)}) copy-start(bf16[3072]{0:T(1024)(128)(2,1)} %b_fc1.1) | copy-start | bytes 18436
  1.6 20.8 %copy-start.15 = (s32[1024]{0:T(1024)S(1)}, s32[1024]{0:T(1024)}, u32[]{:S(2)}) copy-start(s32[1024]{0:T(1024)} %class_slot.1) | copy-start | bytes 12292
  1.6 20.8 %copy-start.16 = (bf16[768]{0:T(1024)(128)(2,1)S(1)}, bf16[768]{0:T(1024)(128)(2,1)}, u32[]{:S(2)}) copy-start(bf16[768]{0:T(1024)(128)(2,1)} %shift2.1) | copy-start | bytes 4612
  1.6 20.8 %copy-start.17 = (bf16[768]{0:T(1024)(128)(2,1)S(1)}, bf16[768]{0:T(1024)(128)(2,1)}, u32[]{:S(2)}) copy-start(bf16[768]{0:T(1024)(128)(2,1)} %b_fc2.1) | copy-start | bytes 4612
  1.7 20.8 %copy-start.18 = (bf16[768]{0:T(1024)(128)(2,1)S(1)}, bf16[768]{0:T(1024)(128)(2,1)}, u32[]{:S(2)}) copy-start(bf16[768]{0:T(1024)(128)(2,1)} %gainf.1) | copy-start | bytes 4612
  1.7 20.8 %copy-start.19 = (bf16[768]{0:T(1024)(128)(2,1)S(1)}, bf16[768]{0:T(1024)(128)(2,1)}, u32[]{:S(2)}) copy-start(bf16[768]{0:T(1024)(128)(2,1)} %shiftf.1) | copy-start | bytes 4612
  1.7 6.0 %collective-permute-start = (f32[2,104,128]{2,1,0:T(8,128)S(1)}, f32[2,104,128]{2,1,0:T(8,128)S(1)}, u32[]{:S(2)}, u32[]{:S(2)}) collective-permute-start(f32[2,104,128]{2,1,0:T(8,128)S(1)} %prep.1), channel_id=1, source_target_pairs={{0,1},{1,0},{2,3},{3,2},{4,5},{5,4},{6,7},{7,6},{8,9},{9,8},{10,11... | collective-permute-start | bytes 319496 | tf_op jit(solution)/shard_map/ppermute | solution.py:707
  34.8 6.8 %collective-permute-start.1 = (bf16[4,192,768]{2,1,0:T(8,128)(2,1)S(1)}, bf16[4,192,768]{2,1,0:T(8,128)(2,1)S(1)}, u32[]{:S(2)}, u32[]{:S(2)}) collective-permute-start(bf16[4,192,768]{2,1,0:T(8,128)(2,1)S(1)} %get-tuple-element.176), channel_id=1, source_target_pairs={{0,2},{1,3},{2,0},{3,1},{4,6},{5,7},{6,4},{7,5},{8,10},{9,11},{10,... | collective-permute-start | bytes 3538952 | tf_op jit(solution)/shard_map/ppermute | solution.py:707
  36.4 10.0 %collective-permute-start.2 = (bf16[4,192,768]{2,1,0:T(8,128)(2,1)S(1)}, bf16[4,192,768]{2,1,0:T(8,128)(2,1)S(1)}, u32[]{:S(2)}, u32[]{:S(2)}) collective-permute-start(bf16[4,192,768]{2,1,0:T(8,128)(2,1)S(1)} %get-tuple-element.186), channel_id=1, source_target_pairs={{0,2},{1,3},{2,0},{3,1},{4,6},{5,7},{6,4},{7,5},{8,10},{9,11},{10,... | collective-permute-start | bytes 3538952 | tf_op jit(solution)/shard_map/ppermute | solution.py:707
  41.5 9.2 %collective-permute-start.4 = (bf16[4,192,768]{2,1,0:T(8,128)(2,1)S(1)}, bf16[4,192,768]{2,1,0:T(8,128)(2,1)S(1)}, u32[]{:S(2)}, u32[]{:S(2)}) collective-permute-start(bf16[4,192,768]{2,1,0:T(8,128)(2,1)S(1)} %get-tuple-element.193), channel_id=1, source_target_pairs={{0,2},{1,3},{2,0},{3,1},{4,6},{5,7},{6,4},{7,5},{8,10},{9,11},{10,... | collective-permute-start | bytes 3538952 | tf_op jit(solution)/shard_map/ppermute | solution.py:707
  45.8 6.7 %collective-permute-start.3 = (bf16[4,192,768]{2,1,0:T(8,128)(2,1)S(1)}, bf16[4,192,768]{2,1,0:T(8,128)(2,1)S(1)}, u32[]{:S(2)}, u32[]{:S(2)}) collective-permute-start(bf16[4,192,768]{2,1,0:T(8,128)(2,1)S(1)} %get-tuple-element.192), channel_id=1, source_target_pairs={{0,2},{1,3},{2,0},{3,1},{4,6},{5,7},{6,4},{7,5},{8,10},{9,11},{10,... | collective-permute-start | bytes 3538952 | tf_op jit(solution)/shard_map/ppermute | solution.py:707
  46.5 15.3 %collective-permute-start.6 = (bf16[4,96,768]{2,1,0:T(8,128)(2,1)S(1)}, bf16[4,96,768]{2,1,0:T(8,128)(2,1)S(1)}, u32[]{:S(2)}, u32[]{:S(2)}) collective-permute-start(bf16[4,96,768]{2,1,0:T(8,128)(2,1)S(1)} %get-tuple-element.209), channel_id=1, source_target_pairs={{0,1},{1,0},{2,3},{3,2},{4,5},{5,4},{6,7},{7,6},{8,9},{9,8},{10,11... | collective-permute-start | bytes 1769480 | tf_op jit(solution)/shard_map/ppermute | solution.py:707
  50.9 15.1 %collective-permute-start.5 = (bf16[2,192,768]{2,1,0:T(8,128)(2,1)S(1)}, bf16[2,192,768]{2,1,0:T(8,128)(2,1)S(1)}, u32[]{:S(2)}, u32[]{:S(2)}) collective-permute-start(bf16[2,192,768]{2,1,0:T(8,128)(2,1)S(1)} %get-tuple-element.207), channel_id=1, source_target_pairs={{0,4},{1,5},{2,6},{3,7},{4,0},{5,1},{6,2},{7,3},{8,12},{9,13},{10,... | collective-permute-start | bytes 1769480 | tf_op jit(solution)/shard_map/ppermute | solution.py:707
  52.5 18.2 %collective-permute-start.9 = (bf16[448,768]{1,0:T(8,128)(2,1)S(1)}, bf16[448,768]{1,0:T(8,128)(2,1)S(1)}, u32[]{:S(2)}, u32[]{:S(2)}) collective-permute-start(bf16[448,768]{1,0:T(8,128)(2,1)S(1)} %get-tuple-element.217), channel_id=1, source_target_pairs={{0,2},{1,3},{2,0},{3,1},{4,6},{5,7},{6,4},{7,5},{8,10},{9,11},{10,... | collective-permute-start | bytes 2064392 | tf_op jit(solution)/shard_map/ppermute | solution.py:707
  65.9 6.0 %collective-permute-start.8 = (bf16[1152,768]{1,0:T(8,128)(2,1)S(1)}, bf16[1152,768]{1,0:T(8,128)(2,1)S(1)}, u32[]{:S(2)}, u32[]{:S(2)}) collective-permute-start(bf16[1152,768]{1,0:T(8,128)(2,1)S(1)} %get-tuple-element.215), channel_id=1, source_target_pairs={{0,2},{1,3},{2,0},{3,1},{4,6},{5,7},{6,4},{7,5},{8,10},{9,11},{10,... | collective-permute-start | bytes 5308424 | tf_op jit(solution)/shard_map/ppermute | solution.py:707
  70.2 1.8 collective-permute-start.10
  72.6 22.2 %collective-permute-start.11 = (bf16[512,768]{1,0:T(8,128)(2,1)S(1)}, bf16[512,768]{1,0:T(8,128)(2,1)S(1)}, u32[]{:S(2)}, u32[]{:S(2)}) collective-permute-start(bf16[512,768]{1,0:T(8,128)(2,1)S(1)} %get-tuple-element.223), channel_id=1, source_target_pairs={{0,1},{1,0},{2,3},{3,2},{4,5},{5,4},{6,7},{7,6},{8,9},{9,8},{10,11... | collective-permute-start | bytes 2359304 | tf_op jit(solution)/shard_map/ppermute | solution.py:707
  73.5 21.3 %collective-permute-start.12 = (bf16[416,768]{1,0:T(8,128)(2,1)S(1)}, bf16[416,768]{1,0:T(8,128)(2,1)S(1)}, u32[]{:S(2)}, u32[]{:S(2)}) collective-permute-start(bf16[416,768]{1,0:T(8,128)(2,1)S(1)} %get-tuple-element.225), channel_id=1, source_target_pairs={{0,4},{1,5},{2,6},{3,7},{4,0},{5,1},{6,2},{7,3},{8,12},{9,13},{10,... | collective-permute-start | bytes 1916936 | tf_op jit(solution)/shard_map/ppermute | solution.py:707
  75.0 19.7 %collective-permute-start.7 = (f32[2,104,128]{2,1,0:T(8,128)S(1)}, f32[2,104,128]{2,1,0:T(8,128)S(1)}, u32[]{:S(2)}, u32[]{:S(2)}) collective-permute-start(f32[2,104,128]{2,1,0:T(8,128)S(1)} %get-tuple-element.214), channel_id=1, source_target_pairs={{0,1},{1,0},{2,3},{3,2},{4,5},{5,4},{6,7},{7,6},{8,9},{9,8},{10,11... | collective-permute-start | bytes 319496 | tf_op jit(solution)/shard_map/ppermute | solution.py:707
  95.4 10.8 %collective-permute-start.13 = (bf16[256,768]{1,0:T(8,128)(2,1)S(1)}, bf16[256,768]{1,0:T(8,128)(2,1)S(1)}, u32[]{:S(2)}, u32[]{:S(2)}) collective-permute-start(bf16[256,768]{1,0:T(8,128)(2,1)S(1)} %get-tuple-element.229), channel_id=1, source_target_pairs={{0,4},{1,5},{2,6},{3,7},{4,0},{5,1},{6,2},{7,3},{8,12},{9,13},{10,... | collective-permute-start | bytes 1179656 | tf_op jit(solution)/shard_map/ppermute | solution.py:707
  96.9 9.2 %collective-permute-start.14 = (bf16[224,768]{1,0:T(8,128)(2,1)S(1)}, bf16[224,768]{1,0:T(8,128)(2,1)S(1)}, u32[]{:S(2)}, u32[]{:S(2)}) collective-permute-start(bf16[224,768]{1,0:T(8,128)(2,1)S(1)} %get-tuple-element.231), channel_id=1, source_target_pairs={{0,1},{1,0},{2,3},{3,2},{4,5},{5,4},{6,7},{7,6},{8,9},{9,8},{10,11... | collective-permute-start | bytes 1032200 | tf_op jit(solution)/shard_map/ppermute | solution.py:707
  106.3 13.8 %collective-permute-start.19 = (bf16[2,192,768]{2,1,0:T(8,128)(2,1)S(1)}, bf16[2,192,768]{2,1,0:T(8,128)(2,1)S(1)}, u32[]{:S(2)}, u32[]{:S(2)}) collective-permute-start(bf16[2,192,768]{2,1,0:T(8,128)(2,1)S(1)} %get-tuple-element.243), channel_id=1, source_target_pairs={{0,4},{1,5},{2,6},{3,7},{4,0},{5,1},{6,2},{7,3},{8,12},{9,13},{10,... | collective-permute-start | bytes 1769480 | tf_op jit(solution)/shard_map/ppermute | solution.py:707
  107.7 13.6 %collective-permute-start.18 = (bf16[4,96,768]{2,1,0:T(8,128)(2,1)S(1)}, bf16[4,96,768]{2,1,0:T(8,128)(2,1)S(1)}, u32[]{:S(2)}, u32[]{:S(2)}) collective-permute-start(bf16[4,96,768]{2,1,0:T(8,128)(2,1)S(1)} %get-tuple-element.241), channel_id=1, source_target_pairs={{0,1},{1,0},{2,3},{3,2},{4,5},{5,4},{6,7},{7,6},{8,9},{9,8},{10,11... | collective-permute-start | bytes 1769480 | tf_op jit(solution)/shard_map/ppermute | solution.py:707
  108.5 12.8 %collective-permute-start.15 = (bf16[144,768]{1,0:T(8,128)(2,1)S(1)}, bf16[144,768]{1,0:T(8,128)(2,1)S(1)}, u32[]{:S(2)}, u32[]{:S(2)}) collective-permute-start(bf16[144,768]{1,0:T(8,128)(2,1)S(1)} %get-tuple-element.235), channel_id=1, source_target_pairs={{0,8},{1,9},{2,10},{3,11},{4,12},{5,13},{6,14},{7,15},{8,0},{9,1},... | collective-permute-start | bytes 663560 | tf_op jit(solution)/shard_map/ppermute | solution.py:707
  110.1 17.9 %collective-permute-start.16 = (bf16[144,768]{1,0:T(8,128)(2,1)S(1)}, bf16[144,768]{1,0:T(8,128)(2,1)S(1)}, u32[]{:S(2)}, u32[]{:S(2)}) collective-permute-start(bf16[144,768]{1,0:T(8,128)(2,1)S(1)} %get-tuple-element.236), channel_id=1, source_target_pairs={{0,16},{1,17},{2,18},{3,19},{4,20},{5,21},{6,22},{7,23},{8,24},{9,... | collective-permute-start | bytes 663560 | tf_op jit(solution)/shard_map/ppermute | solution.py:707
  112.7 15.3 %collective-permute-start.17 = (bf16[144,768]{1,0:T(8,128)(2,1)S(1)}, bf16[144,768]{1,0:T(8,128)(2,1)S(1)}, u32[]{:S(2)}, u32[]{:S(2)}) collective-permute-start(bf16[144,768]{1,0:T(8,128)(2,1)S(1)} %get-tuple-element.237), channel_id=1, source_target_pairs={{0,24},{1,25},{2,26},{3,27},{4,28},{5,29},{6,30},{7,31},{8,16},{9,... | collective-permute-start | bytes 663560 | tf_op jit(solution)/shard_map/ppermute | solution.py:707
  130.3 10.1 %collective-permute-start.24 = (bf16[4,96,768]{2,1,0:T(8,128)(2,1)}, bf16[4,96,768]{2,1,0:T(8,128)(2,1)S(1)}, u32[]{:S(2)}, u32[]{:S(2)}) collective-permute-start(bf16[4,96,768]{2,1,0:T(8,128)(2,1)} %get-tuple-element.250), channel_id=1, source_target_pairs={{0,1},{1,0},{2,3},{3,2},{4,5},{5,4},{6,7},{7,6},{8,9},{9,8},{10,11... | collective-permute-start | bytes 1769480 | tf_op jit(solution)/shard_map/ppermute | solution.py:707
  131.5 10.1 %collective-permute-start.23 = (bf16[4,96,768]{2,1,0:T(8,128)(2,1)}, bf16[4,96,768]{2,1,0:T(8,128)(2,1)S(1)}, u32[]{:S(2)}, u32[]{:S(2)}) collective-permute-start(bf16[4,96,768]{2,1,0:T(8,128)(2,1)} %get-tuple-element.248), channel_id=1, source_target_pairs={{0,4},{1,5},{2,6},{3,7},{4,0},{5,1},{6,2},{7,3},{8,12},{9,13},{10,... | collective-permute-start | bytes 1769480 | tf_op jit(solution)/shard_map/ppermute | solution.py:707
  133.0 11.7 %collective-permute-start.22 = (bf16[128,768]{1,0:T(8,128)(2,1)}, bf16[128,768]{1,0:T(8,128)(2,1)S(1)}, u32[]{:S(2)}, u32[]{:S(2)}) collective-permute-start(bf16[128,768]{1,0:T(8,128)(2,1)} %copy-done.6), channel_id=1, source_target_pairs={{0,24},{1,25},{2,26},{3,27},{4,28},{5,29},{6,30},{7,31},{8,16},{9,... | collective-permute-start | bytes 589832 | tf_op jit(solution)/shard_map/ppermute | solution.py:707
  135.1 9.8 %collective-permute-start.20 = (bf16[128,768]{1,0:T(8,128)(2,1)}, bf16[128,768]{1,0:T(8,128)(2,1)S(1)}, u32[]{:S(2)}, u32[]{:S(2)}) collective-permute-start(bf16[128,768]{1,0:T(8,128)(2,1)} %copy-done.6), channel_id=1, source_target_pairs={{0,8},{1,9},{2,10},{3,11},{4,12},{5,13},{6,14},{7,15},{8,0},{9,1},... | collective-permute-start | bytes 589832 | tf_op jit(solution)/shard_map/ppermute | solution.py:707
  139.2 11.9 %collective-permute-start.21 = (bf16[128,768]{1,0:T(8,128)(2,1)}, bf16[128,768]{1,0:T(8,128)(2,1)S(1)}, u32[]{:S(2)}, u32[]{:S(2)}) collective-permute-start(bf16[128,768]{1,0:T(8,128)(2,1)} %copy-done.6), channel_id=1, source_target_pairs={{0,16},{1,17},{2,18},{3,19},{4,20},{5,21},{6,22},{7,23},{8,24},{9,... | collective-permute-start | bytes 589832 | tf_op jit(solution)/shard_map/ppermute | solution.py:707
  151.2 7.9 %collective-permute-start.26 = (bf16[256,768]{1,0:T(8,128)(2,1)S(1)}, bf16[256,768]{1,0:T(8,128)(2,1)S(1)}, u32[]{:S(2)}, u32[]{:S(2)}) collective-permute-start(bf16[256,768]{1,0:T(8,128)(2,1)S(1)} %get-tuple-element.255.own_b), channel_id=1, source_target_pairs={{0,1},{1,0},{2,3},{3,2},{4,5},{5,4},{6,7},{7,6},{8,9},{9,8},{10,11... | collective-permute-start | bytes 1179656 | tf_op jit(solution)/shard_map/ppermute | solution.py:707
  152.1 7.8 %collective-permute-start.25 = (bf16[256,768]{1,0:T(8,128)(2,1)S(1)}, bf16[256,768]{1,0:T(8,128)(2,1)S(1)}, u32[]{:S(2)}, u32[]{:S(2)}) collective-permute-start(bf16[256,768]{1,0:T(8,128)(2,1)S(1)} %get-tuple-element.254.own_a), channel_id=1, source_target_pairs={{0,4},{1,5},{2,6},{3,7},{4,0},{5,1},{6,2},{7,3},{8,12},{9,13},{10,... | collective-permute-start | bytes 1179656 | tf_op jit(solution)/shard_map/ppermute | solution.py:707
  158.5 12.8 %collective-permute-start.29 = (bf16[4,96,768]{2,1,0:T(8,128)(2,1)}, bf16[4,96,768]{2,1,0:T(8,128)(2,1)S(1)}, u32[]{:S(2)}, u32[]{:S(2)}) collective-permute-start(bf16[4,96,768]{2,1,0:T(8,128)(2,1)} %copy-done.24), channel_id=1, source_target_pairs={{0,8},{1,9},{2,10},{3,11},{4,12},{5,13},{6,14},{7,15},{8,0},{9,1},... | collective-permute-start | bytes 1769480 | tf_op jit(solution)/shard_map/ppermute | solution.py:707
  160.0 13.5 %collective-permute-start.31 = (bf16[512,768]{1,0:T(8,128)(2,1)S(1)}, bf16[512,768]{1,0:T(8,128)(2,1)S(1)}, u32[]{:S(2)}, u32[]{:S(2)}) collective-permute-start(bf16[512,768]{1,0:T(8,128)(2,1)S(1)} %get-tuple-element.260.refs_0_), channel_id=1, source_target_pairs={{0,2},{1,3},{2,0},{3,1},{4,6},{5,7},{6,4},{7,5},{8,10},{9,11},{10,... | collective-permute-start | bytes 2359304 | tf_op jit(solution)/shard_map/ppermute | solution.py:707
  160.0 20.0 %collective-permute-start.27 = (bf16[512,768]{1,0:T(8,128)(2,1)S(1)}, bf16[512,768]{1,0:T(8,128)(2,1)S(1)}, u32[]{:S(2)}, u32[]{:S(2)}) collective-permute-start(bf16[512,768]{1,0:T(8,128)(2,1)S(1)} %get-tuple-element.260.refs_0_), channel_id=1, source_target_pairs={{0,1},{1,0},{2,3},{3,2},{4,5},{5,4},{6,7},{7,6},{8,9},{9,8},{10,11... | collective-permute-start | bytes 2359304 | tf_op jit(solution)/shard_map/ppermute | solution.py:707
  161.3 20.0 %collective-permute-start.32 = (bf16[512,768]{1,0:T(8,128)(2,1)S(1)}, bf16[512,768]{1,0:T(8,128)(2,1)S(1)}, u32[]{:S(2)}, u32[]{:S(2)}) collective-permute-start(bf16[512,768]{1,0:T(8,128)(2,1)S(1)} %get-tuple-element.261.refs_1_.q0), channel_id=1, source_target_pairs={{0,2},{1,3},{2,0},{3,1},{4,6},{5,7},{6,4},{7,5},{8,10},{9,11},{10,... | collective-permute-start | bytes 2359304 | tf_op jit(solution)/shard_map/ppermute | solution.py:707
  161.5 19.8 %collective-permute-start.33 = (bf16[512,768]{1,0:T(8,128)(2,1)S(1)}, bf16[512,768]{1,0:T(8,128)(2,1)S(1)}, u32[]{:S(2)}, u32[]{:S(2)}) collective-permute-start(bf16[512,768]{1,0:T(8,128)(2,1)S(1)} %get-tuple-element.261.refs_1_.q0), channel_id=1, source_target_pairs={{0,4},{1,5},{2,6},{3,7},{4,0},{5,1},{6,2},{7,3},{8,12},{9,13},{10,... | collective-permute-start | bytes 2359304 | tf_op jit(solution)/shard_map/ppermute | solution.py:707
  171.3 13.0 %collective-permute-start.30 = (bf16[2,96,768]{2,1,0:T(8,128)(2,1)S(1)}, bf16[2,96,768]{2,1,0:T(8,128)(2,1)S(1)}, u32[]{:S(2)}, u32[]{:S(2)}) collective-permute-start(bf16[2,96,768]{2,1,0:T(8,128)(2,1)S(1)} %get-tuple-element.265), channel_id=1, source_target_pairs={{0,16},{1,17},{2,18},{3,19},{4,20},{5,21},{6,22},{7,23},{8,24},{9,... | collective-permute-start | bytes 884744 | tf_op jit(solution)/shard_map/ppermute | solution.py:707
  180.0 5.2 %collective-permute-start.28 = (bf16[512,768]{1,0:T(8,128)(2,1)S(1)}, bf16[512,768]{1,0:T(8,128)(2,1)S(1)}, u32[]{:S(2)}, u32[]{:S(2)}) collective-permute-start(bf16[512,768]{1,0:T(8,128)(2,1)S(1)} %collective-permute-done.27.refs_2_), channel_id=1, source_target_pairs={{0,2},{1,3},{2,0},{3,1},{4,6},{5,7},{6,4},{7,5},{8,10},{9,11},{10,... | collective-permute-start | bytes 2359304 | tf_op jit(solution)/shard_map/ppermute | solution.py:707
  181.3 4.0 %collective-permute-start.34 = (bf16[512,768]{1,0:T(8,128)(2,1)S(1)}, bf16[512,768]{1,0:T(8,128)(2,1)S(1)}, u32[]{:S(2)}, u32[]{:S(2)}) collective-permute-start(bf16[512,768]{1,0:T(8,128)(2,1)S(1)} %collective-permute-done.33.refs_3_.q1), channel_id=1, source_target_pairs={{0,2},{1,3},{2,0},{3,1},{4,6},{5,7},{6,4},{7,5},{8,10},{9,11},{10,... | collective-permute-start | bytes 2359304 | tf_op jit(solution)/shard_map/ppermute | solution.py:707
  (13 other events, 29.9 us)
